TPU v7x, 32 devices: a whole 2x2x4 slice. The times are simulated.
32 devices in a mesh: expert: 4 (over z), dp: 8 (over y, x, core).
Axes of the slice: x: 2, y: 2, z: 4, core: 2. Of those that a mesh axis runs over, the one named last changes fastest.
Arguments:
- tokens: bfloat16 [8, 2560, 768], P('dp', 'expert'), may hold values from -6 to 6
- prior_logits: float32 [8, 2560, 12], P('dp', 'expert'), may hold values from -6 to 6
- routes: int32 [8, 2560, 2], P('dp', 'expert'), may hold values from 0 to 11, all different within a row; in each aligned block of 640 rows (0 to 639, 640 to 1279, ..., all dimensions but the last counted through in order) at most 160 rows name the same one
- parents: int32 [8, 12], P('dp'), may hold values from 0 to 4, as said below
- cotangent: bfloat16 [8, 2560, 768], P('dp', 'expert'), may hold values from -6 to 6
- query_weight: bfloat16 [768, 768], replicated, may hold values from -0.3125 to 0.3125
- key_weight: bfloat16 [768, 768], replicated, may hold values from -0.21875 to 0.21875
- value_weight: bfloat16 [768, 768], replicated, may hold values from -0.21875 to 0.21875
- out_weight: bfloat16 [768, 768], replicated, may hold values from -0.875 to 0.875
- attention_gain: float32 [768], replicated, may hold values from 0.5 to 1.5
- expert_gain: float32 [768], replicated, may hold values from 0.5 to 1.5
- router_weight: bfloat16 [768, 12], replicated, may hold values from -0.15625 to 0.15625
- prior_weight: float32 [12, 12], replicated, may hold values from -0.875 to 0.875
- constant_weight: bfloat16 [768, 4], replicated, may hold values from -0.21875 to 0.21875
- constant_vector: float32 [2, 768], replicated, may hold values from -6 to 6
- gate_weight: bfloat16 [8, 768, 2048], P('expert', 'dp'), may hold values from -0.21875 to 0.21875
- up_weight: bfloat16 [8, 768, 2048], P('expert', 'dp'), may hold values from -0.21875 to 0.21875
- down_weight: bfloat16 [8, 2048, 768], P('expert', 'dp'), may hold values from -0.25 to 0.25
Outputs:
- output: bfloat16 [8, 2560, 768], P('dp', 'expert')
- tokens_grad: float32 [8, 2560, 768], P('dp', 'expert')
- prior_grad: float32 [8, 2560, 12], P('dp', 'expert')
- query_grad: float32 [768, 768], P('expert')
- key_grad: float32 [768, 768], P('expert')
- value_grad: float32 [768, 768], P('expert')
- out_grad: float32 [768, 768], P('expert')
- attention_gain_grad: float32 [768], P('expert')
- expert_gain_grad: float32 [768], P('expert')
- router_grad: float32 [768, 12], P('expert')
- prior_weight_grad: float32 [12, 12], P('expert')
- constant_weight_grad: float32 [768, 4], P('expert')
- constant_vector_grad: float32 [2, 768], P(None, 'expert')
- gate_grad: float32 [8, 768, 2048], P('expert', 'dp')
- up_grad: float32 [8, 768, 2048], P('expert', 'dp')
- down_grad: float32 [8, 2048, 768], P('expert', 'dp')
Inputs may be any that keep to these rules, and one draw needn't show every extreme that they name: `routes`: each row names two different experts: 0 to 7 feed-forward, 8 zero, 9 copy, 10 and 11 constant. The rows of one device name no expert more than 160 times, a bound that some block reaches. `parents`: entry i names the parent of segment i + 1: for the branches (i < 4) a segment before it, for the leaves one of the branches 1 to 4.
All inputs are finite; a program needn't handle non-finite values.
Results may differ from a plain program's by a relative error of at most 0.03.
Values may be sent and summed in bfloat16 or wider, within the bound.
A program may use at most 192 MiB of HBM per device.

v0:
```python
import jax
import jax.numpy as jnp
from jax import lax
from jax.sharding import PartitionSpec as P

NFFN = 8
SEG = 128
HEAD_DIM = 64
TRUNK = 1024


epsilon = 1e-06
masked_score = -1e30
precise = lax.Precision.HIGHEST


def segment_of(token_ids):
    return jnp.where(token_ids < TRUNK, 0, 1 + (token_ids - TRUNK) // SEG)


def one_hot_segments(token_ids):
    return (segment_of(token_ids)[:, None] == jnp.arange(13, dtype=jnp.int32)[None, :]).astype(
        jnp.float32
    )


def lineage_of(parent_row):
    segment_total = parent_row.shape[0] + 1
    indices = jnp.arange(segment_total, dtype=jnp.int32)
    parent_all = jnp.concatenate([jnp.zeros((1,), jnp.int32), parent_row])
    parent_step = ((parent_all[:, None] == indices[None, :]) & (indices[:, None] > 0)).astype(
        jnp.float32
    )
    identity = jnp.eye(segment_total, dtype=jnp.float32)
    lineage = identity
    for repeat in range(segment_total - 1):
        lineage = jnp.minimum(1.0, identity + jnp.dot(parent_step, lineage, precision=precise))
    return lineage


def shift_table(lineage):
    counter = jnp.arange(13, dtype=jnp.int32)
    lengths = jnp.where(counter == 0, TRUNK, SEG).astype(jnp.float32)
    starts = jnp.where(counter == 0, 0, TRUNK + (counter - 1) * SEG).astype(jnp.float32)
    proper = lineage - jnp.eye(13, dtype=jnp.float32)
    return jnp.dot(proper, lengths, precision=precise) - starts


def positions(token_ids, shifts):
    return jnp.dot(one_hot_segments(token_ids), shifts, precision=precise) + token_ids.astype(
        jnp.float32
    )


def visible(query_ids, key_ids, lineage):
    reachable = jnp.dot(
        jnp.dot(one_hot_segments(query_ids), lineage, precision=precise),
        one_hot_segments(key_ids).T,
        precision=precise,
    )
    return (reachable > 0.5) & (key_ids[None, :] <= query_ids[:, None])


def rotate(values, places, direction):
    half_size = values.shape[-1] // 2
    frequency = 10000.0 ** (-(jnp.arange(half_size, dtype=jnp.float32) * 2.0 / values.shape[-1]))
    angles = places[:, None] * frequency[None, :]
    cosine = jnp.cos(angles)[:, None, :]
    sine_part = direction * jnp.sin(angles)[:, None, :]
    first_half = values[..., :half_size]
    second = values[..., half_size:]
    return jnp.concatenate(
        [first_half * cosine - second * sine_part, second * cosine + first_half * sine_part], -1
    )


def slot_tables(route_block, owners, capacity):
    row_count = route_block.shape[0]
    expert_ids = jnp.arange(NFFN, dtype=jnp.int32)
    matches = (route_block[:, :, None] == expert_ids[None, None, :]).astype(jnp.int32)
    per_row = jnp.sum(matches, 1)
    before = jnp.cumsum(per_row, 0) - per_row
    ranking = jnp.sum(matches * before[:, None, :], -1)
    per_owner = NFFN // owners
    target = jnp.minimum(route_block, NFFN - 1)
    spare_slot = NFFN * capacity
    flat_slots = target % per_owner * (owners * capacity) + target // per_owner * capacity + ranking
    flat_slots = jnp.where(route_block < NFFN, flat_slots, spare_slot)
    pair_ids = jnp.arange(2 * row_count, dtype=jnp.int32)
    slot_pairs = (
        jnp.full((spare_slot,), 2 * row_count, jnp.int32)
        .at[flat_slots.reshape(-1)]
        .set(pair_ids, mode="drop")
    )
    return (flat_slots, slot_pairs)


def per_device(
    tokens,
    prior_logits,
    routes,
    parents,
    cotangent,
    query_weight,
    key_weight,
    value_weight,
    out_weight,
    attention_gain,
    expert_gain,
    router_weight,
    prior_weight,
    constant_weight,
    constant_vector,
    gate_weight,
    up_weight,
    down_weight,
):
    owners = lax.axis_size("expert")
    member = lax.axis_index("expert")
    inputs = tokens[0].astype(jnp.float32)
    row_count, model_width = inputs.shape
    capacity = row_count // 4
    head_count = model_width // HEAD_DIM
    scaling = HEAD_DIM ** (-0.5)
    tree_length = row_count * owners
    key_block = 4 * SEG
    block_total = tree_length // key_block
    lineage = lineage_of(parents[0])
    shifts = shift_table(lineage)
    query_ids = member * row_count + jnp.arange(row_count, dtype=jnp.int32)
    places = positions(query_ids, shifts)
    inv_first = lax.rsqrt(jnp.mean(inputs * inputs, -1, keepdims=True) + epsilon)
    normed = inputs * inv_first
    normed_b = (normed * attention_gain).astype(jnp.bfloat16)
    query_pre = jnp.dot(normed_b, query_weight, preferred_element_type=jnp.float32)
    key_pre = jnp.dot(normed_b, key_weight, preferred_element_type=jnp.float32)
    queries = rotate(query_pre.reshape(row_count, head_count, HEAD_DIM), places, 1.0).astype(
        jnp.bfloat16
    )
    keys_own = rotate(key_pre.reshape(row_count, head_count, HEAD_DIM), places, 1.0).astype(
        jnp.bfloat16
    )
    keys_own = keys_own.reshape(row_count, model_width)
    values_own = jnp.dot(normed_b, value_weight, preferred_element_type=jnp.float32).astype(
        jnp.bfloat16
    )
    keys_all, values_all = (
        lax.all_gather(keys_own, "expert", axis=0, tiled=True),
        lax.all_gather(values_own, "expert", axis=0, tiled=True),
    )

    def key_slice(start):
        key_part = lax.dynamic_slice_in_dim(keys_all, start, key_block, 0).reshape(
            key_block, head_count, HEAD_DIM
        )
        value_part = lax.dynamic_slice_in_dim(values_all, start, key_block, 0).reshape(
            key_block, head_count, HEAD_DIM
        )
        key_ids = start + jnp.arange(key_block, dtype=jnp.int32)
        return (key_part, value_part, visible(query_ids, key_ids, lineage))

    def forward_block(carry, block_index):
        running_max, running_sum, accumulated = carry
        key_part, value_part, allowed = key_slice(block_index * key_block)
        scores = (
            jnp.einsum("qhd,khd->hqk", queries, key_part, preferred_element_type=jnp.float32)
            * scaling
        )
        scores = jnp.where(allowed[None], scores, masked_score)
        new_max = jnp.maximum(running_max, jnp.max(scores, -1))
        weights_now = jnp.where(allowed[None], jnp.exp(scores - new_max[..., None]), 0.0)
        factor = jnp.exp(running_max - new_max)
        running_sum = running_sum * factor + jnp.sum(weights_now, -1)
        accumulated = accumulated * factor.T[:, :, None] + jnp.einsum(
            "hqk,khd->qhd",
            weights_now.astype(jnp.bfloat16),
            value_part,
            preferred_element_type=jnp.float32,
        )
        return ((new_max, running_sum, accumulated), None)

    start_state = (
        jnp.full((head_count, row_count), masked_score, jnp.float32),
        jnp.zeros((head_count, row_count), jnp.float32),
        jnp.zeros((row_count, head_count, HEAD_DIM), jnp.float32),
    )
    (final_max, final_sum, accumulated), unused = lax.scan(
        forward_block, start_state, jnp.arange(block_total)
    )
    attended = accumulated / final_sum.T[:, :, None]
    log_total = final_max + jnp.log(final_sum)
    attended_b = attended.reshape(row_count, model_width).astype(jnp.bfloat16)
    resid = inputs + jnp.dot(attended_b, out_weight, preferred_element_type=jnp.float32)
    inv_second = lax.rsqrt(jnp.mean(resid * resid, -1, keepdims=True) + epsilon)
    normed_two = resid * inv_second
    hidden_in = normed_two * expert_gain
    hidden_b = hidden_in.astype(jnp.bfloat16)
    hidden_f = hidden_b.astype(jnp.float32)
    prior_rows = prior_logits[0]
    route_rows = routes[0]
    logits = jnp.dot(hidden_b, router_weight, preferred_element_type=jnp.float32) + jnp.dot(
        prior_rows, prior_weight, precision=precise
    )
    picked = (
        route_rows[:, :, None] == jnp.arange(NFFN + 4, dtype=jnp.int32)[None, None, :]
    ).astype(jnp.float32)
    chosen = jnp.einsum("lce,le->lc", picked, logits, precision=precise)
    gate_probs = jax.nn.softmax(chosen, -1)
    const_logits = jnp.dot(hidden_b, constant_weight, preferred_element_type=jnp.float32).reshape(
        row_count, 2, 2
    )
    mixing = jax.nn.softmax(const_logits, -1)
    constants = (
        mixing[:, :, 0:1] * hidden_in[:, None, :] + mixing[:, :, 1:2] * constant_vector[None]
    )
    flat_slots, slot_pairs = slot_tables(route_rows, owners, capacity)
    local_experts = gate_weight.shape[0]
    padded_rows = jnp.concatenate([hidden_b, jnp.zeros((1, model_width), jnp.bfloat16)], 0)
    outgoing = padded_rows[slot_pairs // 2].reshape(local_experts, owners, capacity, model_width)
    gate_full, up_full, down_full = (
        lax.all_gather(gate_weight, "dp", axis=1, tiled=True),
        lax.all_gather(up_weight, "dp", axis=1, tiled=True),
        lax.all_gather(down_weight, "dp", axis=1, tiled=True),
    )
    incoming = lax.all_to_all(outgoing, "expert", split_axis=1, concat_axis=1, tiled=True).reshape(
        local_experts, owners * capacity, model_width
    )
    gate_pre = jnp.einsum("erd,edf->erf", incoming, gate_full, preferred_element_type=jnp.float32)
    up_pre = jnp.einsum("erd,edf->erf", incoming, up_full, preferred_element_type=jnp.float32)
    activated = jax.nn.silu(gate_pre)
    hidden_mid = (activated * up_pre).astype(jnp.bfloat16)
    expert_out = jnp.einsum(
        "erf,efd->erd", hidden_mid, down_full, preferred_element_type=jnp.float32
    ).astype(jnp.bfloat16)
    returned = lax.all_to_all(
        expert_out.reshape(local_experts, owners, capacity, model_width),
        "expert",
        split_axis=1,
        concat_axis=1,
        tiled=True,
    )
    returned = jnp.concatenate(
        [returned.reshape(-1, model_width), jnp.zeros((1, model_width), jnp.bfloat16)], 0
    )
    routed = returned[flat_slots].astype(jnp.float32)
    branches = (
        routed
        + picked[:, :, NFFN + 1, None] * hidden_in[:, None, :]
        + picked[:, :, NFFN + 2, None] * constants[:, None, 0, :]
        + picked[:, :, NFFN + 3, None] * constants[:, None, 1, :]
    )
    result = resid + jnp.sum(gate_probs[:, :, None] * branches, 1)
    upstream = cotangent[0].astype(jnp.float32)
    gate_grads = jnp.sum(upstream[:, None, :] * branches, -1)
    chosen_grads = gate_probs * (gate_grads - jnp.sum(gate_probs * gate_grads, -1, keepdims=True))
    logit_grads = jnp.einsum("lc,lce->le", chosen_grads, picked, precision=precise)
    prior_grad = jnp.dot(logit_grads, prior_weight.T, precision=precise)
    prior_weight_grad = jnp.dot(prior_rows.T, logit_grads, precision=precise)
    router_grad = jnp.dot(hidden_f.T, logit_grads, precision=precise)
    branch_grads = gate_probs[:, :, None] * upstream[:, None, :]
    padded_grads = jnp.concatenate(
        [
            branch_grads.reshape(2 * row_count, model_width),
            jnp.zeros((1, model_width), jnp.float32),
        ],
        0,
    )
    grads_out = (
        padded_grads[slot_pairs]
        .astype(jnp.bfloat16)
        .reshape(local_experts, owners, capacity, model_width)
    )
    grads_in = lax.all_to_all(grads_out, "expert", split_axis=1, concat_axis=1, tiled=True).reshape(
        local_experts, owners * capacity, model_width
    )
    gate_back, up_back, down_back = (
        lax.all_gather(gate_weight, "dp", axis=1, tiled=True),
        lax.all_gather(up_weight, "dp", axis=1, tiled=True),
        lax.all_gather(down_weight, "dp", axis=1, tiled=True),
    )
    mid_grads = jnp.einsum("erd,efd->erf", grads_in, down_back, preferred_element_type=jnp.float32)
    down_local = jnp.einsum(
        "erf,erd->efd", hidden_mid, grads_in, preferred_element_type=jnp.float32
    )
    sigmoid_gate = jax.nn.sigmoid(gate_pre)
    gate_grads_b = (
        mid_grads * up_pre * sigmoid_gate * (1.0 + gate_pre * (1.0 - sigmoid_gate))
    ).astype(jnp.bfloat16)
    up_grads_b = (mid_grads * activated).astype(jnp.bfloat16)
    gate_local = jnp.einsum(
        "erd,erf->edf", incoming, gate_grads_b, preferred_element_type=jnp.float32
    )
    up_local = jnp.einsum("erd,erf->edf", incoming, up_grads_b, preferred_element_type=jnp.float32)
    input_grads = (
        jnp.einsum("erf,edf->erd", gate_grads_b, gate_back, preferred_element_type=jnp.float32)
        + jnp.einsum("erf,edf->erd", up_grads_b, up_back, preferred_element_type=jnp.float32)
    ).astype(jnp.bfloat16)
    back_grads = lax.all_to_all(
        input_grads.reshape(local_experts, owners, capacity, model_width),
        "expert",
        split_axis=1,
        concat_axis=1,
        tiled=True,
    )
    gate_part, up_part, down_part = (
        lax.psum_scatter(gate_local, "dp", scatter_dimension=1, tiled=True),
        lax.psum_scatter(up_local, "dp", scatter_dimension=1, tiled=True),
        lax.psum_scatter(down_local, "dp", scatter_dimension=1, tiled=True),
    )
    back_grads = jnp.concatenate(
        [back_grads.reshape(-1, model_width), jnp.zeros((1, model_width), jnp.bfloat16)], 0
    )
    routed_grads = jnp.sum(back_grads[flat_slots].astype(jnp.float32), 1)
    const_grads = jnp.stack(
        [
            jnp.sum(picked[:, :, NFFN + 2, None] * branch_grads, 1),
            jnp.sum(picked[:, :, NFFN + 3, None] * branch_grads, 1),
        ],
        1,
    )
    constant_vector_grad = jnp.sum(mixing[:, :, 1:2] * const_grads, 0)
    mix_grads = jnp.stack(
        [
            jnp.sum(const_grads * hidden_in[:, None, :], -1),
            jnp.sum(const_grads * constant_vector[None], -1),
        ],
        -1,
    )
    const_logit_grads = (
        mixing * (mix_grads - jnp.sum(mixing * mix_grads, -1, keepdims=True))
    ).reshape(row_count, 4)
    constant_weight_grad = jnp.dot(hidden_f.T, const_logit_grads, precision=precise)
    hidden_grads = (
        jnp.dot(logit_grads, router_weight.astype(jnp.float32).T, precision=precise)
        + jnp.dot(const_logit_grads, constant_weight.astype(jnp.float32).T, precision=precise)
        + jnp.sum(mixing[:, :, 0:1] * const_grads, 1)
        + jnp.sum(picked[:, :, NFFN + 1, None] * branch_grads, 1)
        + routed_grads
    )
    expert_gain_grad = jnp.sum(hidden_grads * normed_two, 0)
    scaled_two = hidden_grads * expert_gain
    resid_grads = (
        inv_second
        * (scaled_two - normed_two * jnp.mean(scaled_two * normed_two, -1, keepdims=True))
        + upstream
    )
    resid_b = resid_grads.astype(jnp.bfloat16)
    out_grad = jnp.einsum("nd,ne->de", attended_b, resid_b, preferred_element_type=jnp.float32)
    attn_grads = jnp.einsum(
        "ne,de->nd", resid_b, out_weight, preferred_element_type=jnp.float32
    ).astype(jnp.bfloat16)
    attn_grads = attn_grads.reshape(row_count, head_count, HEAD_DIM)
    row_delta = jnp.sum(attn_grads.astype(jnp.float32) * attended, -1).T

    def score_block(key_part, value_part, allowed):
        scores = (
            jnp.einsum("qhd,khd->hqk", queries, key_part, preferred_element_type=jnp.float32)
            * scaling
        )
        weights_now = jnp.where(allowed[None], jnp.exp(scores - log_total[..., None]), 0.0)
        weight_grads = jnp.einsum(
            "qhd,khd->hqk", attn_grads, value_part, preferred_element_type=jnp.float32
        )
        score_grads = (weights_now * (weight_grads - row_delta[..., None])).astype(jnp.bfloat16)
        return (weights_now, score_grads)

    def backward_block(query_grads, block_index):
        key_part, value_part, allowed = key_slice(block_index * key_block)
        weights_now, score_grads = score_block(key_part, value_part, allowed)
        query_grads = query_grads + jnp.einsum(
            "hqk,khd->qhd", score_grads, key_part, preferred_element_type=jnp.float32
        )
        key_grads = (
            jnp.einsum("hqk,qhd->khd", score_grads, queries, preferred_element_type=jnp.float32)
            * scaling
        )
        value_grads = jnp.einsum(
            "hqk,qhd->khd",
            weights_now.astype(jnp.bfloat16),
            attn_grads,
            preferred_element_type=jnp.float32,
        )
        return (
            query_grads,
            jnp.concatenate(
                [
                    key_grads.reshape(key_block, model_width),
                    value_grads.reshape(key_block, model_width),
                ],
                -1,
            ),
        )

    query_grads, pair_terms = lax.scan(
        backward_block,
        jnp.zeros((row_count, head_count, HEAD_DIM), jnp.float32),
        jnp.arange(block_total),
    )
    pair_sums = lax.psum_scatter(
        pair_terms.reshape(tree_length, 2 * model_width).astype(jnp.bfloat16),
        "expert",
        scatter_dimension=0,
        tiled=True,
    ).astype(jnp.float32)
    own_key_grads = pair_sums[:, :model_width]
    own_value_grads = pair_sums[:, model_width:]
    query_back = (
        rotate(query_grads * scaling, places, -1.0)
        .reshape(row_count, model_width)
        .astype(jnp.bfloat16)
    )
    key_back = rotate(own_key_grads.reshape(row_count, head_count, HEAD_DIM), places, -1.0)
    key_back = key_back.reshape(row_count, model_width).astype(jnp.bfloat16)
    value_back = own_value_grads.astype(jnp.bfloat16)
    query_grad = jnp.einsum("nd,ne->de", normed_b, query_back, preferred_element_type=jnp.float32)
    key_grad = jnp.einsum("nd,ne->de", normed_b, key_back, preferred_element_type=jnp.float32)
    value_grad = jnp.einsum("nd,ne->de", normed_b, value_back, preferred_element_type=jnp.float32)
    first_grads = (
        jnp.einsum("ne,de->nd", query_back, query_weight, preferred_element_type=jnp.float32)
        + jnp.einsum("ne,de->nd", key_back, key_weight, preferred_element_type=jnp.float32)
        + jnp.einsum("ne,de->nd", value_back, value_weight, preferred_element_type=jnp.float32)
    )
    attention_gain_grad = jnp.sum(first_grads * normed, 0)
    scaled_one = first_grads * attention_gain
    tokens_grad = (
        inv_first * (scaled_one - normed * jnp.mean(scaled_one * normed, -1, keepdims=True))
        + resid_grads
    )
    (
        query_shard,
        key_shard,
        value_shard,
        out_shard,
        attention_shard,
        expert_shard,
        router_shard,
        prior_shard,
        constant_shard,
        vector_shard,
    ) = (
        lax.psum_scatter(
            query_grad.astype(jnp.bfloat16), "expert", scatter_dimension=0, tiled=True
        ).astype(jnp.float32),
        lax.psum_scatter(
            key_grad.astype(jnp.bfloat16), "expert", scatter_dimension=0, tiled=True
        ).astype(jnp.float32),
        lax.psum_scatter(
            value_grad.astype(jnp.bfloat16), "expert", scatter_dimension=0, tiled=True
        ).astype(jnp.float32),
        lax.psum_scatter(
            out_grad.astype(jnp.bfloat16), "expert", scatter_dimension=0, tiled=True
        ).astype(jnp.float32),
        lax.psum_scatter(
            attention_gain_grad.astype(jnp.bfloat16), "expert", scatter_dimension=0, tiled=True
        ).astype(jnp.float32),
        lax.psum_scatter(
            expert_gain_grad.astype(jnp.bfloat16), "expert", scatter_dimension=0, tiled=True
        ).astype(jnp.float32),
        lax.psum_scatter(
            router_grad.astype(jnp.bfloat16), "expert", scatter_dimension=0, tiled=True
        ).astype(jnp.float32),
        lax.psum_scatter(
            prior_weight_grad.astype(jnp.bfloat16), "expert", scatter_dimension=0, tiled=True
        ).astype(jnp.float32),
        lax.psum_scatter(
            constant_weight_grad.astype(jnp.bfloat16), "expert", scatter_dimension=0, tiled=True
        ).astype(jnp.float32),
        lax.psum_scatter(
            constant_vector_grad.astype(jnp.bfloat16), "expert", scatter_dimension=1, tiled=True
        ).astype(jnp.float32),
    )
    (
        query_total,
        key_total,
        value_total,
        out_total,
        attention_total,
        expert_total,
        router_total,
        prior_total,
        constant_total,
        vector_total,
    ) = lax.psum(
        (
            query_shard,
            key_shard,
            value_shard,
            out_shard,
            attention_shard,
            expert_shard,
            router_shard,
            prior_shard,
            constant_shard,
            vector_shard,
        ),
        "dp",
    )
    return (
        result.astype(jnp.bfloat16)[None],
        tokens_grad[None],
        prior_grad[None],
        query_total,
        key_total,
        value_total,
        out_total,
        attention_total,
        expert_total,
        router_total,
        prior_total,
        constant_total,
        vector_total,
        gate_part,
        up_part,
        down_part,
    )


def solution(mesh):
    in_specs = (
        P("dp", "expert", None),
        P("dp", "expert", None),
        P("dp", "expert", None),
        P("dp", None),
        P("dp", "expert", None),
        P(),
        P(),
        P(),
        P(),
        P(),
        P(),
        P(),
        P(),
        P(),
        P(),
        P("expert", "dp", None),
        P("expert", "dp", None),
        P("expert", "dp", None),
    )
    out_specs = (
        P("dp", "expert", None),
        P("dp", "expert", None),
        P("dp", "expert", None),
        P("expert", None),
        P("expert", None),
        P("expert", None),
        P("expert", None),
        P("expert"),
        P("expert"),
        P("expert", None),
        P("expert", None),
        P("expert", None),
        P(None, "expert"),
        P("expert", "dp", None),
        P("expert", "dp", None),
        P("expert", "dp", None),
    )
    return jax.shard_map(
        per_device, mesh=mesh, in_specs=in_specs, out_specs=out_specs, check_vma=False
    )
```

profile of v0, /device:TPU:1, one launch (start us, length us, event | category | flops | bytes accessed | tf_op | source)
XLA Modules:
  0.0 1546.0 jit_solution(11736290527924113482)
XLA Ops:
  37.2 53.6 %all-gather.8.cloned.1.call-done = bf16[2560,768]{1,0:T(8,128)(2,1)} async-done(((bf16[640,768]{1,0:T(8,128)(2,1)}), bf16[2560,768]{1,0:T(8,128)(2,1)}) %all-gather.8.cloned.1.call-update) | async-done | bytes 3932176 | tf_op jit(solution)/shard_map/all_gather | solution.py:149
  97.0 70.9 %all-gather.6.cloned.1.call-done = bf16[2560,768]{0,1:T(8,128)(2,1)} async-done(((bf16[640,768]{0,1:T(8,128)(2,1)}), bf16[2560,768]{0,1:T(8,128)(2,1)}) %all-gather.6.cloned.1.call-update) | async-done | bytes 3932176 | tf_op jit(solution)/shard_map/all_gather | solution.py:148
  168.0 153.2 %while.36 = (s32[]{:T(128)}, f32[12,640]{1,0:T(8,128)S(1)}, f32[12,640]{1,0:T(8,128)S(1)}, f32[640,12,64]{0,2,1:T(8,128)}, s32[5]{0:T(128)S(1)}, /*index=5*/f32[...) while((s32[]{:T(128)}, f32[12,640]{1,0:T(8,128)S(1)}, ...), condition=%wide.region_4.5_spmd.clone, body=%wide.region_1.4_spmd.clone.sunk | while | flops 1111390336 | bytes 74397456 | solution.py:187
  365.0 19.7 %all-to-all-done = bf16[2,4,160,768]{3,2,0,1:T(8,128)(2,1)} async-done(((bf16[2,4,160,768]{3,2,0,1:T(8,128)(2,1)}), bf16[2,4,160,768]{3,2,0,1:T(8,128)(2,1)}, u32[]{:S(2)}, u32[]{:S(2)}) %all-to-all-start) | async-done | bytes 1966112 | tf_op jit(solution)/shard_map/all_to_all | solution.py:225
  391.3 41.8 %all-to-all-done.2 = bf16[2,4,160,768]{3,2,0,1:T(8,128)(2,1)S(1)} async-done(((bf16[2,4,160,768]{3,2,0,1:T(8,128)(2,1)}), bf16[2,4,160,768]{3,2,0,1:T(8,128)(2,1)S(1)}, u32[]{:S(2)}, u32[]{:S(2)}) %all-to-all-start.2) | async-done | bytes 1966112 | tf_op jit(solution)/shard_map/all_to_all | solution.py:273
  434.5 11.7 fusion.172
  446.2 11.6 fusion.173
  457.8 19.9 %multiply_convert_fusion = (bf16[2,640,2048]{2,1,0:T(8,128)(2,1)}, bf16[2,640,2048]{2,1,0:T(8,128)(2,1)}, bf16[2,640,2048]{2,1,0:T(8,128)(2,1)}) fusion(f32[2,640,2048]{2,1,0:T(8,128)} %fusion.172, f32[2,640,2048]{2,1,0:T(8,128)} %fusion.173, bf16[2,640,768]{2,1,0:T(8,128)(2,1)S(1)} %bitcast.388, bf16[2,2048,768]{2,1,0:T(8,128)(2,1)} %all-gather.14.cloned.1.call-done), kind=kOutput, calls=%fused_computation.68 | convolution fusion | flops 4065853440 | bytes 44957696 | tf_op jit(solution)/shard_map/erd,efd->erf/dot_general | solution.py:281
  513.5 31.9 %all-to-all-done.3 = bf16[2,4,160,768]{3,2,0,1:T(8,128)(2,1)} async-done(((bf16[2,4,160,768]{3,2,0,1:T(8,128)(2,1)}), bf16[2,4,160,768]{3,2,0,1:T(8,128)(2,1)}, u32[]{:S(2)}, u32[]{:S(2)}) %all-to-all-start.3) | async-done | bytes 1966112 | tf_op jit(solution)/shard_map/all_to_all | solution.py:298
  582.4 12.4 all-to-all-done.1
  607.2 31.4 %multiply_reduce_fusion.4 = (f32[640,2]{1,0:T(8,128)}, f32[640,768]{1,0:T(8,128)}, f32[640,768]{1,0:T(8,128)}, f32[640,768]{1,0:T(8,128)}, f32[640,768]{1,0:T(8,128)}) fusion(f32[640,768]{1,0:T(8,128)} %copy-done.13, f32[640,2]{1,0:T(8,128)} %copy-done.34, f32[640,2]{1,0:T(8,128)} %get-tuple-element.851, f32[640,2]{1,0:T(8,128)} %get-tuple-element.849, ...), kind=kLoop, calls=%fused_computation.88 | loop fusion | flops 14744320 | bytes 19686400 | tf_op jit(solution)/shard_map/reduce_sum | solution.py:254
  650.7 16.0 %multiply_reduce_fusion = (bf16[2,768]{1,0:T(2,128)(2,1)}, f32[640,2]{1,0:T(8,128)}, f32[640,768]{1,0:T(8,128)}, f32[640,2]{1,0:T(8,128)S(1)}) fusion(f32[640,2]{1,0:T(8,128)S(1)} %bitcast.382, f32[640,1,768]{2,1,0:T(1,128)S(1)} %stack.19, f32[640,1,768]{2,1,0:T(1,128)S(1)} %stack.18, f32[2,768]{1,0:T(2,128)S(1)} %copy-done.80, f32[640,2]{1,0:T(8,128)S(1)} %bitcast.384, ...), kind=kLoop, calls=%fused_computation.83 | loop fusion | flops 8351744 | bytes 7894016 | tf_op jit(solution)/shard_map/reduce_sum | solution.py:321
  682.9 226.9 %while.37 = (s32[]{:T(128)}, f32[640,12,64]{0,2,1:T(8,128)}, bf16[5,512,1536]{2,1,0:T(8,128)(2,1)}, s32[5]{0:T(128)S(1)}, bf16[2560,768]{0,1:T(8,128)(2,1)}, /*i...) while((s32[]{:T(128)}, f32[640,12,64]{0,2,1:T(8,128)}, ...), condition=%wide.region_29.30_spmd.clone, body=%wide.region_28.29_spmd.clone.sunk | while | flops 2612937728 | bytes 166272848 | solution.py:394
  920.6 125.4 %reduce-scatter.19.cloned.1.call-done = bf16[640,1536]{1,0:T(8,128)(2,1)} async-done(((bf16[2560,1536]{1,0:T(8,128)(2,1)}), bf16[640,1536]{1,0:T(8,128)(2,1)}) %reduce-scatter.19.cloned.1.call-update) | async-done | bytes 1966096 | tf_op jit(solution)/shard_map/reduce_scatter | solution.py:399
  1065.7 10.8 fusion.179
  1076.6 10.8 fusion.180
  1107.8 30.9 %reduce-scatter.27.cloned.1.call-done = bf16[192,768]{1,0:T(8,128)(2,1)} async-done(((bf16[768,768]{1,0:T(8,128)(2,1)}), bf16[192,768]{1,0:T(8,128)(2,1)}) %reduce-scatter.27.cloned.1.call-update) | async-done | bytes 294928 | tf_op jit(solution)/shard_map/reduce_scatter | solution.py:450
  1157.7 11.8 reduce-scatter.21.cloned.1.call-done
  1169.5 30.2 %reduce-scatter.23.cloned.1.call-done = bf16[192,768]{1,0:T(8,128)(2,1)} async-done(((bf16[768,768]{1,0:T(8,128)(2,1)}), bf16[192,768]{1,0:T(8,128)(2,1)}) %reduce-scatter.23.cloned.1.call-update) | async-done | bytes 294928 | tf_op jit(solution)/shard_map/reduce_scatter | solution.py:444
  1199.7 30.3 %reduce-scatter.25.cloned.1.call-done = bf16[192,768]{1,0:T(8,128)(2,1)} async-done(((bf16[768,768]{1,0:T(8,128)(2,1)}), bf16[192,768]{1,0:T(8,128)(2,1)}) %reduce-scatter.25.cloned.1.call-update) | async-done | bytes 294928 | tf_op jit(solution)/shard_map/reduce_scatter | solution.py:447
  1230.1 75.6 %all-reduce.10 = (f32[192,768]{1,0:T(8,128)}, f32[192,768]{1,0:T(8,128)}, f32[192,768]{1,0:T(8,128)}, f32[192,768]{1,0:T(8,128)}, f32[192]{0:T(256)}, /*index=5*...) all-reduce(bf16[192,768]{1,0:T(8,128)(2,1)} %reduce-scatter.21.clon, ...), channel_id=1, replica_groups=mesh['expert'=4,'dp'=8] {'dp'}, use_global_device_ids=true, to_apply=%region_33.34 | all-reduce | flops 593700 | bytes 3563040 | tf_op jit(solution)/shard_map/psum | solution.py:483
  1306.3 39.4 %reduce-scatter.29.cloned.1.call-done = f32[2,96,2048]{2,1,0:T(8,128)} async-done(((f32[2,768,2048]{2,1,0:T(8,128)}), f32[2,96,2048]{2,1,0:T(8,128)}) %reduce-scatter.29.cloned.1.call-update) | async-done | bytes 1572880 | tf_op jit(solution)/shard_map/reduce_scatter | solution.py:306
  1345.8 96.8 %reduce-scatter.31.cloned.1.call-done = f32[2,96,2048]{2,1,0:T(8,128)} async-done(((f32[2,768,2048]{2,1,0:T(8,128)}), f32[2,96,2048]{2,1,0:T(8,128)}) %reduce-scatter.31.cloned.1.call-update) | async-done | bytes 1572880 | tf_op jit(solution)/shard_map/reduce_scatter | solution.py:307
  1442.5 96.8 %reduce-scatter.33.cloned.1.call-done = f32[2,256,768]{2,1,0:T(8,128)} async-done(((f32[2,2048,768]{2,1,0:T(8,128)}), f32[2,256,768]{2,1,0:T(8,128)}) %reduce-scatter.33.cloned.1.call-update) | async-done | bytes 1572880 | tf_op jit(solution)/shard_map/reduce_scatter | solution.py:308
  (558 shorter events, 642.4 us)
Async XLA Ops:
  7.2 83.6 %all-gather.8.cloned.1.call-start = ((), (), s32[]{:S(2)}) async-start(), calls=%async_computation.16 | async-start | bytes 4915200 | tf_op jit(solution)/shard_map/all_gather | solution.py:149
  12.1 155.9 %all-gather.6.cloned.1.call-start = ((), (), s32[]{:S(2)}) async-start(), calls=%async_computation.15 | async-start | bytes 4915200 | tf_op jit(solution)/shard_map/all_gather | solution.py:148
  24.6 409.9 %all-gather.10.cloned.1.call-start = ((), (), s32[]{:S(2)}) async-start(), calls=%async_computation.17 | async-start | bytes 7077888 | tf_op jit(solution)/shard_map/all_gather | solution.py:221
  25.4 420.8 %all-gather.12.cloned.1.call-start = ((), (), s32[]{:S(2)}) async-start(), calls=%async_computation.18 | async-start | bytes 7077888 | tf_op jit(solution)/shard_map/all_gather | solution.py:222
  26.0 431.8 %all-gather.14.cloned.1.call-start = ((), (), s32[]{:S(2)}) async-start(), calls=%async_computation.19 | async-start | bytes 7077888 | tf_op jit(solution)/shard_map/all_gather | solution.py:223
  334.7 49.9 %all-to-all-start = ((bf16[2,4,160,768]{3,2,0,1:T(8,128)(2,1)}), bf16[2,4,160,768]{3,2,0,1:T(8,128)(2,1)}, u32[]{:S(2)}, u32[]{:S(2)}) async-start(bf16[2,4,160,768]{3,2,0,1:T(8,128)(2,1)} %copy.169), calls=%async_computation | async-start | bytes 3932160 | tf_op jit(solution)/shard_map/all_to_all | solution.py:225
  384.7 48.4 %all-to-all-start.2 = ((bf16[2,4,160,768]{3,2,0,1:T(8,128)(2,1)}), bf16[2,4,160,768]{3,2,0,1:T(8,128)(2,1)S(1)}, u32[]{:S(2)}, u32[]{:S(2)}) async-start(bf16[2,4,160,768]{3,2,0,1:T(8,128)(2,1)} %copy.178), calls=%async_computation.2 | async-start | bytes 3932160 | tf_op jit(solution)/shard_map/all_to_all | solution.py:273
  495.9 49.5 %all-to-all-start.3 = ((bf16[2,4,160,768]{3,2,0,1:T(8,128)(2,1)}), bf16[2,4,160,768]{3,2,0,1:T(8,128)(2,1)}, u32[]{:S(2)}, u32[]{:S(2)}) async-start(bf16[2,4,160,768]{3,2,0,1:T(8,128)(2,1)} %copy.180), calls=%async_computation.3 | async-start | bytes 3932160 | tf_op jit(solution)/shard_map/all_to_all | solution.py:298
  513.5 36.4 %copy-start.7 = (bf16[640,768]{1,0:T(8,128)(2,1)S(1)}, bf16[640,768]{1,0:T(8,128)(2,1)}, u32[]{:S(2)}) copy-start(bf16[640,768]{1,0:T(8,128)(2,1)} %copy-done.6) | copy-start | bytes 2949124
  513.5 36.4 %copy-start.81 = (bf16[768,4]{0,1:T(4,128)(2,1)S(1)}, bf16[768,4]{0,1:T(4,128)(2,1)}, u32[]{:S(2)}) copy-start(bf16[768,4]{0,1:T(4,128)(2,1)} %param.35) | copy-start | bytes 18436
  513.5 38.6 %copy-start.36 = (f32[12,640]{1,0:T(8,128)S(1)}, f32[12,640]{1,0:T(8,128)}, u32[]{:S(2)}) copy-start(f32[12,640]{1,0:T(8,128)} %copy-done.35) | copy-start | bytes 92164
  545.4 49.4 %all-to-all-start.1 = ((bf16[2,4,160,768]{3,2,0,1:T(8,128)(2,1)}), bf16[2,4,160,768]{3,2,0,1:T(8,128)(2,1)}, u32[]{:S(2)}, u32[]{:S(2)}) async-start(bf16[2,4,160,768]{3,2,0,1:T(8,128)(2,1)} %copy.171), calls=%async_computation.1 | async-start | bytes 3932160 | tf_op jit(solution)/shard_map/all_to_all | solution.py:235
  549.9 496.2 %reduce-scatter.19.cloned.1.call-start = ((), (), s32[]{:S(2)}) async-start(), calls=%async_computation.20 | async-start | bytes 9830400 | tf_op jit(solution)/shard_map/reduce_scatter | solution.py:399
  909.9 192.4 %reduce-scatter.39.cloned.1.call-start = ((), (), s32[]{:S(2)}) async-start(), calls=%async_computation.30 | async-start | bytes 245760
  911.4 191.8 %reduce-scatter.37.cloned.1.call-start = ((), (), s32[]{:S(2)}) async-start(), calls=%async_computation.29 | async-start | bytes 245760
  912.8 194.1 %reduce-scatter.35.cloned.1.call-start = ((), (), s32[]{:S(2)}) async-start(), calls=%async_computation.28 | async-start | bytes 245760
  914.5 224.1 %reduce-scatter.27.cloned.1.call-start = ((), (), s32[]{:S(2)}) async-start(), calls=%async_computation.24 | async-start | bytes 1474560 | tf_op jit(solution)/shard_map/reduce_scatter | solution.py:450
  919.1 250.4 %reduce-scatter.21.cloned.1.call-start = ((), (), s32[]{:S(2)}) async-start(), calls=%async_computation.21 | async-start | bytes 1474560 | tf_op jit(solution)/shard_map/reduce_scatter | solution.py:441
  1058.6 141.1 %reduce-scatter.23.cloned.1.call-start = ((), (), s32[]{:S(2)}) async-start(), calls=%async_computation.22 | async-start | bytes 1474560 | tf_op jit(solution)/shard_map/reduce_scatter | solution.py:444
  1062.1 168.0 %reduce-scatter.25.cloned.1.call-start = ((), (), s32[]{:S(2)}) async-start(), calls=%async_computation.23 | async-start | bytes 1474560 | tf_op jit(solution)/shard_map/reduce_scatter | solution.py:447
  1065.7 280.1 %reduce-scatter.29.cloned.1.call-start = ((), (), s32[]{:S(2)}) async-start(), calls=%async_computation.25 | async-start | bytes 14155776 | tf_op jit(solution)/shard_map/reduce_scatter | solution.py:306
  1076.5 366.0 %reduce-scatter.31.cloned.1.call-start = ((), (), s32[]{:S(2)}) async-start(), calls=%async_computation.26 | async-start | bytes 14155776 | tf_op jit(solution)/shard_map/reduce_scatter | solution.py:307
  1087.4 451.9 %reduce-scatter.33.cloned.1.call-start = ((), (), s32[]{:S(2)}) async-start(), calls=%async_computation.27 | async-start | bytes 14155776 | tf_op jit(solution)/shard_map/reduce_scatter | solution.py:308
  1153.7 76.3 %copy-start.53 = (bf16[192,768]{1,0:T(8,128)(2,1)S(1)}, bf16[192,768]{1,0:T(8,128)(2,1)}, u32[]{:S(2)}) copy-start(bf16[192,768]{1,0:T(8,128)(2,1)} %reduce-scatter.27.cloned.1.call-done) | copy-start | bytes 884740
  (109 other events, 560.4 us)
Sparse Core Ops, SparseCore 0:
  12.2 78.5 all-gather.7
  92.9 75.0 all-gather.5
  169.9 44.5 all-gather.9
  216.2 45.5 all-gather.11
  263.5 45.5 all-gather.13
  910.0 136.0 reduce-scatter.18
  1048.3 17.6 reduce-scatter.38
  1068.9 17.5 reduce-scatter.36
  1089.3 17.5 reduce-scatter.34
  1109.2 29.4 reduce-scatter.26
  1141.1 28.4 reduce-scatter.20
  1171.8 27.8 reduce-scatter.22
  1202.1 27.8 reduce-scatter.24
  1234.4 111.3 reduce-scatter.28
  1350.1 92.4 reduce-scatter.30
  1446.9 92.3 reduce-scatter.32
where the time goes:
time: 1560 us; the launch traced here: 1550 us
  waiting for transfers between devices  697 us (45%)
  matrix products  406 us (26%)
  local copies, waits for them, and re-layouts  175 us (11%)
  other arithmetic  142 us (9%)
  blocking collectives  83.7 us (5%)
  starting transfers between devices  18.6 us (1%)
  between operations  16.8 us (1%)
    reduce_scatter x1, waiting for transfers between devices, per_device(): lax.psum_scatter(pair_terms.reshape(tree_length, 2 * model_width).astype(...  125 us
    reduce_scatter x1, waiting for transfers between devices, per_device(): lax.psum_scatter(up_local, 'dp', scatter_dimension=1, tiled=True)  96.8 us
    reduce_scatter x1, waiting for transfers between devices, per_device(): lax.psum_scatter(down_local, 'dp', scatter_dimension=1, tiled=True)  96.8 us
    psum x1, blocking collectives, per_device(): lax.psum((query_shard, key_shard, value_shard, out_shard, attention_shard...  75.6 us
    all_gather x1, waiting for transfers between devices, per_device(): lax.all_gather(keys_own, 'expert', axis=0, tiled=True)  70.9 us
    all_gather x1, waiting for transfers between devices, per_device(): lax.all_gather(values_own, 'expert', axis=0, tiled=True)  53.6 us
    dot_general x5, matrix products, backward_block(): jnp.einsum('hqk,qhd->khd', weights_now.astype(jnp.bfloat16), attn_grads,...  48.7 us
    reduce_sum x5, other arithmetic, forward_block(): running_sum = running_sum * factor + jnp.sum(weights_now, -1)  47.3 us
  transfers between devices with their start and end apart: 20, of which 15 were waited for; matrix products, arithmetic and copies ran while one was open for 23% of the time, Pallas kernels for 0%

commit v1 on v0

v1 whole, which is shorter than its diff:
```python
import jax
import jax.numpy as jnp
from jax import lax
from jax.experimental import pallas as pl
from jax.experimental.pallas import tpu as pltpu
from jax.sharding import Mesh
from jax.sharding import PartitionSpec as P

NFFN = 8
NEXP = 12
SEG = 128
HEAD_DIM = 64
TRUNK = 1024
TILE = 2 * SEG
LOG2E = 1.4426950408889634
masked_score = -1e30
MIB = 2**20
epsilon = 1e-06
precise = lax.Precision.HIGHEST


def dot_nt(left, right):
    return lax.dot_general(left, right, (((1,), (1,)), ((), ())), preferred_element_type=jnp.float32)


def dot_nn(left, right):
    return jnp.dot(left, right, preferred_element_type=jnp.float32)


def tile_parts(tile, start):
    trunk_tiles = TRUNK // TILE
    if tile is not None and tile < trunk_tiles:
        return [(k * TILE, False, k == tile) for k in range(tile + 1)]
    parts = [(k * TILE, False, False) for k in range(trunk_tiles)]
    branch_tiles = 2
    if tile is None:
        parts += [(TRUNK + k * TILE, True, False) for k in range(branch_tiles)]
    else:
        parts += [(TRUNK + k * TILE, True, False) for k in range(tile - trunk_tiles)]
    parts += [(start, True, True)]
    return parts


def causal_bias():
    key_ids = lax.broadcasted_iota(jnp.int32, (TILE, TILE), 0)
    query_ids = lax.broadcasted_iota(jnp.int32, (TILE, TILE), 1)
    return jnp.where(key_ids <= query_ids, 0.0, masked_score).astype(jnp.float32)


def part_scores(scores, part, columns, bias_ref, triangle):
    first, by_lineage, causal = part
    if by_lineage:
        segment = 1 + (first - TRUNK) // SEG
        rows = [bias_ref[pl.ds(segment + i, 1), columns] for i in range(TILE // SEG)]
        scores = jnp.concatenate(
            [scores[i * SEG : (i + 1) * SEG] + rows[i] for i in range(TILE // SEG)], 0
        )
    if causal:
        scores = scores + triangle[...]
    return scores


def for_tiles(length, body):
    trunk_tiles = TRUNK // TILE
    for tile in range(trunk_tiles + 2):
        body(tile, tile * TILE)
    first_leaf = trunk_tiles + 2

    @pl.loop(first_leaf, length // TILE)
    def _(tile):
        body(None, pl.multiple_of(tile * TILE, TILE))


def attend_kernel(bias_ref, qkv_ref, out_ref, lse_ref, q_ref, k_ref, v_ref, o_ref, s_ref, triangle):
    sources, _, rows = qkv_ref.shape
    length = sources * rows
    factor = HEAD_DIM ** (-0.5) * LOG2E
    triangle[...] = causal_bias()
    extra = lax.broadcasted_iota(jnp.int32, (16, length), 0)
    v_ref[HEAD_DIM:, :] = jnp.where(extra == 0, 1.0, 0.0).astype(jnp.bfloat16)
    for z in range(sources):
        span = pl.ds(z * rows, rows)
        q_ref[:, span] = qkv_ref[z, :HEAD_DIM]
        k_ref[span, :] = qkv_ref[z, HEAD_DIM : 2 * HEAD_DIM].astype(jnp.float32).T.astype(jnp.bfloat16)
        v_ref[:HEAD_DIM, span] = qkv_ref[z, 2 * HEAD_DIM :]

    def body(tile, start):
        columns = pl.ds(start, TILE)
        parts = tile_parts(tile, start)
        query = q_ref[:, columns]
        peak = None
        for i, part in enumerate(parts):
            scores = dot_nn(k_ref[pl.ds(part[0], TILE), :], query)
            scores = part_scores(scores, part, columns, bias_ref, triangle)
            s_ref[i * TILE : (i + 1) * TILE, :] = scores
            top = jnp.max(scores, 0, keepdims=True)
            peak = top if peak is None else jnp.maximum(peak, top)
        shift = peak * factor
        total = None
        for i, part in enumerate(parts):
            weights = jnp.exp2(s_ref[i * TILE : (i + 1) * TILE, :] * factor - shift)
            term = dot_nn(v_ref[:, pl.ds(part[0], TILE)], weights.astype(jnp.bfloat16))
            total = term if total is None else total + term
        norm = total[HEAD_DIM : HEAD_DIM + 1]
        o_ref[:, columns] = (total[:HEAD_DIM] / norm).astype(jnp.bfloat16)
        lse_ref[:, columns] = shift + jnp.log2(norm)

    for_tiles(length, body)
    for z in range(sources):
        out_ref[z] = o_ref[:, pl.ds(z * rows, rows)]


def attend(bias, qkv):
    sources, _, rows = qkv.shape
    length = sources * rows
    part_total = TRUNK // TILE + 3
    return pl.pallas_call(
        attend_kernel,
        out_shape=(
            jax.ShapeDtypeStruct((sources, HEAD_DIM, rows), jnp.bfloat16),
            jax.ShapeDtypeStruct((1, length), jnp.float32),
        ),
        scratch_shapes=[
            pltpu.VMEM((HEAD_DIM, length), jnp.bfloat16),
            pltpu.VMEM((length, HEAD_DIM), jnp.bfloat16),
            pltpu.VMEM((HEAD_DIM + 16, length), jnp.bfloat16),
            pltpu.VMEM((HEAD_DIM, length), jnp.bfloat16),
            pltpu.VMEM((part_total * TILE, TILE), jnp.float32),
            pltpu.VMEM((TILE, TILE), jnp.float32),
        ],
        compiler_params=pltpu.CompilerParams(vmem_limit_bytes=48 * MIB),
        cost_estimate=pl.CostEstimate(flops=2 * 10**9, bytes_accessed=4 * 10**6, transcendentals=3 * 10**6),
    )(bias, qkv)


def attend_back_kernel(
    bias_ref, cos_ref, sin_ref, qkv_ref, out_ref, lse_ref, grad_ref, back_ref,
    qt_ref, kt_ref, dt_ref, q_ref, k_ref, v_ref, d_ref, delta_ref, dq_ref, dk_ref, dv_ref, triangle,
):
    sources, _, rows = qkv_ref.shape
    length = sources * rows
    scaling = HEAD_DIM ** (-0.5)
    factor = scaling * LOG2E
    triangle[...] = causal_bias()

    def turned(values):
        return values.astype(jnp.float32).T.astype(jnp.bfloat16)

    for z in range(sources):
        span = pl.ds(z * rows, rows)
        query, key, value = (qkv_ref[z, i * HEAD_DIM : (i + 1) * HEAD_DIM] for i in range(3))
        grad = grad_ref[z]
        qt_ref[:, span] = query
        kt_ref[:, span] = key
        dt_ref[:, span] = grad
        q_ref[span, :] = turned(query)
        k_ref[span, :] = turned(key)
        v_ref[span, :] = turned(value)
        d_ref[span, :] = turned(grad)
        delta_ref[:, span] = jnp.sum(
            grad.astype(jnp.float32) * out_ref[z].astype(jnp.float32), 0, keepdims=True
        )
    dk_ref[...] = jnp.zeros_like(dk_ref)
    dv_ref[...] = jnp.zeros_like(dv_ref)

    def body(tile, start):
        columns = pl.ds(start, TILE)
        query_t, grad_t = qt_ref[:, columns], dt_ref[:, columns]
        query, grad = q_ref[columns, :], d_ref[columns, :]
        lse, delta = lse_ref[:, columns], delta_ref[:, columns]
        total = None
        for part in tile_parts(tile, start):
            span = pl.ds(part[0], TILE)
            scores = dot_nn(k_ref[span, :], query_t) * factor - lse
            scores = part_scores(scores, part, columns, bias_ref, triangle)
            weights = jnp.exp2(scores)
            weight_grads = dot_nn(v_ref[span, :], grad_t)
            score_grads = (weights * (weight_grads - delta)).astype(jnp.bfloat16)
            dv_ref[span, :] += dot_nn(weights.astype(jnp.bfloat16), grad)
            dk_ref[span, :] += dot_nn(score_grads, query)
            term = dot_nn(kt_ref[:, span], score_grads)
            total = term if total is None else total + term
        dq_ref[:, columns] = total

    for_tiles(length, body)
    half = HEAD_DIM // 2
    for z in range(sources):
        span = pl.ds(z * rows, rows)
        cosine, sine = cos_ref[:, span], sin_ref[:, span]
        for i, values in enumerate((dq_ref[:, span], dk_ref[span, :].T)):
            values = values * scaling
            first, second = values[:half], values[half:]
            back_ref[z, i * HEAD_DIM : (i + 1) * HEAD_DIM] = jnp.concatenate(
                [first * cosine + second * sine, second * cosine - first * sine], 0
            ).astype(jnp.bfloat16)
        back_ref[z, 2 * HEAD_DIM :] = dv_ref[span, :].T.astype(jnp.bfloat16)


def attend_back(bias, cosine, sine, qkv, out, lse, grad):
    sources, _, rows = qkv.shape
    length = sources * rows
    turned = pltpu.VMEM((HEAD_DIM, length), jnp.bfloat16)
    plain = pltpu.VMEM((length, HEAD_DIM), jnp.bfloat16)
    wide = pltpu.VMEM((length, HEAD_DIM), jnp.float32)
    return pl.pallas_call(
        attend_back_kernel,
        out_shape=jax.ShapeDtypeStruct((sources, 3 * HEAD_DIM, rows), jnp.bfloat16),
        scratch_shapes=[
            turned, turned, turned, plain, plain, plain, plain,
            pltpu.VMEM((1, length), jnp.float32),
            pltpu.VMEM((HEAD_DIM, length), jnp.float32),
            wide, wide,
            pltpu.VMEM((TILE, TILE), jnp.float32),
        ],
        compiler_params=pltpu.CompilerParams(vmem_limit_bytes=48 * MIB),
        cost_estimate=pl.CostEstimate(flops=5 * 10**9, bytes_accessed=6 * 10**6, transcendentals=3 * 10**6),
    )(bias, cosine, sine, qkv, out, lse, grad)


def params(limit):
    return pltpu.CompilerParams(vmem_limit_bytes=limit * MIB)


def cost(flops, moved):
    return pl.CostEstimate(flops=int(flops), bytes_accessed=int(moved), transcendentals=0)


def project_kernel(tokens_ref, gain_ref, query_ref, key_ref, value_ref, cos_ref, sin_ref, out_ref):
    inputs = tokens_ref[...].astype(jnp.float32)
    inverse = lax.rsqrt(jnp.mean(inputs * inputs, -1, keepdims=True) + epsilon)
    normed = (inputs * inverse * gain_ref[...]).astype(jnp.bfloat16)
    half = HEAD_DIM // 2
    cosine, sine = cos_ref[...], sin_ref[...]
    for i, weight in enumerate((query_ref, key_ref, value_ref)):
        turned = dot_nn(normed, weight[...]).T
        for z in range(out_ref.shape[0]):
            first = turned[z * HEAD_DIM : z * HEAD_DIM + half]
            second = turned[z * HEAD_DIM + half : (z + 1) * HEAD_DIM]
            if i < 2:
                first, second = first * cosine - second * sine, second * cosine + first * sine
            base = i * HEAD_DIM
            out_ref[z, base : base + half] = first.astype(jnp.bfloat16)
            out_ref[z, base + half : base + HEAD_DIM] = second.astype(jnp.bfloat16)


def project(chunk, owners, tokens, gain, weights, cosine, sine):
    rows, width = tokens.shape
    columns = owners * HEAD_DIM
    whole = lambda shape: pl.BlockSpec(shape, lambda i: (0,) * len(shape))
    part = pl.BlockSpec((width, columns), lambda i: (0, chunk))
    return pl.pallas_call(
        project_kernel,
        grid=(1,),
        in_specs=[whole((rows, width)), whole((1, width)), part, part, part]
        + [whole((HEAD_DIM // 2, rows))] * 2,
        out_specs=whole((owners, 3 * HEAD_DIM, rows)),
        out_shape=jax.ShapeDtypeStruct((owners, 3 * HEAD_DIM, rows), jnp.bfloat16),
        compiler_params=params(48),
        cost_estimate=cost(6 * rows * width * columns, 4e6),
    )(tokens, gain, *weights, cosine, sine)


def lane_pick(values, lanes, index):
    return jnp.sum(jnp.where(lanes == index, values, 0.0), -1, keepdims=True)


def middle_kernel(
    tokens_ref, a0_ref, a1_ref, a2_ref, out_weight_ref, gain_ref, mixer_ref, prior_ref, prior_weight_ref,
    routes_ref, codes_ref, resid_ref, small_ref, first_ref, second_ref, hidden_ref,
):
    rows, width = tokens_ref.shape

    @pl.loop(0, rows // SEG)
    def _(step):
        span = pl.ds(pl.multiple_of(step * SEG, SEG), SEG)
        attended = jnp.concatenate([ref[:, span] for ref in (a0_ref, a1_ref, a2_ref)], 0)
        attended = attended.astype(jnp.float32).T.astype(jnp.bfloat16)
        resid = tokens_ref[span, :].astype(jnp.float32) + dot_nn(attended, out_weight_ref[...])
        inverse = lax.rsqrt(jnp.mean(resid * resid, -1, keepdims=True) + epsilon)
        hidden = (resid * inverse * gain_ref[...]).astype(jnp.bfloat16)
        resid_ref[span, :] = resid
        hidden_ref[span, :] = hidden
        logits = dot_nn(hidden, mixer_ref[...])
        logits = logits + jnp.dot(
            prior_ref[span, :], prior_weight_ref[...], precision=precise, preferred_element_type=jnp.float32
        )
        lanes = lax.broadcasted_iota(jnp.int32, logits.shape, 1)
        routes = routes_ref[span, :]
        columns = []
        pairs = [[lane_pick(logits, lanes, routes[:, c : c + 1]) for c in range(2)]]
        pairs += [[logits[:, NEXP + 2 * m + c : NEXP + 2 * m + c + 1] for c in range(2)] for m in range(2)]
        for one, two in pairs:
            peak = jnp.maximum(one, two)
            one, two = jnp.exp(one - peak), jnp.exp(two - peak)
            columns += [one / (one + two), two / (one + two)]
        columns.append(inverse)
        small = jnp.zeros_like(logits)
        for i, column in enumerate(columns):
            small = jnp.where(lanes == i, column, small)
        small_ref[span, :] = small

    slots = first_ref.shape[0]
    for half, ref in enumerate((first_ref, second_ref)):
        index = lax.broadcasted_iota(jnp.int32, (slots, rows), 0) + half * slots
        chosen = (codes_ref[0:1, :] == index) | (codes_ref[1:2, :] == index)
        ref[...] = dot_nn(chosen.astype(jnp.bfloat16), hidden_ref[...]).astype(jnp.bfloat16)


def middle(tokens, attended, out_weight, gain, mixer, prior, prior_weight, routes, codes_row):
    rows, width = tokens.shape
    slots = rows
    return pl.pallas_call(
        middle_kernel,
        out_shape=(
            jax.ShapeDtypeStruct((rows, width), jnp.float32),
            jax.ShapeDtypeStruct((rows, 128), jnp.float32),
            jax.ShapeDtypeStruct((slots, width), jnp.bfloat16),
            jax.ShapeDtypeStruct((slots, width), jnp.bfloat16),
        ),
        scratch_shapes=[pltpu.VMEM((rows, width), jnp.bfloat16)],
        compiler_params=params(48),
        cost_estimate=cost(4 * rows * width * width + 4 * rows * rows * width, 1e7),
    )(tokens, *attended, out_weight, gain, mixer, prior, prior_weight, routes, codes_row)


def scatter_kernel(small_ref, grad_ref, codes_ref, first_ref, second_ref, scaled_ref):
    rows, width = grad_ref.shape
    small = small_ref[...]
    grad = grad_ref[...].astype(jnp.float32)
    for c in range(2):
        scaled_ref[c * rows : (c + 1) * rows, :] = (small[:, c : c + 1] * grad).astype(jnp.bfloat16)
    slots = first_ref.shape[0]
    for half, ref in enumerate((first_ref, second_ref)):
        index = lax.broadcasted_iota(jnp.int32, (slots, rows), 0) + half * slots
        chosen = jnp.concatenate([(codes_ref[c : c + 1, :] == index).astype(jnp.bfloat16) for c in range(2)], 1)
        ref[...] = dot_nn(chosen, scaled_ref[...]).astype(jnp.bfloat16)


def scatter(small, grad, codes_row):
    rows, width = grad.shape
    return pl.pallas_call(
        scatter_kernel,
        out_shape=(jax.ShapeDtypeStruct((rows, width), jnp.bfloat16),) * 2,
        scratch_shapes=[pltpu.VMEM((2 * rows, width), jnp.bfloat16)],
        compiler_params=params(48),
        cost_estimate=cost(8 * rows * rows * width, 4e6),
    )(small, grad, codes_row)


def expert_kernel(
    x_ref, d_ref, gate_ref, up_ref, down_ref, f_ref, back_ref, dots_ref, hid_ref, dg_ref, du_ref, f_sum, back_sum
):
    step = pl.program_id(0)
    rows = x_ref.shape[0]
    part = rows // 2
    for r in range(2):
        span = pl.ds(r * part, part)
        x, d = x_ref[span, :], d_ref[span, :]
        gate_pre = dot_nn(x, gate_ref[...])
        up_pre = dot_nn(x, up_ref[...])
        mid = dot_nt(d, down_ref[...])
        sigmoid = 1.0 / (1.0 + jnp.exp(-gate_pre))
        active = gate_pre * sigmoid
        hid = (active * up_pre).astype(jnp.bfloat16)
        du = (mid * active).astype(jnp.bfloat16)
        dg = (mid * up_pre * (sigmoid + active * (1.0 - sigmoid))).astype(jnp.bfloat16)
        hid_ref[span, :] = hid
        du_ref[span, :] = du
        dg_ref[span, :] = dg
        f_term = dot_nn(hid, down_ref[...])
        back_term = dot_nt(dg, gate_ref[...]) + dot_nt(du, up_ref[...])

        @pl.when(step == 0)
        def _():
            f_sum[span, :] = f_term
            back_sum[span, :] = back_term

        @pl.when(step > 0)
        def _():
            f_sum[span, :] += f_term
            back_sum[span, :] += back_term

    @pl.when(step == pl.num_programs(0) - 1)
    def _():
        back_ref[...] = back_sum[...].astype(jnp.bfloat16)
        f = f_sum[...].astype(jnp.bfloat16)
        f_ref[...] = f
        dots = jnp.sum(f.astype(jnp.float32) * d_ref[...].astype(jnp.float32), -1, keepdims=True)
        dots_ref[...] = jnp.broadcast_to(dots, (rows, 128)).T[:8]


def expert(x, d, gate, up, down):
    rows, width = x.shape
    units = gate.shape[1]
    part = 512
    whole = pl.BlockSpec((rows, width), lambda i: (0, 0))
    columns = pl.BlockSpec((width, part), lambda i: (0, i))
    mids = pl.BlockSpec((rows, part), lambda i: (0, i))
    return pl.pallas_call(
        expert_kernel,
        grid=(units // part,),
        in_specs=[whole, whole, columns, columns, pl.BlockSpec((part, width), lambda i: (i, 0))],
        out_specs=(whole, whole, pl.BlockSpec((8, rows), lambda i: (0, 0)), mids, mids, mids),
        out_shape=(
            jax.ShapeDtypeStruct((rows, width), jnp.bfloat16),
            jax.ShapeDtypeStruct((rows, width), jnp.bfloat16),
            jax.ShapeDtypeStruct((8, rows), jnp.float32),
        )
        + (jax.ShapeDtypeStruct((rows, units), jnp.bfloat16),) * 3,
        scratch_shapes=[pltpu.VMEM((rows, width), jnp.float32)] * 2,
        compiler_params=params(52),
        cost_estimate=cost(12 * rows * width * units, 3e7),
    )(x, d, gate, up, down)


def weights_kernel(
    xa_ref, xb_ref, da_ref, db_ref, ha_ref, hb_ref, ga_ref, gb_ref, ua_ref, ub_ref,
    gate_ref, up_ref, down_ref, x_turned, d_turned,
):
    rows = xa_ref.shape[0]

    @pl.when(pl.program_id(0) == 0)
    def _():
        for i, (x, d) in enumerate(((xa_ref, da_ref), (xb_ref, db_ref))):
            span = pl.ds(i * rows, rows)
            x_turned[:, span] = x[...].astype(jnp.float32).T.astype(jnp.bfloat16)
            d_turned[:, span] = d[...].astype(jnp.float32).T.astype(jnp.bfloat16)

    both = lambda one, two: jnp.concatenate([one[...], two[...]], 0)
    gate_ref[...] = dot_nn(x_turned[...], both(ga_ref, gb_ref)).astype(jnp.bfloat16)
    up_ref[...] = dot_nn(x_turned[...], both(ua_ref, ub_ref)).astype(jnp.bfloat16)
    down_ref[...] = dot_nn(d_turned[...], both(ha_ref, hb_ref)).T.astype(jnp.bfloat16)


def weight_grads(xs, ds, hids, gates, ups):
    rows, width = xs[0].shape
    units = hids[0].shape[1]
    part = 256
    whole = pl.BlockSpec((rows, width), lambda i: (0, 0))
    mids = pl.BlockSpec((rows, part), lambda i: (0, i))
    columns = pl.BlockSpec((width, part), lambda i: (0, i))
    return pl.pallas_call(
        weights_kernel,
        grid=(units // part,),
        in_specs=[whole] * 4 + [mids] * 6,
        out_specs=(columns, columns, pl.BlockSpec((part, width), lambda i: (i, 0))),
        out_shape=(
            jax.ShapeDtypeStruct((width, units), jnp.bfloat16),
            jax.ShapeDtypeStruct((width, units), jnp.bfloat16),
            jax.ShapeDtypeStruct((units, width), jnp.bfloat16),
        ),
        scratch_shapes=[pltpu.VMEM((width, 2 * rows), jnp.bfloat16)] * 2,
        compiler_params=params(52),
        cost_estimate=cost(12 * rows * width * units, 3e7),
    )(*xs, *ds, *hids, *gates, *ups)


def split_dot(dot, left, right):
    high = left.astype(jnp.bfloat16)
    low = (left - high.astype(jnp.float32)).astype(jnp.bfloat16)
    return dot(high, right) + dot(low, right)


def turn_kernel(
    resid_ref, small_ref, grad_ref, prior_ref, routes_ref, codes_ref, ra_ref, rb_ref, dots_ref, vector_ref,
    gain_ref, mixer_ref, prior_turned_ref, out_weight_ref, a0_ref, a1_ref, a2_ref,
    resid_grad_ref, g0_ref, g1_ref, g2_ref, out_grad_ref, sums_ref, prior_sums_ref, prior_grad_ref, back_ref,
):
    rows, width = resid_ref.shape
    slots = 2 * ra_ref.shape[0]
    sums_ref[...] = jnp.zeros_like(sums_ref)
    prior_sums_ref[...] = jnp.zeros_like(prior_sums_ref)

    @pl.loop(0, rows // SEG)
    def _(step):
        span = pl.ds(pl.multiple_of(step * SEG, SEG), SEG)
        small = small_ref[span, :]
        routes, codes = routes_ref[span, :], codes_ref[span, :]
        gates = [small[:, c : c + 1] for c in range(2)]
        mixing = [[small[:, 2 + 2 * m + c : 3 + 2 * m + c] for c in range(2)] for m in range(2)]
        inverse = small[:, 6:7]
        normed = resid_ref[span, :] * inverse
        hidden = normed * gain_ref[...]
        hidden_b = hidden.astype(jnp.bfloat16)
        grad_b = grad_ref[span, :]
        grad = grad_b.astype(jnp.float32)
        index = lax.broadcasted_iota(jnp.int32, (SEG, slots), 1)
        hits = [codes[:, c : c + 1] == index for c in range(2)]
        dots = dots_ref[...]
        terms = [jnp.sum(jnp.where(hit, dots, 0.0), -1, keepdims=True) for hit in hits]
        chosen = (hits[0] | hits[1]).astype(jnp.bfloat16)
        half = slots // 2
        routed = dot_nn(chosen[:, :half], ra_ref[...]) + dot_nn(chosen[:, half:], rb_ref[...])
        along = jnp.sum(grad * hidden, -1, keepdims=True)
        across = [jnp.sum(grad * vector_ref[m : m + 1, :], -1, keepdims=True) for m in range(2)]
        to_copy = 0.0
        to_mix = [0.0, 0.0]
        for c in range(2):
            route = routes[:, c : c + 1]
            copied = jnp.where(route == NFFN + 1, gates[c], 0.0)
            to_copy = to_copy + copied
            terms[c] = terms[c] + copied * along
            for m in range(2):
                mixed = jnp.where(route == NFFN + 2 + m, gates[c], 0.0)
                to_mix[m] = to_mix[m] + mixed
                terms[c] = terms[c] + mixed * (mixing[m][0] * along + mixing[m][1] * across[m])
        both = terms[0] + terms[1]
        lanes = lax.broadcasted_iota(jnp.int32, (SEG, 128), 1)
        logit_grads = jnp.zeros((SEG, 128), jnp.float32)
        for c in range(2):
            logit_grads = jnp.where(lanes == routes[:, c : c + 1], terms[c] - gates[c] * both, logit_grads)
        scores = logit_grads
        direct = to_copy
        for m in range(2):
            pair = (to_mix[m] * along, to_mix[m] * across[m])
            mean = mixing[m][0] * pair[0] + mixing[m][1] * pair[1]
            for c in range(2):
                scores = jnp.where(lanes == NEXP + 2 * m + c, mixing[m][c] * (pair[c] - mean), scores)
            direct = direct + mixing[m][0] * to_mix[m]
        prior_grad_ref[span, :] = jnp.dot(
            logit_grads, prior_turned_ref[...], precision=precise, preferred_element_type=jnp.float32
        )[:, : prior_grad_ref.shape[1]]
        hidden_grads = split_dot(dot_nn, scores, mixer_ref[...]) + direct * grad + routed
        scaled = hidden_grads * gain_ref[...]
        resid_grads = inverse * (scaled - normed * jnp.mean(scaled * normed, -1, keepdims=True)) + grad
        resid_grad_ref[span, :] = resid_grads
        back_ref[span, :] = resid_grads.astype(jnp.bfloat16)
        weights = jnp.zeros((SEG, 128), jnp.float32)
        for m in range(2):
            weights = jnp.where(lanes == m, mixing[m][1] * to_mix[m], weights)
        sums_ref[0:16, :] += split_dot(dot_nn, scores.T[0:16], hidden_b)
        sums_ref[16:24, :] += split_dot(dot_nn, weights.T[0:8], grad_b)
        sums_ref[24:32, :] += jnp.sum((hidden_grads * normed).reshape(SEG // 8, 8, width), 0)
        prior_sums_ref[...] += jnp.dot(
            prior_ref[span, :].T, logit_grads, precision=precise, preferred_element_type=jnp.float32
        )

    back = back_ref[...]
    part = a0_ref.shape[0]
    for j, (a_ref, g_ref) in enumerate(((a0_ref, g0_ref), (a1_ref, g1_ref), (a2_ref, g2_ref))):
        span = pl.ds(j * part, part)
        g_ref[...] = dot_nt(out_weight_ref[span, :], back).astype(jnp.bfloat16)
        out_grad_ref[span, :] = dot_nn(a_ref[...], back).astype(jnp.bfloat16)


def turn(resid, small, grad, prior, routes, codes, returned, dots, vector, gain, mixer_turned, prior_turned, out_weight, attended):
    rows, width = resid.shape
    part = attended[0].shape[0]
    return pl.pallas_call(
        turn_kernel,
        out_shape=(
            jax.ShapeDtypeStruct((rows, width), jnp.float32),
            *(jax.ShapeDtypeStruct((part, rows), jnp.bfloat16),) * 3,
            jax.ShapeDtypeStruct((width, width), jnp.bfloat16),
            jax.ShapeDtypeStruct((32, width), jnp.float32),
            jax.ShapeDtypeStruct((prior.shape[1], 128), jnp.float32),
            jax.ShapeDtypeStruct(prior.shape, jnp.float32),
        ),
        scratch_shapes=[pltpu.VMEM((rows, width), jnp.bfloat16)],
        compiler_params=params(56),
        cost_estimate=cost(4 * rows * width * width + 4 * rows * rows * width, 1.5e7),
    )(resid, small, grad, prior, routes, codes, *returned, dots, vector, gain, mixer_turned, prior_turned, out_weight, *attended)


def combine_kernel(resid_ref, small_ref, routes_ref, codes_ref, fa_ref, fb_ref, vector_ref, gain_ref, out_ref):
    rows, width = resid_ref.shape
    half = fa_ref.shape[0]

    @pl.loop(0, rows // SEG)
    def _(step):
        span = pl.ds(pl.multiple_of(step * SEG, SEG), SEG)
        small = small_ref[span, :]
        routes, codes = routes_ref[span, :], codes_ref[span, :]
        resid = resid_ref[span, :]
        hidden = resid * small[:, 6:7] * gain_ref[...]
        index = lax.broadcasted_iota(jnp.int32, (SEG, 2 * half), 1)
        total = resid
        direct = 0.0
        for c in range(2):
            gate, route = small[:, c : c + 1], routes[:, c : c + 1]
            chosen = (codes[:, c : c + 1] == index).astype(jnp.bfloat16)
            routed = dot_nn(chosen[:, :half], fa_ref[...]) + dot_nn(chosen[:, half:], fb_ref[...])
            total = total + gate * routed
            direct = direct + jnp.where(route == NFFN + 1, gate, 0.0)
            for m in range(2):
                mixed = jnp.where(route == NFFN + 2 + m, gate, 0.0)
                direct = direct + mixed * small[:, 2 + 2 * m : 3 + 2 * m]
                total = total + mixed * small[:, 3 + 2 * m : 4 + 2 * m] * vector_ref[m : m + 1, :]
        out_ref[span, :] = (total + direct * hidden).astype(jnp.bfloat16)


def combine(resid, small, routes, codes, outs, vector, gain):
    rows, width = resid.shape
    return pl.pallas_call(
        combine_kernel,
        out_shape=jax.ShapeDtypeStruct((rows, width), jnp.bfloat16),
        compiler_params=params(48),
        cost_estimate=cost(8 * rows * rows * width, 8e6),
    )(resid, small, routes, codes, *outs, vector, gain)


def last_kernel(
    tokens_ref, gain_ref, b0_ref, b1_ref, b2_ref, query_ref, key_ref, value_ref, resid_grad_ref,
    tokens_grad_ref, weight_grad_ref, normed_turned, back_turned,
):
    rows, width = tokens_ref.shape
    inputs = tokens_ref[...].astype(jnp.float32)
    inverse = lax.rsqrt(jnp.mean(inputs * inputs, -1, keepdims=True) + epsilon)
    normed = inputs * inverse
    normed_turned[...] = (normed * gain_ref[...]).T.astype(jnp.bfloat16)
    owners = b0_ref.shape[0]
    for i in range(3):
        for j, ref in enumerate((b0_ref, b1_ref, b2_ref)):
            for z in range(owners):
                head = j * owners + z
                back_turned[i, head * HEAD_DIM : (head + 1) * HEAD_DIM, :] = ref[z, i * HEAD_DIM : (i + 1) * HEAD_DIM]
    total = None
    for i, ref in enumerate((query_ref, key_ref, value_ref)):
        term = dot_nn(ref[...], back_turned[i])
        total = term if total is None else total + term
        weight_grad_ref[:, i * width : (i + 1) * width] = dot_nt(normed_turned[...], back_turned[i]).astype(jnp.bfloat16)
    first_grads = total.T
    summed = jnp.sum((first_grads * normed).reshape(rows // 8, 8, width), 0)
    column = jnp.sum(summed.T, -1, keepdims=True)
    weight_grad_ref[:, 3 * width :] = jnp.broadcast_to(column, (width, 128)).astype(jnp.bfloat16)
    scaled = first_grads * gain_ref[...]
    tokens_grad_ref[...] = (
        inverse * (scaled - normed * jnp.mean(scaled * normed, -1, keepdims=True)) + resid_grad_ref[...]
    )


def last(tokens, gain, backs, weights, resid_grads):
    rows, width = tokens.shape
    return pl.pallas_call(
        last_kernel,
        out_shape=(
            jax.ShapeDtypeStruct((rows, width), jnp.float32),
            jax.ShapeDtypeStruct((width, 3 * width + 128), jnp.bfloat16),
        ),
        scratch_shapes=[
            pltpu.VMEM((width, rows), jnp.bfloat16),
            pltpu.VMEM((3, width, rows), jnp.bfloat16),
        ],
        compiler_params=params(56),
        cost_estimate=cost(12 * rows * width * width, 2e7),
    )(tokens, gain, *backs, *weights, resid_grads)


def lineage_of(parent_row):
    segment_total = parent_row.shape[0] + 1
    indices = jnp.arange(segment_total, dtype=jnp.int32)
    parent_all = jnp.concatenate([jnp.full((1,), -1, jnp.int32), parent_row])
    reach = (parent_all[:, None] == indices[None, :]) | (indices[:, None] == indices[None, :])
    for repeat in range(3):
        reach = jnp.any(reach[:, :, None] & reach[None, :, :], 1)
    return reach


def slot_codes(routes, half_slots):
    rows = routes.shape[0]
    experts = jnp.arange(NFFN, dtype=jnp.int32)
    matches = routes[:, :, None] == experts
    per_row = jnp.sum(matches.astype(jnp.float32), 1)
    earlier = jnp.arange(rows)[:, None] > jnp.arange(rows)[None, :]
    before = jnp.dot(
        earlier.astype(jnp.bfloat16), per_row.astype(jnp.bfloat16), preferred_element_type=jnp.float32
    )
    rank = jnp.sum(jnp.where(matches, before[:, None, :], 0.0), -1).astype(jnp.int32)
    late = (rank >= half_slots).astype(jnp.int32)
    code = late * (NFFN * half_slots) + routes * half_slots + rank - late * half_slots
    return jnp.where(routes < NFFN, code, 4 * NFFN * half_slots)


def per_device(
    tokens, prior_logits, routes, parents, cotangent, query_weight, key_weight, value_weight, out_weight,
    attention_gain, expert_gain, router_weight, prior_weight, constant_weight, constant_vector,
    gate_weight, up_weight, down_weight,
):
    owners = lax.axis_size("expert")
    member = lax.axis_index("expert")
    core = lax.axis_index("core")
    tokens, prior, routes, grad = tokens[0], prior_logits[0], routes[0], cotangent[0]
    rows, width = tokens.shape
    length = rows * owners
    chunks = width // HEAD_DIM // owners
    half_slots = rows // 8
    planes, everyone = ("expert", "core"), ("expert", "xy", "core")

    def swap(values):
        return lax.ppermute(values, "core", [(0, 1), (1, 0)])

    def exchange(values, axes):
        return lax.all_to_all(values, axes, split_axis=0, concat_axis=0, tiled=True)

    def gather_weight(weight):
        mine = jnp.where(core == 0, weight[0], weight[1])
        other = swap(jnp.where(core == 0, weight[1], weight[0]))
        pair = jnp.concatenate([jnp.where(core == 0, mine, other), jnp.where(core == 0, other, mine)], 0)
        return lax.all_gather(pair, "xy", axis=0, tiled=True)

    def scatter_weight(grads):
        part = lax.psum_scatter(grads, "xy", scatter_dimension=0, tiled=True)
        part = part.reshape(2, part.shape[0] // 2, part.shape[1])
        mine = jnp.where(core == 0, part[0], part[1])
        other = swap(jnp.where(core == 0, part[1], part[0]))
        return jnp.stack(
            [jnp.where(core == 0, mine, other), jnp.where(core == 0, other, mine)], 0
        ).astype(jnp.float32)

    lineage = lineage_of(parents[0])
    segments = lineage.shape[0]
    lengths = jnp.where(jnp.arange(segments) == 0, TRUNK, SEG)
    begins = jnp.where(jnp.arange(segments) == 0, 0, TRUNK + (jnp.arange(segments) - 1) * SEG)
    shifts = jnp.sum(jnp.where(lineage, lengths[None, :], 0), 1) - lengths - begins
    ids = jnp.arange(length, dtype=jnp.int32)
    segment = jnp.where(ids < TRUNK, 0, 1 + (ids - TRUNK) // SEG)
    own = segment[None, :] == jnp.arange(segments)[:, None]
    places = (jnp.sum(jnp.where(own, shifts[:, None], 0), 0) + ids).astype(jnp.float32)
    reach = jnp.any(own[:, None, :] & lineage[:, :, None], 0)
    bias = jnp.where(reach, 0.0, masked_score).astype(jnp.float32)
    bias = jnp.concatenate([bias, jnp.zeros((16 - segments, length), jnp.float32)], 0)
    frequency = 10000.0 ** (-(jnp.arange(HEAD_DIM // 2, dtype=jnp.float32) * 2.0 / HEAD_DIM))
    angles = frequency[:, None] * places[None, :]
    cosine, sine = jnp.cos(angles), jnp.sin(angles)
    own_cosine, own_sine = (lax.dynamic_slice_in_dim(table, member * rows, rows, 1) for table in (cosine, sine))

    attention_row, expert_row = attention_gain[None], expert_gain[None]
    qkv_weights = (query_weight, key_weight, value_weight)
    sent = [project(j, owners, tokens, attention_row, qkv_weights, own_cosine, own_sine) for j in range(chunks)]
    heads = [exchange(chunk, "expert") for chunk in sent]
    gate, up, down = (gather_weight(weight) for weight in (gate_weight, up_weight, down_weight))
    codes = slot_codes(routes, half_slots)
    codes_row = codes.T

    attended, logs, outs = [], [], []
    for chunk in heads:
        out, log = attend(bias, chunk)
        outs.append(out)
        logs.append(log)
        attended.append(exchange(out, "expert").reshape(owners * HEAD_DIM, rows))

    mixer = jnp.concatenate(
        [router_weight, constant_weight, jnp.zeros((width, 128 - NEXP - 4), jnp.bfloat16)], 1
    )
    prior_wide = jnp.pad(prior_weight, ((0, 0), (0, 128 - NEXP)))
    prior_turned = jnp.pad(prior_weight.T, ((0, 128 - NEXP), (0, 128 - NEXP)))
    resid, small, *x_out = middle(
        tokens, attended, out_weight, expert_row, mixer, prior, prior_wide, routes, codes_row
    )
    d_out = scatter(small, grad, codes_row)

    def to_experts(values):
        return exchange(values.reshape(NFFN, half_slots, -1), planes).reshape(values.shape)

    xs, ds, fs, backs, dots, hids, gates, ups = ([] for _ in range(8))
    for x_part, d_part in zip(x_out, d_out):
        x, d = to_experts(x_part), to_experts(d_part)
        f, back, dot, hid, dg, du = expert(x, d, gate, up, down)
        backs.append(to_experts(back))
        dots.append(exchange(dot[0].reshape(NFFN, half_slots), planes).reshape(1, rows))
        for kept, item in zip((xs, ds, fs, hids, gates, ups), (x, d, to_experts(f), hid, dg, du)):
            kept.append(item)
    gate_part, up_part, down_part = (
        scatter_weight(grads) for grads in weight_grads(xs, ds, hids, gates, ups)
    )

    vector = jnp.concatenate([constant_vector, jnp.zeros((6, width), jnp.float32)], 0)
    resid_grads, *grads_out, out_grad, sums, prior_sums, prior_grad = turn(
        resid, small, grad, prior, routes, codes, backs, jnp.concatenate(dots, 1), vector, expert_row,
        mixer.T, prior_turned, out_weight, attended,
    )
    result = combine(resid, small, routes, codes, fs, vector, expert_row)

    own_backs = []
    for j in range(chunks):
        head_grads = exchange(grads_out[j].reshape(owners, HEAD_DIM, rows), "expert")
        back = attend_back(bias, cosine, sine, heads[j], outs[j], logs[j], head_grads)
        own_backs.append(exchange(back, "expert"))
    tokens_grad, qkv_grads = last(tokens, attention_row, own_backs, qkv_weights, resid_grads)

    def reduce_rows(partial):
        part = lax.psum_scatter(partial, ("xy", "core"), scatter_dimension=1, tiled=True)
        part = lax.psum_scatter(part, "expert", scatter_dimension=0, tiled=True)
        return lax.all_gather(part, ("xy", "core"), axis=1, tiled=True).astype(jnp.float32)

    out_total = reduce_rows(out_grad)
    qkv_total = reduce_rows(qkv_grads)
    sums, prior_sums = lax.psum((sums, prior_sums), everyone)
    share = width // owners
    mine = lax.dynamic_slice_in_dim(sums, member * share, share, 1)
    return (
        result[None],
        tokens_grad[None],
        prior_grad[None],
        *(qkv_total[:, i * width : (i + 1) * width] for i in range(3)),
        out_total,
        qkv_total[:, 3 * width],
        jnp.sum(mine[24:32], 0),
        mine[:NEXP].T,
        lax.dynamic_slice_in_dim(prior_sums, member * (NEXP // owners), NEXP // owners, 0)[:, :NEXP],
        mine[NEXP : NEXP + 4].T,
        mine[16:18],
        gate_part,
        up_part,
        down_part,
    )


def solution(mesh):
    owners, copies = mesh.shape["expert"], mesh.shape["dp"]
    cores = 2
    mesh = Mesh(mesh.devices.reshape(owners, copies // cores, cores), ("expert", "xy", "core"))
    dp = ("xy", "core")
    rows = P(dp, "expert", None)
    shard = P("expert", dp, None)
    in_specs = (rows, rows, rows, P(dp, None), rows) + (P(),) * 10 + (shard,) * 3
    out_specs = (
        (rows,) * 3
        + (P("expert", None),) * 4
        + (P("expert"),) * 2
        + (P("expert", None),) * 3
        + (P(None, "expert"),)
        + (shard,) * 3
    )
    return jax.shard_map(per_device, mesh=mesh, in_specs=in_specs, out_specs=out_specs, check_vma=False)
```

time: 1560 us -> 837 us (0.54)
  waiting for transfers between devices: 697 us -> 287 us
  matrix products: 406 us -> 0.26 us
  Pallas kernels: 0 us -> 184 us
  local copies, waits for them, and re-layouts: 175 us -> 55.8 us
  other arithmetic: 142 us -> 24.5 us
  blocking collectives: 83.7 us -> 176 us
  starting transfers between devices: 18.6 us -> 84.3 us
    dot_general x91 -> x1, matrix products: 406 us -> 0.26 us  [slot_codes(): jnp.dot(earlier.astype(jnp.bfloat16), per_row.astype(jnp.bfloat16), prefe...]
    reduce_scatter x8 -> x5, waiting for transfers between devices: 462 us -> 58.4 us  [the longest x3 40.4 us: scatter_weight(): part = lax.psum_scatter(grads, 'xy', scatter_dimension=0, tiled=True)]
    pallas_call x0 -> x17, Pallas kernels: none -> 184 us  [the longest x2 44.7 us: expert(): pl.pallas_call(expert_kernel, grid=(units // part,), in_specs=[whole, who...]
    all_gather x5 -> x3, waiting for transfers between devices: 125 us -> 0.02 us  [gather_weight(): return lax.all_gather(pair, 'xy', axis=0, tiled=True)]
    all_to_all x0 -> x5, blocking collectives: none -> 107 us  [exchange(): return lax.all_to_all(values, axes, split_axis=0, concat_axis=0, tiled=True)]
    reduce_sum x16 -> x5, other arithmetic: 107 us -> 2.15 us  [the longest x1 1.36 us: per_device(): jnp.sum(mine[24:32], 0)]
    unnamed x19 -> x13, waiting for transfers between devices: 4.78 us -> 86.5 us
    all_to_all x4 -> x17, starting transfers between devices: 17.6 us -> 80.8 us  [exchange(): return lax.all_to_all(values, axes, split_axis=0, concat_axis=0, tiled=True)]
  transfers between devices with their start and end apart: 20 -> 34, of which waited for: 15 -> 17; matrix products, arithmetic and copies ran while one was open for 23% -> 6% of each run, Pallas kernels for 0% -> 20%
where the time goes in v1:
time: 837 us; the launch traced here: 827 us
  waiting for transfers between devices  287 us (34%)
  Pallas kernels  184 us (22%)
  blocking collectives  176 us (21%)
  starting transfers between devices  84.3 us (10%)
  local copies, waits for them, and re-layouts  55.8 us (7%)
  other arithmetic  24.5 us (3%)
  between operations  14.9 us (2%)
    all_to_all x17, waiting for transfers between devices, exchange(): return lax.all_to_all(values, axes, split_axis=0, concat_axis=0, tiled=True)  141 us
    all_to_all x5, blocking collectives, exchange(): return lax.all_to_all(values, axes, split_axis=0, concat_axis=0, tiled=True)  107 us
    unnamed x13, waiting for transfers between devices  86.5 us
    all_to_all x17, starting transfers between devices, exchange(): return lax.all_to_all(values, axes, split_axis=0, concat_axis=0, tiled=True)  80.8 us
    pallas_call x2, Pallas kernels, expert(): pl.pallas_call(expert_kernel, grid=(units // part,), in_specs=[whole, who...  44.7 us
    psum x1, blocking collectives, per_device(): sums, prior_sums = lax.psum((sums, prior_sums), everyone)  43.4 us
    pallas_call x3, Pallas kernels, attend_back(): pl.pallas_call(attend_back_kernel, out_shape=jax.ShapeDtypeStruct((source...  43 us
    reduce_scatter x3, waiting for transfers between devices, scatter_weight(): part = lax.psum_scatter(grads, 'xy', scatter_dimension=0, tiled=True)  40.4 us
  transfers between devices with their start and end apart: 34, of which 17 were waited for; matrix products, arithmetic and copies ran while one was open for 6% of the time, Pallas kernels for 20%

profile of v1, /device:TPU:1, one launch (start us, length us, event | category | flops | bytes accessed | tf_op | source)
XLA Modules:
  0.0 826.6 jit_solution(10361449162444296974)
XLA Ops:
  30.1 19.1 %all-to-all-done.qkv_ref = bf16[4,192,640]{2,1,0:T(8,128)(2,1)} async-done(((bf16[4,192,640]{2,1,0:T(8,128)(2,1)}), bf16[4,192,640]{2,1,0:T(8,128)(2,1)}, u32[]{:S(2)}, u32[]{:S(2)}) %all-to-all-start) | async-done | bytes 983072 | tf_op jit(solution)/shard_map/all_to_all | solution.py:693
  89.6 15.0 %all-to-all-done.4.qkv_ref = bf16[4,192,640]{2,1,0:T(8,128)(2,1)S(1)} async-done(((bf16[4,192,640]{2,1,0:T(8,128)(2,1)}), bf16[4,192,640]{2,1,0:T(8,128)(2,1)S(1)}, u32[]{:S(2)}, u32[]{:S(2)}) %all-to-all-start.4) | async-done | bytes 983072 | tf_op jit(solution)/shard_map/all_to_all | solution.py:693
  163.5 21.4 %all-to-all-done.6 = bf16[8,80,768]{2,1,0:T(8,128)(2,1)S(1)} async-done(((bf16[8,80,768]{2,1,0:T(8,128)(2,1)}), bf16[8,80,768]{2,1,0:T(8,128)(2,1)S(1)}, u32[]{:S(2)}, u32[]{:S(2)}) %all-to-all-start.6) | async-done | bytes 983072 | tf_op jit(solution)/shard_map/all_to_all | solution.py:693
  195.3 19.3 %all-to-all-done.9 = bf16[8,80,768]{2,1,0:T(8,128)(2,1)} async-done(((bf16[8,80,768]{2,1,0:T(8,128)(2,1)}), bf16[8,80,768]{2,1,0:T(8,128)(2,1)}, u32[]{:S(2)}, u32[]{:S(2)}) %all-to-all-start.9) | async-done | bytes 983072 | tf_op jit(solution)/shard_map/all_to_all | solution.py:693
  214.6 29.3 %all_to_all.118 = bf16[8,80,768]{2,1,0:T(8,128)(2,1)} all-to-all(bf16[8,80,768]{2,1,0:T(8,128)(2,1)} %bitcast.98), channel_id=1, replica_groups=mesh['expert'=4,'xy'=4,'core'=2] {'expert','core'}, dimensions={0} | all-to-all | bytes 1966080 | tf_op jit(solution)/shard_map/all_to_all | solution.py:693
  248.3 22.5 %shard_map.306 = (bf16[640,768]{1,0:T(8,128)(2,1)}, bf16[640,768]{1,0:T(8,128)(2,1)}, f32[8,640]{1,0:T(8,128)S(1)}, bf16[640,2048]{1,0:T(8,128)(2,1)}, bf16[640,...) custom-call(bf16[640,768]{1,0:T(8,128)(2,1)} %bitcast.22.x_ref.xb_ref, bf16[640,768]{1,0:T(8,128)(2,1)} %bitcast.111, ...), custom_call_target="tpu_custom_call" | custom-call | flops 12079595520 | bytes 30000000 | tf_op jit(solution)/shard_map/pallas_call | solution.py:399
  276.7 22.2 %shard_map.305 = (bf16[640,768]{1,0:T(8,128)(2,1)}, bf16[640,768]{1,0:T(8,128)(2,1)S(1)}, f32[8,640]{1,0:T(8,128)S(1)}, bf16[640,2048]{1,0:T(8,128)(2,1)}, bf16[...) custom-call(bf16[640,768]{1,0:T(8,128)(2,1)} %bitcast.91, bf16[640,768]{1,0:T(8,128)(2,1)} %bitcast.113, ...), custom_call_target="tpu_custom_call" | custom-call | flops 12079595520 | bytes 30000000 | tf_op jit(solution)/shard_map/pallas_call | solution.py:399
  308.8 28.2 %all_to_all.120 = bf16[8,80,768]{2,1,0:T(8,128)(2,1)} all-to-all(bf16[8,80,768]{2,1,0:T(8,128)(2,1)S(1)} %bitcast.97), channel_id=1, replica_groups=mesh['expert'=4,'xy'=4,'core'=2] {'expert','core'}, dimensions={0} | all-to-all | bytes 1966080 | tf_op jit(solution)/shard_map/all_to_all | solution.py:693
  345.6 20.1 %all-to-all-done.13 = bf16[8,80,768]{2,1,0:T(8,128)(2,1)S(1)} async-done(((bf16[8,80,768]{2,1,0:T(8,128)(2,1)}), bf16[8,80,768]{2,1,0:T(8,128)(2,1)S(1)}, u32[]{:S(2)}, u32[]{:S(2)}) %all-to-all-start.13) | async-done | bytes 983072 | tf_op jit(solution)/shard_map/all_to_all | solution.py:693
  366.7 18.1 %shard_map.308 = (f32[640,768]{1,0:T(8,128)}, bf16[256,640]{1,0:T(8,128)(2,1)}, bf16[256,640]{1,0:T(8,128)(2,1)}, bf16[256,640]{1,0:T(8,128)(2,1)}, bf16[768,768...) custom-call(f32[640,768]{1,0:T(8,128)} %get-tuple-element.56.resid_ref, ...), custom_call_target="tpu_custom_call" | custom-call | flops 2768240640 | bytes 15000000 | tf_op jit(solution)/shard_map/pallas_call | solution.py:549
  387.9 35.3 %reduce-scatter.24.cloned.1.call-done = bf16[96,768]{1,0:T(8,128)(2,1)} async-done(((bf16[768,768]{1,0:T(8,128)(2,1)}), bf16[96,768]{1,0:T(8,128)(2,1)}) %reduce-scatter.24.cloned.1.call-update) | async-done | bytes 147472
  425.0 19.2 %shard_map.313 = (bf16[768,2048]{1,0:T(8,128)(2,1)}, bf16[768,2048]{1,0:T(8,128)(2,1)}, bf16[2048,768]{1,0:T(8,128)(2,1)}) custom-call(bf16[640,768]{1,0:T(8,128)(2,1)S(1)} %bitcast.92, bf16[640,768]{1,0:T(8,128)(2,1)} %bitcast.22.x_ref.xb_ref, bf16[640,768]{1,0:T(8,128)(2,1)} %bitcast.114, bf16[640,768]{1,0:T(8,128)(2,1)} %bitcast.112, ...), custom_call_target="tpu_custom_call" | custom-call | flops 12079595520 | bytes 30000000 | tf_op jit(solution)/shard_map/pallas_call | solution.py:442
  458.1 12.1 %all_to_all.121.grad_ref = bf16[4,64,640]{2,1,0:T(8,128)(2,1)S(1)} all-to-all(bf16[4,64,640]{2,1,0:T(8,128)(2,1)S(1)} %bitcast.119), channel_id=1, replica_groups=mesh['expert'=4,'xy'=4,'core'=2] {'expert'}, dimensions={0} | all-to-all | bytes 655360 | tf_op jit(solution)/shard_map/all_to_all | solution.py:693
  474.3 14.8 %shard_map.309 = bf16[4,192,640]{2,1,0:T(8,128)(2,1)} custom-call(f32[16,2560]{1,0:T(8,128)S(1)} %copy-done.32, f32[32,2560]{1,0:T(8,128)S(1)} %copy-done.27, f32[32,2560]{1,0:T(8,128)S(1)} %copy-done.25, bf16[4,192,640]{2,1,0:T(8,128)(2,1)} %all-to-all-done.qkv_ref, bf16[4,64,640]{2,1,0:T(8,128)(2,1)} %get-tuple-element.53.out_ref, ...), custom_call_target="tpu_custom_call" | custom-call | flops 5000000000 | bytes 6000000 | tf_op jit(solution)/shard_map/pallas_call | solution.py:205
  493.8 14.8 %shard_map.310 = bf16[4,192,640]{2,1,0:T(8,128)(2,1)} custom-call(f32[16,2560]{1,0:T(8,128)S(1)} %copy-done.32, f32[32,2560]{1,0:T(8,128)S(1)} %copy-done.27, f32[32,2560]{1,0:T(8,128)S(1)} %copy-done.25, bf16[4,192,640]{2,1,0:T(8,128)(2,1)} %all-to-all-done.2.qkv_ref, bf16[4,64,640]{2,1,0:T(8,128)(2,1)} %get-tuple-element.54.out_ref, ...), custom_call_target="tpu_custom_call" | custom-call | flops 5000000000 | bytes 6000000 | tf_op jit(solution)/shard_map/pallas_call | solution.py:205
  522.5 13.5 %shard_map.311 = bf16[4,192,640]{2,1,0:T(8,128)(2,1)S(1)} custom-call(f32[16,2560]{1,0:T(8,128)S(1)} %copy-done.32, f32[32,2560]{1,0:T(8,128)S(1)} %copy-done.27, f32[32,2560]{1,0:T(8,128)S(1)} %copy-done.25, bf16[4,192,640]{2,1,0:T(8,128)(2,1)S(1)} %all-to-all-done.4.qkv_ref, bf16[4,64,640]{2,1,0:T(8,128)(2,1)} %get-tuple-element.55.out_ref, ...), custom_call_target="tpu_custom_call" | custom-call | flops 5000000000 | bytes 6000000 | tf_op jit(solution)/shard_map/pallas_call | solution.py:205
  546.9 27.9 %all_to_all.122.b2_ref = bf16[4,192,640]{2,1,0:T(8,128)(2,1)} all-to-all(bf16[4,192,640]{2,1,0:T(8,128)(2,1)S(1)} %shard_map.311), channel_id=1, replica_groups=mesh['expert'=4,'xy'=4,'core'=2] {'expert'}, dimensions={0} | all-to-all | bytes 1966080 | tf_op jit(solution)/shard_map/all_to_all | solution.py:693
  581.2 12.5 %shard_map.312 = (f32[640,768]{1,0:T(8,128)}, bf16[768,2432]{1,0:T(8,128)(2,1)}) custom-call(bf16[640,768]{1,0:T(8,128)(2,1)} %bitcast.81, f32[1,768]{1,0:T(1,128)} %copy-done.33, bf16[4,192,640]{2,1,0:T(8,128)(2,1)} %all-to-all-done.17.b0_ref, bf16[4,192,640]{2,1,0:T(8,128)(2,1)} %all-to-all-done.19.b1_ref, bf16[4,192,640]{2,1,0:T(8,128)(2,1)} %all_to_all.122.b2_ref, ...), custom_call_target="tpu_custom_call" | custom-call | flops 4529848320 | bytes 20000000 | tf_op jit(solution)/shard_map/pallas_call | solution.py:634
  610.4 43.4 %psum.15 = f32[12,128]{1,0:T(8,128)S(1)} all-reduce(f32[12,128]{1,0:T(8,128)S(1)} %copy-done.57), channel_id=1, replica_groups=mesh['expert'=4,'xy'=4,'core'=2] {'expert','xy','core'}, use_global_device_ids=true, to_apply=%region_14.15 | all-reduce | flops 1536 | bytes 12288 | tf_op jit(solution)/shard_map/psum | solution.py:788
  668.0 11.4 %all_gather.19 = bf16[192,768]{0,1:T(8,128)(2,1)S(1)} all-gather(bf16[192,96]{0,1:T(8,128)(2,1)S(1)} %copy.99), channel_id=1, replica_groups=mesh['expert'=4,'xy'=4,'core'=2] {'xy','core'}, dimensions={1}, use_global_device_ids=true | all-gather | bytes 331776 | tf_op jit(solution)/shard_map/all_gather | solution.py:784
  683.4 40.4 %reduce-scatter.20.cloned.1.call-done = bf16[512,768]{1,0:T(8,128)(2,1)} async-done(((bf16[2048,768]{1,0:T(8,128)(2,1)}), bf16[512,768]{1,0:T(8,128)(2,1)}) %reduce-scatter.20.cloned.1.call-update) | async-done | bytes 786448 | tf_op jit(solution)/shard_map/reduce_scatter | solution.py:702
  727.0 49.2 %reduce-scatter.22.cloned.1.call-done = bf16[304,768]{1,0:T(8,128)(2,1)} async-done(((bf16[2432,768]{1,0:T(8,128)(2,1)}), bf16[304,768]{1,0:T(8,128)(2,1)}) %reduce-scatter.22.cloned.1.call-update) | async-done | bytes 466960
  781.1 18.0 %reduce-scatter.12.cloned.1.call-done = bf16[192,304]{1,0:T(8,128)(2,1)} async-done(((bf16[768,304]{1,0:T(8,128)(2,1)}), bf16[192,304]{1,0:T(8,128)(2,1)}) %reduce-scatter.12.cloned.1.call-update) | async-done | bytes 116752 | tf_op jit(solution)/shard_map/reduce_scatter | solution.py:783
  799.1 14.1 %all-gather = bf16[8,304,192]{1,2,0:T(8,128)(2,1)S(1)} all-gather(bf16[1,304,192]{1,2,0:T(8,128)(2,1)} %bitcast.120), channel_id=1, replica_groups=mesh['expert'=4,'xy'=4,'core'=2] {'xy','core'}, dimensions={0}, use_global_device_ids=true | all-gather | bytes 1050624 | tf_op jit(solution)/shard_map/all_gather | solution.py:784
  (288 shorter events, 270.1 us)
Async XLA Ops:
  7.2 241.1 %all-gather.5.cloned.1.call-start = ((), (), s32[]{:S(2)}) async-start(), calls=%async_computation.29 | async-start | bytes 3932160 | tf_op jit(solution)/shard_map/all_gather | solution.py:699
  18.9 30.3 %all-to-all-start = ((bf16[4,192,640]{2,1,0:T(8,128)(2,1)}), bf16[4,192,640]{2,1,0:T(8,128)(2,1)}, u32[]{:S(2)}, u32[]{:S(2)}) async-start(bf16[4,192,640]{2,1,0:T(8,128)(2,1)} %copy-done.10), calls=%async_computation | async-start | bytes 1966080 | tf_op jit(solution)/shard_map/all_to_all | solution.py:693
  49.2 28.1 %all-to-all-start.2 = ((bf16[4,192,640]{2,1,0:T(8,128)(2,1)}), bf16[4,192,640]{2,1,0:T(8,128)(2,1)}, u32[]{:S(2)}, u32[]{:S(2)}) async-start(bf16[4,192,640]{2,1,0:T(8,128)(2,1)} %copy-done.9), calls=%async_computation.2 | async-start | bytes 1966080 | tf_op jit(solution)/shard_map/all_to_all | solution.py:693
  53.4 194.9 %all-gather.7.cloned.1.call-start = ((), (), s32[]{:S(2)}) async-start(), calls=%async_computation.30 | async-start | bytes 3932160 | tf_op jit(solution)/shard_map/all_gather | solution.py:699
  152.6 32.3 %all-to-all-start.6 = ((bf16[8,80,768]{2,1,0:T(8,128)(2,1)}), bf16[8,80,768]{2,1,0:T(8,128)(2,1)S(1)}, u32[]{:S(2)}, u32[]{:S(2)}) async-start(bf16[8,80,768]{2,1,0:T(8,128)(2,1)} %bitcast.96), calls=%async_computation.6 | async-start | bytes 1966080 | tf_op jit(solution)/shard_map/all_to_all | solution.py:693
  160.6 87.7 %all-gather.9.cloned.1.call-start = ((), (), s32[]{:S(2)}) async-start(), calls=%async_computation.31 | async-start | bytes 3932160 | tf_op jit(solution)/shard_map/all_gather | solution.py:699
  184.9 29.7 %all-to-all-start.9 = ((bf16[8,80,768]{2,1,0:T(8,128)(2,1)}), bf16[8,80,768]{2,1,0:T(8,128)(2,1)}, u32[]{:S(2)}, u32[]{:S(2)}) async-start(bf16[8,80,768]{2,1,0:T(8,128)(2,1)} %bitcast.95), calls=%async_computation.9 | async-start | bytes 1966080 | tf_op jit(solution)/shard_map/all_to_all | solution.py:693
  243.9 28.8 %all-to-all-start.7 = ((bf16[8,80,768]{2,1,0:T(8,128)(2,1)}), bf16[8,80,768]{2,1,0:T(8,128)(2,1)S(1)}, u32[]{:S(2)}, u32[]{:S(2)}) async-start(bf16[8,80,768]{2,1,0:T(8,128)(2,1)} %bitcast.11), calls=%async_computation.7 | async-start | bytes 1966080 | tf_op jit(solution)/shard_map/all_to_all | solution.py:693
  337.0 28.8 %all-to-all-start.13 = ((bf16[8,80,768]{2,1,0:T(8,128)(2,1)}), bf16[8,80,768]{2,1,0:T(8,128)(2,1)S(1)}, u32[]{:S(2)}, u32[]{:S(2)}) async-start(bf16[8,80,768]{2,1,0:T(8,128)(2,1)} %bitcast.30), calls=%async_computation.13 | async-start | bytes 1966080 | tf_op jit(solution)/shard_map/all_to_all | solution.py:693
  341.4 81.8 %reduce-scatter.24.cloned.1.call-start = ((), (), s32[]{:S(2)}) async-start(), calls=%async_computation.39 | async-start | bytes 1327104
  387.3 274.3 %all-reduce.6.cloned.1.call-start = ((), (), s32[]{:S(2)}) async-start(), calls=%async_computation.34 | async-start | bytes 196608 | tf_op jit(solution)/shard_map/psum | solution.py:788
  387.9 279.2 %reduce-scatter.14.cloned.1.call-start = ((), (), s32[]{:S(2)}) async-start(), calls=%async_computation.33 | async-start | bytes 245760 | tf_op jit(solution)/shard_map/reduce_scatter | solution.py:783
  424.9 255.4 %reduce-scatter.16.cloned.1.call-start = ((), (), s32[]{:S(2)}) async-start(), calls=%async_computation.35 | async-start | bytes 3932160 | tf_op jit(solution)/shard_map/reduce_scatter | solution.py:702
  444.2 237.6 %reduce-scatter.18.cloned.1.call-start = ((), (), s32[]{:S(2)}) async-start(), calls=%async_computation.36 | async-start | bytes 3932160 | tf_op jit(solution)/shard_map/reduce_scatter | solution.py:702
  449.3 274.5 %reduce-scatter.20.cloned.1.call-start = ((), (), s32[]{:S(2)}) async-start(), calls=%async_computation.37 | async-start | bytes 3932160 | tf_op jit(solution)/shard_map/reduce_scatter | solution.py:702
  489.1 28.9 %all-to-all-start.17 = ((bf16[4,192,640]{2,1,0:T(8,128)(2,1)}), bf16[4,192,640]{2,1,0:T(8,128)(2,1)}, u32[]{:S(2)}, u32[]{:S(2)}) async-start(bf16[4,192,640]{2,1,0:T(8,128)(2,1)} %shard_map.309), calls=%async_computation.17 | async-start | bytes 1966080 | tf_op jit(solution)/shard_map/all_to_all | solution.py:693
  518.0 28.9 %all-to-all-start.19 = ((bf16[4,192,640]{2,1,0:T(8,128)(2,1)}), bf16[4,192,640]{2,1,0:T(8,128)(2,1)}, u32[]{:S(2)}, u32[]{:S(2)}) async-start(bf16[4,192,640]{2,1,0:T(8,128)(2,1)} %shard_map.310), calls=%async_computation.19 | async-start | bytes 1966080 | tf_op jit(solution)/shard_map/all_to_all | solution.py:693
  574.8 30.6 %all-to-all-start.8 = ((bf16[8,80,768]{2,1,0:T(8,128)(2,1)}), bf16[8,80,768]{2,1,0:T(8,128)(2,1)S(1)}, u32[]{:S(2)}, u32[]{:S(2)}) async-start(bf16[8,80,768]{2,1,0:T(8,128)(2,1)} %bitcast.19), calls=%async_computation.8 | async-start | bytes 1966080 | tf_op jit(solution)/shard_map/all_to_all | solution.py:693
  581.0 195.2 %reduce-scatter.22.cloned.1.call-start = ((), (), s32[]{:S(2)}) async-start(), calls=%async_computation.38 | async-start | bytes 4202496
  605.3 49.1 %all-to-all-start.11 = ((bf16[8,80,768]{2,1,0:T(8,128)(2,1)}), bf16[8,80,768]{2,1,0:T(8,128)(2,1)S(1)}, u32[]{:S(2)}, u32[]{:S(2)}) async-start(bf16[8,80,768]{2,1,0:T(8,128)(2,1)} %bitcast.25), calls=%async_computation.11 | async-start | bytes 1966080 | tf_op jit(solution)/shard_map/all_to_all | solution.py:693
  609.7 189.4 %reduce-scatter.12.cloned.1.call-start = ((), (), s32[]{:S(2)}) async-start(), calls=%async_computation.32 | async-start | bytes 737280 | tf_op jit(solution)/shard_map/reduce_scatter | solution.py:783
  681.6 44.1 %collective-permute-start.3 = (bf16[96,2048]{1,0:T(8,128)(2,1)S(1)}, bf16[96,2048]{1,0:T(8,128)(2,1)S(1)}, u32[]{:S(2)}, u32[]{:S(2)}) collective-permute-start(bf16[96,2048]{1,0:T(8,128)(2,1)S(1)} %broadcast_select_fusion.7), channel_id=1, source_target_pairs={{0,1},{1,0},{2,3},{3,2},{4,5},{5,4},{6,7},{7,6},{8,9},{9,8},{10,11... | collective-permute-start | bytes 1179656 | tf_op jit(solution)/shard_map/ppermute | solution.py:690
  683.0 96.7 %collective-permute-start.4 = (bf16[96,2048]{1,0:T(8,128)(2,1)S(1)}, bf16[96,2048]{1,0:T(8,128)(2,1)S(1)}, u32[]{:S(2)}, u32[]{:S(2)}) collective-permute-start(bf16[96,2048]{1,0:T(8,128)(2,1)S(1)} %broadcast_select_fusion.5), channel_id=1, source_target_pairs={{0,1},{1,0},{2,3},{3,2},{4,5},{5,4},{6,7},{7,6},{8,9},{9,8},{10,11... | collective-permute-start | bytes 1179656 | tf_op jit(solution)/shard_map/ppermute | solution.py:690
  724.9 53.3 %collective-permute-start.5 = (bf16[256,768]{1,0:T(8,128)(2,1)S(1)}, bf16[256,768]{1,0:T(8,128)(2,1)S(1)}, u32[]{:S(2)}, u32[]{:S(2)}) collective-permute-start(bf16[256,768]{1,0:T(8,128)(2,1)S(1)} %broadcast_select_fusion.1), channel_id=1, source_target_pairs={{0,1},{1,0},{2,3},{3,2},{4,5},{5,4},{6,7},{7,6},{8,9},{9,8},{10,11... | collective-permute-start | bytes 1179656 | tf_op jit(solution)/shard_map/ppermute | solution.py:690
  (71 other events, 1018.6 us)
Sparse Core Ops, SparseCore 0:
  12.3 46.1 all-gather.4
  67.1 44.8 all-gather.6
  163.7 44.7 all-gather.8
  387.4 35.7 reduce-scatter.23
  429.5 129.5 all-reduce.5
  561.9 18.3 reduce-scatter.13
  583.2 45.1 reduce-scatter.15
  631.4 44.6 reduce-scatter.17
  679.1 44.6 reduce-scatter.19
  727.1 49.0 reduce-scatter.21
  779.1 19.8 reduce-scatter.11

commit v2 on v1

--- a/solution.py
+++ b/solution.py
@@ -71,7 +71,7 @@
         body(None, pl.multiple_of(tile * TILE, TILE))
 
 
-def attend_kernel(bias_ref, qkv_ref, out_ref, lse_ref, q_ref, k_ref, v_ref, o_ref, s_ref, triangle):
+def attend_head(bias_ref, qkv_ref, out_ref, lse_ref, q_ref, k_ref, v_ref, o_ref, s_ref, triangle):
     sources, _, rows = qkv_ref.shape
     length = sources * rows
     factor = HEAD_DIM ** (-0.5) * LOG2E
@@ -110,29 +110,6 @@
         out_ref[z] = o_ref[:, pl.ds(z * rows, rows)]
 
 
-def attend(bias, qkv):
-    sources, _, rows = qkv.shape
-    length = sources * rows
-    part_total = TRUNK // TILE + 3
-    return pl.pallas_call(
-        attend_kernel,
-        out_shape=(
-            jax.ShapeDtypeStruct((sources, HEAD_DIM, rows), jnp.bfloat16),
-            jax.ShapeDtypeStruct((1, length), jnp.float32),
-        ),
-        scratch_shapes=[
-            pltpu.VMEM((HEAD_DIM, length), jnp.bfloat16),
-            pltpu.VMEM((length, HEAD_DIM), jnp.bfloat16),
-            pltpu.VMEM((HEAD_DIM + 16, length), jnp.bfloat16),
-            pltpu.VMEM((HEAD_DIM, length), jnp.bfloat16),
-            pltpu.VMEM((part_total * TILE, TILE), jnp.float32),
-            pltpu.VMEM((TILE, TILE), jnp.float32),
-        ],
-        compiler_params=pltpu.CompilerParams(vmem_limit_bytes=48 * MIB),
-        cost_estimate=pl.CostEstimate(flops=2 * 10**9, bytes_accessed=4 * 10**6, transcendentals=3 * 10**6),
-    )(bias, qkv)
-
-
 def attend_back_kernel(
     bias_ref, cos_ref, sin_ref, qkv_ref, out_ref, lse_ref, grad_ref, back_ref,
     qt_ref, kt_ref, dt_ref, q_ref, k_ref, v_ref, d_ref, delta_ref, dq_ref, dk_ref, dv_ref, triangle,
@@ -225,39 +202,177 @@
     return pl.CostEstimate(flops=int(flops), bytes_accessed=int(moved), transcendentals=0)
 
 
-def project_kernel(tokens_ref, gain_ref, query_ref, key_ref, value_ref, cos_ref, sin_ref, out_ref):
+def greet(ring, copies):
+    barrier = pltpu.get_barrier_semaphore()
+    for target in ring + copies:
+        pl.semaphore_signal(barrier, inc=1, device_id=target, device_id_type=pl.DeviceIdType.MESH)
+    pl.semaphore_wait(barrier, len(ring) + len(copies))
+
+
+def ring_partners(owners):
+    member = lax.axis_index("expert")
+    result = []
+    for step in sorted(range(1, owners), key=lambda k: -min(k, owners - k)):
+        index = lax.rem(member + step, owners)
+        result.append((step, index, {"expert": index}))
+    return result
+
+
+def copy_partners(total):
+    place = lax.axis_index("xy") * 2 + lax.axis_index("core")
+    result = []
+    for step in sorted(range(1, total), key=lambda k: -(k % 8 in (6, 2, 4))):
+        index = lax.rem(place + step, total)
+        result.append((step, lax.rem(index, 2), {"xy": index // 2, "core": lax.rem(index, 2)}))
+    return result
+
+
+def remote(source, target, send, receive, device):
+    return pltpu.make_async_remote_copy(
+        src_ref=source, dst_ref=target, send_sem=send, recv_sem=receive,
+        device_id=device, device_id_type=pl.DeviceIdType.MESH,
+    )
+
+
+def attend_phase_kernel(
+    tokens_ref, gain_ref, query_ref, key_ref, value_ref, cos_ref, sin_ref, bias_ref, gate_ref, up_ref, down_ref,
+    attended_ref, lse_ref, heads_ref, outs_ref, gate_full, up_full, down_full,
+    normed_ref, qkv_sent, qkv_got, out_sent, out_got, q_ref, k_ref, v_ref, o_ref, s_ref, triangle,
+    qkv_send, qkv_recv, out_send, out_recv, weight_send, weight_recv, local_sem,
+):
+    chunks, owners, _, rows = qkv_sent.shape
+    member = lax.axis_index("expert")
+    copies = gate_full.shape[0]
+    ring, others = ring_partners(owners), copy_partners(copies)
+    greet([item[2] for item in ring], [item[2] for item in others])
+    weights = ((gate_ref, gate_full), (up_ref, up_full), (down_ref, down_full))
+    place = lax.axis_index("xy") * 2 + lax.axis_index("core")
+    core = lax.axis_index("core")
+    started = []
+
     inputs = tokens_ref[...].astype(jnp.float32)
     inverse = lax.rsqrt(jnp.mean(inputs * inputs, -1, keepdims=True) + epsilon)
-    normed = (inputs * inverse * gain_ref[...]).astype(jnp.bfloat16)
+    normed_ref[...] = (inputs * inverse * gain_ref[...]).astype(jnp.bfloat16)
     half = HEAD_DIM // 2
-    cosine, sine = cos_ref[...], sin_ref[...]
-    for i, weight in enumerate((query_ref, key_ref, value_ref)):
-        turned = dot_nn(normed, weight[...]).T
-        for z in range(out_ref.shape[0]):
-            first = turned[z * HEAD_DIM : z * HEAD_DIM + half]
-            second = turned[z * HEAD_DIM + half : (z + 1) * HEAD_DIM]
-            if i < 2:
-                first, second = first * cosine - second * sine, second * cosine + first * sine
+    span_width = owners * HEAD_DIM
+    qkv_copies = []
+    for j in range(chunks):
+        for i, weight in enumerate((query_ref, key_ref, value_ref)):
+            turned = dot_nn(normed_ref[...], weight[:, j * span_width : (j + 1) * span_width]).T
             base = i * HEAD_DIM
-            out_ref[z, base : base + half] = first.astype(jnp.bfloat16)
-            out_ref[z, base + half : base + HEAD_DIM] = second.astype(jnp.bfloat16)
-
-
-def project(chunk, owners, tokens, gain, weights, cosine, sine):
+            for z in range(owners):
+                first = turned[z * HEAD_DIM : z * HEAD_DIM + half]
+                second = turned[z * HEAD_DIM + half : (z + 1) * HEAD_DIM]
+                if i < 2:
+                    cosine, sine = cos_ref[...], sin_ref[...]
+                    first, second = first * cosine - second * sine, second * cosine + first * sine
+                qkv_sent[j, z, base : base + half] = first.astype(jnp.bfloat16)
+                qkv_sent[j, z, base + half : base + HEAD_DIM] = second.astype(jnp.bfloat16)
+        local = pltpu.make_async_copy(qkv_sent.at[j, member], qkv_got.at[j, member], local_sem.at[j])
+        local.start()
+        group = []
+        for step, index, device in ring:
+            copy = remote(
+                qkv_sent.at[j, index], qkv_got.at[j, member],
+                qkv_send.at[j, step - 1], qkv_recv.at[j, step - 1], device,
+            )
+            copy.start()
+            group.append(copy)
+        qkv_copies.append((local, group))
+        if j == 0:
+            for i, (shard, full) in enumerate(weights):
+                local = pltpu.make_async_copy(shard.at[core], full.at[place], weight_send.at[i, 0])
+                local.start()
+                started.append((local, None))
+                for step, other_core, device in others:
+                    copy = remote(
+                        shard.at[other_core], full.at[place], weight_send.at[i, step], weight_recv.at[i, step], device
+                    )
+                    copy.start()
+                    started.append((None, copy))
+
+    out_copies = []
+    kept = []
+    for j in range(chunks):
+        local, group = qkv_copies[j]
+        local.wait()
+        for copy in group:
+            copy.wait_recv()
+        keep = pltpu.make_async_copy(qkv_got.at[j], heads_ref.at[j], local_sem.at[chunks + j])
+        keep.start()
+        kept.append(keep)
+        attend_head(
+            bias_ref, qkv_got.at[j], out_sent.at[j], lse_ref.at[j : j + 1], q_ref, k_ref, v_ref, o_ref, s_ref, triangle
+        )
+        local = pltpu.make_async_copy(out_sent.at[j, member], out_got.at[j, member], local_sem.at[2 * chunks + j])
+        local.start()
+        keep = pltpu.make_async_copy(out_sent.at[j], outs_ref.at[j], local_sem.at[3 * chunks + j])
+        keep.start()
+        kept += [local, keep]
+        for step, index, device in ring:
+            copy = remote(
+                out_sent.at[j, index], out_got.at[j, member],
+                out_send.at[j, step - 1], out_recv.at[j, step - 1], device,
+            )
+            copy.start()
+            out_copies.append(copy)
+    for copy in out_copies:
+        copy.wait_recv()
+    for copy in kept:
+        copy.wait()
+    attended_ref[...] = out_got[...]
+    for local, group in qkv_copies:
+        for copy in group:
+            copy.wait_send()
+    for copy in out_copies:
+        copy.wait_send()
+    for local, copy in started:
+        if copy is None:
+            local.wait()
+        else:
+            copy.wait()
+
+
+def attend_phase(tokens, gain, weights, cosine, sine, bias, shards, copies):
     rows, width = tokens.shape
-    columns = owners * HEAD_DIM
-    whole = lambda shape: pl.BlockSpec(shape, lambda i: (0,) * len(shape))
-    part = pl.BlockSpec((width, columns), lambda i: (0, chunk))
+    owners = lax.axis_size("expert")
+    length = rows * owners
+    chunks = width // HEAD_DIM // owners
+    head = (chunks, owners, 3 * HEAD_DIM, rows)
+    out = (chunks, owners, HEAD_DIM, rows)
+    vmem, hbm = pl.BlockSpec(memory_space=pltpu.VMEM), pl.BlockSpec(memory_space=pl.ANY)
+    fulls = [jax.ShapeDtypeStruct((copies, *shard.shape[1:]), shard.dtype) for shard in shards]
+    part_total = TRUNK // TILE + 3
+    sems = lambda *shape: pltpu.SemaphoreType.DMA(shape)
     return pl.pallas_call(
-        project_kernel,
-        grid=(1,),
-        in_specs=[whole((rows, width)), whole((1, width)), part, part, part]
-        + [whole((HEAD_DIM // 2, rows))] * 2,
-        out_specs=whole((owners, 3 * HEAD_DIM, rows)),
-        out_shape=jax.ShapeDtypeStruct((owners, 3 * HEAD_DIM, rows), jnp.bfloat16),
-        compiler_params=params(48),
-        cost_estimate=cost(6 * rows * width * columns, 4e6),
-    )(tokens, gain, *weights, cosine, sine)
+        attend_phase_kernel,
+        in_specs=[vmem] * 8 + [hbm] * 3,
+        out_specs=(vmem, vmem, hbm, hbm, hbm, hbm, hbm),
+        out_shape=(
+            jax.ShapeDtypeStruct(out, jnp.bfloat16),
+            jax.ShapeDtypeStruct((8, length), jnp.float32),
+            jax.ShapeDtypeStruct(head, jnp.bfloat16),
+            jax.ShapeDtypeStruct(out, jnp.bfloat16),
+            *fulls,
+        ),
+        scratch_shapes=[
+            pltpu.VMEM((rows, width), jnp.bfloat16),
+            pltpu.VMEM(head, jnp.bfloat16),
+            pltpu.VMEM(head, jnp.bfloat16),
+            pltpu.VMEM(out, jnp.bfloat16),
+            pltpu.VMEM(out, jnp.bfloat16),
+            pltpu.VMEM((HEAD_DIM, length), jnp.bfloat16),
+            pltpu.VMEM((length, HEAD_DIM), jnp.bfloat16),
+            pltpu.VMEM((HEAD_DIM + 16, length), jnp.bfloat16),
+            pltpu.VMEM((HEAD_DIM, length), jnp.bfloat16),
+            pltpu.VMEM((part_total * TILE, TILE), jnp.float32),
+            pltpu.VMEM((TILE, TILE), jnp.float32),
+            sems(chunks, owners - 1), sems(chunks, owners - 1), sems(chunks, owners - 1), sems(chunks, owners - 1),
+            sems(3, copies), sems(3, copies), sems(4 * chunks),
+        ],
+        compiler_params=pltpu.CompilerParams(vmem_limit_bytes=56 * MIB, collective_id=1, has_side_effects=True),
+        cost_estimate=cost(1e10, 5e7),
+    )(tokens, gain, *weights, cosine, sine, bias, *shards)
 
 
 def lane_pick(values, lanes, index):
@@ -464,7 +579,7 @@
 def turn_kernel(
     resid_ref, small_ref, grad_ref, prior_ref, routes_ref, codes_ref, ra_ref, rb_ref, dots_ref, vector_ref,
     gain_ref, mixer_ref, prior_turned_ref, out_weight_ref, a0_ref, a1_ref, a2_ref,
-    resid_grad_ref, g0_ref, g1_ref, g2_ref, out_grad_ref, sums_ref, prior_sums_ref, prior_grad_ref, back_ref,
+    resid_grad_ref, g0_ref, g1_ref, g2_ref, out_grad_ref, prior_grad_ref, back_ref, sums_ref, prior_sums_ref, extra_ref,
 ):
     rows, width = resid_ref.shape
     slots = 2 * ra_ref.shape[0]
@@ -532,15 +647,25 @@
         sums_ref[16:24, :] += split_dot(dot_nn, weights.T[0:8], grad_b)
         sums_ref[24:32, :] += jnp.sum((hidden_grads * normed).reshape(SEG // 8, 8, width), 0)
         prior_sums_ref[...] += jnp.dot(
-            prior_ref[span, :].T, logit_grads, precision=precise, preferred_element_type=jnp.float32
+            prior_ref[span, :].T,
+            jnp.concatenate([logit_grads[:, 96:], logit_grads[:, :96]], 1),
+            precision=precise,
+            preferred_element_type=jnp.float32,
         )
 
+    sums_ref[24:25, :] = jnp.sum(sums_ref[24:32, :], 0, keepdims=True)
+    extra_ref[...] = jnp.concatenate([sums_ref[...], jnp.zeros((96, width), jnp.float32)], 0).T
+    owners = a0_ref.shape[0] // HEAD_DIM
+    kept = NEXP // owners
+    for z in range(owners):
+        extra_ref[pl.ds(z * (width // owners), kept), :] += prior_sums_ref[z * kept : (z + 1) * kept, :]
+    out_grad_ref[:, width:] = extra_ref[...].astype(jnp.bfloat16)
     back = back_ref[...]
     part = a0_ref.shape[0]
     for j, (a_ref, g_ref) in enumerate(((a0_ref, g0_ref), (a1_ref, g1_ref), (a2_ref, g2_ref))):
         span = pl.ds(j * part, part)
         g_ref[...] = dot_nt(out_weight_ref[span, :], back).astype(jnp.bfloat16)
-        out_grad_ref[span, :] = dot_nn(a_ref[...], back).astype(jnp.bfloat16)
+        out_grad_ref[span, :width] = dot_nn(a_ref[...], back).astype(jnp.bfloat16)
 
 
 def turn(resid, small, grad, prior, routes, codes, returned, dots, vector, gain, mixer_turned, prior_turned, out_weight, attended):
@@ -551,12 +676,15 @@
         out_shape=(
             jax.ShapeDtypeStruct((rows, width), jnp.float32),
             *(jax.ShapeDtypeStruct((part, rows), jnp.bfloat16),) * 3,
-            jax.ShapeDtypeStruct((width, width), jnp.bfloat16),
-            jax.ShapeDtypeStruct((32, width), jnp.float32),
-            jax.ShapeDtypeStruct((prior.shape[1], 128), jnp.float32),
+            jax.ShapeDtypeStruct((width, width + 128), jnp.bfloat16),
             jax.ShapeDtypeStruct(prior.shape, jnp.float32),
         ),
-        scratch_shapes=[pltpu.VMEM((rows, width), jnp.bfloat16)],
+        scratch_shapes=[
+            pltpu.VMEM((rows, width), jnp.bfloat16),
+            pltpu.VMEM((32, width), jnp.float32),
+            pltpu.VMEM((prior.shape[1], 128), jnp.float32),
+            pltpu.VMEM((width, 128), jnp.float32),
+        ],
         compiler_params=params(56),
         cost_estimate=cost(4 * rows * width * width + 4 * rows * rows * width, 1.5e7),
     )(resid, small, grad, prior, routes, codes, *returned, dots, vector, gain, mixer_turned, prior_turned, out_weight, *attended)
@@ -599,15 +727,38 @@
     )(resid, small, routes, codes, *outs, vector, gain)
 
 
+def head_grads_kernel(tokens_ref, gain_ref, back_ref, out_ref, turned_ref):
+    inputs = tokens_ref[...].astype(jnp.float32)
+    inverse = lax.rsqrt(jnp.mean(inputs * inputs, -1, keepdims=True) + epsilon)
+    normed = (inputs * inverse * gain_ref[...]).T.astype(jnp.bfloat16)
+    owners = back_ref.shape[0]
+    for i in range(3):
+        for z in range(owners):
+            row = (i * owners + z) * HEAD_DIM
+            turned_ref[row : row + HEAD_DIM, :] = back_ref[z, i * HEAD_DIM : (i + 1) * HEAD_DIM]
+    out_ref[...] = dot_nt(normed, turned_ref[...]).astype(jnp.bfloat16)
+
+
+def head_grads(tokens, gain, back):
+    rows, width = tokens.shape
+    columns = back.shape[0] * back.shape[1]
+    return pl.pallas_call(
+        head_grads_kernel,
+        out_shape=jax.ShapeDtypeStruct((width, columns), jnp.bfloat16),
+        scratch_shapes=[pltpu.VMEM((columns, rows), jnp.bfloat16)],
+        compiler_params=params(48),
+        cost_estimate=cost(2 * rows * width * columns, 4e6),
+    )(tokens, gain, back)
+
+
 def last_kernel(
     tokens_ref, gain_ref, b0_ref, b1_ref, b2_ref, query_ref, key_ref, value_ref, resid_grad_ref,
-    tokens_grad_ref, weight_grad_ref, normed_turned, back_turned,
+    tokens_grad_ref, gain_grad_ref, back_turned,
 ):
     rows, width = tokens_ref.shape
     inputs = tokens_ref[...].astype(jnp.float32)
     inverse = lax.rsqrt(jnp.mean(inputs * inputs, -1, keepdims=True) + epsilon)
     normed = inputs * inverse
-    normed_turned[...] = (normed * gain_ref[...]).T.astype(jnp.bfloat16)
     owners = b0_ref.shape[0]
     for i in range(3):
         for j, ref in enumerate((b0_ref, b1_ref, b2_ref)):
@@ -618,11 +769,10 @@
     for i, ref in enumerate((query_ref, key_ref, value_ref)):
         term = dot_nn(ref[...], back_turned[i])
         total = term if total is None else total + term
-        weight_grad_ref[:, i * width : (i + 1) * width] = dot_nt(normed_turned[...], back_turned[i]).astype(jnp.bfloat16)
     first_grads = total.T
     summed = jnp.sum((first_grads * normed).reshape(rows // 8, 8, width), 0)
     column = jnp.sum(summed.T, -1, keepdims=True)
-    weight_grad_ref[:, 3 * width :] = jnp.broadcast_to(column, (width, 128)).astype(jnp.bfloat16)
+    gain_grad_ref[...] = jnp.broadcast_to(column, (width, 128)).astype(jnp.bfloat16)
     scaled = first_grads * gain_ref[...]
     tokens_grad_ref[...] = (
         inverse * (scaled - normed * jnp.mean(scaled * normed, -1, keepdims=True)) + resid_grad_ref[...]
@@ -635,14 +785,11 @@
         last_kernel,
         out_shape=(
             jax.ShapeDtypeStruct((rows, width), jnp.float32),
-            jax.ShapeDtypeStruct((width, 3 * width + 128), jnp.bfloat16),
+            jax.ShapeDtypeStruct((width, 128), jnp.bfloat16),
         ),
-        scratch_shapes=[
-            pltpu.VMEM((width, rows), jnp.bfloat16),
-            pltpu.VMEM((3, width, rows), jnp.bfloat16),
-        ],
+        scratch_shapes=[pltpu.VMEM((3, width, rows), jnp.bfloat16)],
         compiler_params=params(56),
-        cost_estimate=cost(12 * rows * width * width, 2e7),
+        cost_estimate=cost(6 * rows * width * width, 2e7),
     )(tokens, gain, *backs, *weights, resid_grads)
 
 
@@ -681,6 +828,7 @@
     core = lax.axis_index("core")
     tokens, prior, routes, grad = tokens[0], prior_logits[0], routes[0], cotangent[0]
     rows, width = tokens.shape
+    copies = lax.axis_size("xy") * lax.axis_size("core")
     length = rows * owners
     chunks = width // HEAD_DIM // owners
     half_slots = rows // 8
@@ -726,18 +874,13 @@
 
     attention_row, expert_row = attention_gain[None], expert_gain[None]
     qkv_weights = (query_weight, key_weight, value_weight)
-    sent = [project(j, owners, tokens, attention_row, qkv_weights, own_cosine, own_sine) for j in range(chunks)]
-    heads = [exchange(chunk, "expert") for chunk in sent]
-    gate, up, down = (gather_weight(weight) for weight in (gate_weight, up_weight, down_weight))
+    attended, logs, heads, outs, gate, up, down = attend_phase(
+        tokens, attention_row, qkv_weights, own_cosine, own_sine, bias, (gate_weight, up_weight, down_weight), copies
+    )
+    attended = [attended[j].reshape(owners * HEAD_DIM, rows) for j in range(chunks)]
+    gate, up, down = (full.reshape(-1, full.shape[-1]) for full in (gate, up, down))
     codes = slot_codes(routes, half_slots)
     codes_row = codes.T
-
-    attended, logs, outs = [], [], []
-    for chunk in heads:
-        out, log = attend(bias, chunk)
-        outs.append(out)
-        logs.append(log)
-        attended.append(exchange(out, "expert").reshape(owners * HEAD_DIM, rows))
 
     mixer = jnp.concatenate(
         [router_weight, constant_weight, jnp.zeros((width, 128 - NEXP - 4), jnp.bfloat16)], 1
@@ -758,48 +901,63 @@
         f, back, dot, hid, dg, du = expert(x, d, gate, up, down)
         backs.append(to_experts(back))
         dots.append(exchange(dot[0].reshape(NFFN, half_slots), planes).reshape(1, rows))
-        for kept, item in zip((xs, ds, fs, hids, gates, ups), (x, d, to_experts(f), hid, dg, du)):
+        for kept, item in zip((xs, ds, fs, hids, gates, ups), (x, d, f, hid, dg, du)):
             kept.append(item)
-    gate_part, up_part, down_part = (
-        scatter_weight(grads) for grads in weight_grads(xs, ds, hids, gates, ups)
+    *backs, grads_gate, grads_up, grads_down = lax.optimization_barrier(
+        (*backs, *weight_grads(xs, ds, hids, gates, ups))
     )
+    gate_part, up_part, down_part = (scatter_weight(grads) for grads in (grads_gate, grads_up, grads_down))
 
     vector = jnp.concatenate([constant_vector, jnp.zeros((6, width), jnp.float32)], 0)
-    resid_grads, *grads_out, out_grad, sums, prior_sums, prior_grad = turn(
+    resid_grads, *grads_out, out_grad, prior_grad = turn(
         resid, small, grad, prior, routes, codes, backs, jnp.concatenate(dots, 1), vector, expert_row,
         mixer.T, prior_turned, out_weight, attended,
     )
-    result = combine(resid, small, routes, codes, fs, vector, expert_row)
-
-    own_backs = []
+    fs[0], grads_out[0] = lax.optimization_barrier((fs[0], grads_out[0]))
+
+    def over_copies(partial):
+        return lax.psum_scatter(partial, ("xy", "core"), scatter_dimension=1, tiled=True)
+
+    out_grad, gate_part = lax.optimization_barrier((out_grad, gate_part))
+    own_backs, parts = [], [over_copies(out_grad)]
     for j in range(chunks):
-        head_grads = exchange(grads_out[j].reshape(owners, HEAD_DIM, rows), "expert")
-        back = attend_back(bias, cosine, sine, heads[j], outs[j], logs[j], head_grads)
-        own_backs.append(exchange(back, "expert"))
-    tokens_grad, qkv_grads = last(tokens, attention_row, own_backs, qkv_weights, resid_grads)
-
-    def reduce_rows(partial):
-        part = lax.psum_scatter(partial, ("xy", "core"), scatter_dimension=1, tiled=True)
-        part = lax.psum_scatter(part, "expert", scatter_dimension=0, tiled=True)
-        return lax.all_gather(part, ("xy", "core"), axis=1, tiled=True).astype(jnp.float32)
-
-    out_total = reduce_rows(out_grad)
-    qkv_total = reduce_rows(qkv_grads)
-    sums, prior_sums = lax.psum((sums, prior_sums), everyone)
+        grads_in = exchange(grads_out[j].reshape(owners, HEAD_DIM, rows), "expert")
+        back = exchange(attend_back(bias, cosine, sine, heads[j], outs[j], logs[j : j + 1], grads_in), "expert")
+        own_backs.append(back)
+        parts.append(over_copies(head_grads(tokens, attention_row, back)))
+    fs[1], own_backs[0] = lax.optimization_barrier((fs[1], own_backs[0]))
+    result = combine(resid, small, routes, codes, [to_experts(f) for f in fs], vector, expert_row)
+    tokens_grad, gain_grads = last(tokens, attention_row, own_backs, qkv_weights, resid_grads)
+    parts.append(over_copies(gain_grads))
+    sizes = [part.shape[1] for part in parts]
     share = width // owners
-    mine = lax.dynamic_slice_in_dim(sums, member * share, share, 1)
+    joined = jnp.concatenate(parts, 1)
+    joined = exchange(joined.reshape(owners, share, joined.shape[1]), "expert")
+    joined = jnp.sum(joined.astype(jnp.float32), 0).astype(jnp.bfloat16)
+    joined = lax.all_gather(joined, ("xy", "core"), axis=0, tiled=False)
+    totals, begin = [], 0
+    for size in sizes:
+        part = joined[:, :, begin : begin + size].transpose(1, 0, 2).reshape(share, -1)
+        totals.append(part.astype(jnp.float32))
+        begin += size
+    out_total, *head_totals, gain_total = totals
+    span = owners * HEAD_DIM
+    qkv_totals = [
+        jnp.concatenate([part[:, i * span : (i + 1) * span] for part in head_totals], 1) for i in range(3)
+    ]
+    small_total = out_total[:, width:]
     return (
         result[None],
         tokens_grad[None],
         prior_grad[None],
-        *(qkv_total[:, i * width : (i + 1) * width] for i in range(3)),
-        out_total,
-        qkv_total[:, 3 * width],
-        jnp.sum(mine[24:32], 0),
-        mine[:NEXP].T,
-        lax.dynamic_slice_in_dim(prior_sums, member * (NEXP // owners), NEXP // owners, 0)[:, :NEXP],
-        mine[NEXP : NEXP + 4].T,
-        mine[16:18],
+        *qkv_totals,
+        out_total[:, :width],
+        gain_total[:, 0],
+        small_total[:, 24],
+        small_total[:, :NEXP],
+        small_total[: NEXP // owners, 32 : 32 + NEXP],
+        small_total[:, NEXP : NEXP + 4],
+        small_total[:, 16:18].T,
         gate_part,
         up_part,
         down_part,

time: 837 us -> 860 us (1.027)
  Pallas kernels: 184 us -> 268 us
  blocking collectives: 176 us -> 117 us
  waiting for transfers between devices: 287 us -> 320 us
  starting transfers between devices: 84.3 us -> 56 us
    pallas_call x6 -> x4, Pallas kernels: 28.3 us -> 119 us  [the longest x1 115 us: attend_phase(): pl.pallas_call(attend_phase_kernel, in_specs=[vmem] * 8 + [hbm] * 3, out_...]
    unnamed x13 -> x14, waiting for transfers between devices: 86.5 us -> 172 us
    all_to_all x17 -> x12, waiting for transfers between devices: 141 us -> 93 us  [exchange(): return lax.all_to_all(values, axes, split_axis=0, concat_axis=0, tiled=True)]
    psum x1 -> x0, blocking collectives: 43.4 us -> none  [per_device(): sums, prior_sums = lax.psum((sums, prior_sums), everyone)]
    all_to_all x17 -> x12, starting transfers between devices: 80.8 us -> 52.3 us  [exchange(): return lax.all_to_all(values, axes, split_axis=0, concat_axis=0, tiled=True)]
    all_gather x2 -> x0, blocking collectives: 25.5 us -> none  [reduce_rows(): lax.all_gather(part, ('xy', 'core'), axis=1, tiled=True).astype(jnp.float32)]
    all_gather x3 -> x1, waiting for transfers between devices: 0.02 us -> 24.1 us  [per_device(): joined = lax.all_gather(joined, ('xy', 'core'), axis=0, tiled=False)]
    reduce_scatter x2 -> x0, waiting for transfers between devices: 18 us -> none  [reduce_rows(): part = lax.psum_scatter(part, 'expert', scatter_dimension=0, tiled=True)]
  transfers between devices with their start and end apart: 34 -> 24, of which waited for: 17 -> 17; matrix products, arithmetic and copies ran while one was open for 6% -> 4% of each run, Pallas kernels for 20% -> 15%
where the time goes in v2:
time: 860 us; the launch traced here: 854 us
  waiting for transfers between devices  320 us (37%)
  Pallas kernels  268 us (31%)
  blocking collectives  117 us (14%)
  starting transfers between devices  56 us (7%)
  local copies, waits for them, and re-layouts  55.2 us (6%)
  other arithmetic  21.8 us (3%)
  between operations  15.1 us (2%)
    unnamed x14, waiting for transfers between devices  172 us
    all_to_all x5, blocking collectives, exchange(): return lax.all_to_all(values, axes, split_axis=0, concat_axis=0, tiled=True)  117 us
    pallas_call x1, Pallas kernels, attend_phase(): pl.pallas_call(attend_phase_kernel, in_specs=[vmem] * 8 + [hbm] * 3, out_...  115 us
    all_to_all x12, waiting for transfers between devices, exchange(): return lax.all_to_all(values, axes, split_axis=0, concat_axis=0, tiled=True)  93 us
    all_to_all x12, starting transfers between devices, exchange(): return lax.all_to_all(values, axes, split_axis=0, concat_axis=0, tiled=True)  52.3 us
    pallas_call x2, Pallas kernels, expert(): pl.pallas_call(expert_kernel, grid=(units // part,), in_specs=[whole, who...  44.7 us
    pallas_call x3, Pallas kernels, attend_back(): pl.pallas_call(attend_back_kernel, out_shape=jax.ShapeDtypeStruct((source...  39.6 us
    unnamed x141, local copies, waits for them, and re-layouts  30.5 us
  transfers between devices with their start and end apart: 24, of which 17 were waited for; matrix products, arithmetic and copies ran while one was open for 4% of the time, Pallas kernels for 15%

profile of v2, /device:TPU:1, one launch (start us, length us, event | category | flops | bytes accessed | tf_op | source)
XLA Modules:
  0.0 854.2 jit_solution(12084271504123781033)
XLA Ops:
  13.0 114.5 %shard_map.297 = (bf16[3,4,64,640]{3,2,1,0:T(8,128)(2,1)}, f32[8,2560]{1,0:T(8,128)}, bf16[3,4,192,640]{3,2,1,0:T(8,128)(2,1)}, bf16[3,4,64,640]{3,2,1,0:T(8,128...) custom-call(bf16[640,768]{1,0:T(8,128)(2,1)} %bitcast.93, ...), custom_call_target="tpu_custom_call" | custom-call | flops 10000000000 | bytes 50000000 | tf_op jit(solution)/shard_map/pallas_call | solution.py:347
  135.3 10.3 %shard_map.298 = (f32[640,768]{1,0:T(8,128)}, f32[640,128]{1,0:T(8,128)S(1)}, bf16[640,768]{1,0:T(8,128)(2,1)S(1)}, bf16[640,768]{1,0:T(8,128)(2,1)}) custom-call(bf16[640,768]{1,0:T(8,128)(2,1)S(1)} %bitcast.95, bf16[256,640]{1,0:T(8,128)(2,1)S(1)} %bitcast.119, bf16[256,640]{1,0:T(8,128)(2,1)S(1)} %bitcast.117, bf16[256,640]{1,0:T(8,128)(2,1)S(1)} %bitcast.115, ...), custom_call_target="tpu_custom_call" | custom-call | flops 2768240640 | bytes 10000000 | tf_op jit(solution)/shard_map/pallas_call | solution.py:427
  145.6 27.9 %all_to_all.93 = bf16[8,80,768]{2,1,0:T(8,128)(2,1)} all-to-all(bf16[8,80,768]{2,1,0:T(8,128)(2,1)S(1)} %bitcast.112), channel_id=1, replica_groups=mesh['expert'=4,'xy'=4,'core'=2] {'expert','core'}, dimensions={0} | all-to-all | bytes 1966080 | tf_op jit(solution)/shard_map/all_to_all | solution.py:841
  182.2 20.2 %all-to-all-done.3 = bf16[8,80,768]{2,1,0:T(8,128)(2,1)S(1)} async-done(((bf16[8,80,768]{2,1,0:T(8,128)(2,1)}), bf16[8,80,768]{2,1,0:T(8,128)(2,1)S(1)}, u32[]{:S(2)}, u32[]{:S(2)}) %all-to-all-start.3) | async-done | bytes 983072 | tf_op jit(solution)/shard_map/all_to_all | solution.py:841
  202.3 28.2 %all_to_all.94 = bf16[8,80,768]{2,1,0:T(8,128)(2,1)} all-to-all(bf16[8,80,768]{2,1,0:T(8,128)(2,1)S(1)} %bitcast.111), channel_id=1, replica_groups=mesh['expert'=4,'xy'=4,'core'=2] {'expert','core'}, dimensions={0} | all-to-all | bytes 1966080 | tf_op jit(solution)/shard_map/all_to_all | solution.py:841
  235.0 22.4 %shard_map.301 = (bf16[640,768]{1,0:T(8,128)(2,1)}, bf16[640,768]{1,0:T(8,128)(2,1)}, f32[8,640]{1,0:T(8,128)S(1)}, bf16[640,2048]{1,0:T(8,128)(2,1)}, bf16[640,...) custom-call(bf16[640,768]{1,0:T(8,128)(2,1)} %bitcast.106, bf16[640,768]{1,0:T(8,128)(2,1)} %bitcast.131, ...), custom_call_target="tpu_custom_call" | custom-call | flops 12079595520 | bytes 30000000 | tf_op jit(solution)/shard_map/pallas_call | solution.py:514
  263.8 22.2 %shard_map.300 = (bf16[640,768]{1,0:T(8,128)(2,1)}, bf16[640,768]{1,0:T(8,128)(2,1)S(1)}, f32[8,640]{1,0:T(8,128)S(1)}, bf16[640,2048]{1,0:T(8,128)(2,1)}, bf16[...) custom-call(bf16[640,768]{1,0:T(8,128)(2,1)} %bitcast.104, bf16[640,768]{1,0:T(8,128)(2,1)} %bitcast.133, ...), custom_call_target="tpu_custom_call" | custom-call | flops 12079595520 | bytes 30000000 | tf_op jit(solution)/shard_map/pallas_call | solution.py:514
  286.2 9.8 %all_to_all.95 = f32[8,1,80]{2,1,0:T(1,128)S(1)} all-to-all(f32[8,1,80]{2,1,0:T(1,128)S(1)} %bitcast.148), channel_id=1, replica_groups=mesh['expert'=4,'xy'=4,'core'=2] {'expert','core'}, dimensions={0} | all-to-all | bytes 5120 | tf_op jit(solution)/shard_map/all_to_all | solution.py:841
  296.0 28.2 %all_to_all.96 = bf16[8,80,768]{2,1,0:T(8,128)(2,1)} all-to-all(bf16[8,80,768]{2,1,0:T(8,128)(2,1)S(1)} %bitcast.110), channel_id=1, replica_groups=mesh['expert'=4,'xy'=4,'core'=2] {'expert','core'}, dimensions={0} | all-to-all | bytes 1966080 | tf_op jit(solution)/shard_map/all_to_all | solution.py:841
  329.9 18.7 %shard_map.302 = (bf16[768,2048]{1,0:T(8,128)(2,1)}, bf16[768,2048]{1,0:T(8,128)(2,1)}, bf16[2048,768]{1,0:T(8,128)(2,1)}) custom-call(bf16[640,768]{1,0:T(8,128)(2,1)S(1)} %bitcast.105, bf16[640,768]{1,0:T(8,128)(2,1)S(1)} %bitcast.107, bf16[640,768]{1,0:T(8,128)(2,1)} %bitcast.134, bf16[640,768]{1,0:T(8,128)(2,1)} %bitcast.132, ...), custom_call_target="tpu_custom_call" | custom-call | flops 12079595520 | bytes 30000000 | tf_op jit(solution)/shard_map/pallas_call | solution.py:557
  353.8 18.5 %shard_map.303 = (f32[640,768]{1,0:T(8,128)}, bf16[256,640]{1,0:T(8,128)(2,1)}, bf16[256,640]{1,0:T(8,128)(2,1)}, bf16[256,640]{1,0:T(8,128)(2,1)}, bf16[768,896]{1,0:T(8,128)(2,1)}, /*index=5*/f32[640,12]{1,0:T(8,128)}) custom-call(f32[640,768]{1,0:T(8,128)} %get-tuple-element.64.resid_ref, f32[640,128]{1,0:T(8,128)} %copy-done.39, ...), custom_call_target="tpu_custom_call" | custom-call | flops 2768240640 | bytes 15000000 | tf_op jit(solution)/shard_map/pallas_call | solution.py:674
  402.6 12.6 %shard_map.304 = bf16[4,192,640]{2,1,0:T(8,128)(2,1)S(1)} custom-call(f32[16,2560]{1,0:T(8,128)S(1)} %copy-done.32, f32[32,2560]{1,0:T(8,128)S(1)} %copy-done.21, f32[32,2560]{1,0:T(8,128)S(1)} %copy-done.19, bf16[4,192,640]{2,1,0:T(8,128)(2,1)S(1)} %get-tuple-element.224.qkv_ref, bf16[4,64,640]{2,1,0:T(8,128)(2,1)S(1)} %get-tuple-element.236.out_ref, ...), custom_call_target="tpu_custom_call" | custom-call | flops 5000000000 | bytes 6000000 | tf_op jit(solution)/shard_map/pallas_call | solution.py:182
  422.6 13.5 %shard_map.306 = bf16[4,192,640]{2,1,0:T(8,128)(2,1)S(1)} custom-call(f32[16,2560]{1,0:T(8,128)S(1)} %copy-done.32, f32[32,2560]{1,0:T(8,128)S(1)} %copy-done.22, f32[32,2560]{1,0:T(8,128)S(1)} %copy-done.19, bf16[4,192,640]{2,1,0:T(8,128)(2,1)S(1)} %get-tuple-element.223.qkv_ref, bf16[4,64,640]{2,1,0:T(8,128)(2,1)S(1)} %copy-done.31, ...), custom_call_target="tpu_custom_call" | custom-call | flops 5000000000 | bytes 6000000 | tf_op jit(solution)/shard_map/pallas_call | solution.py:182
  449.3 13.5 %shard_map.307 = bf16[4,192,640]{2,1,0:T(8,128)(2,1)S(1)} custom-call(f32[16,2560]{1,0:T(8,128)S(1)} %copy-done.32, f32[32,2560]{1,0:T(8,128)S(1)} %copy-done.23, f32[32,2560]{1,0:T(8,128)S(1)} %copy-done.19, bf16[4,192,640]{2,1,0:T(8,128)(2,1)S(1)} %get-tuple-element.222.qkv_ref, bf16[4,64,640]{2,1,0:T(8,128)(2,1)S(1)} %copy-done.30, ...), custom_call_target="tpu_custom_call" | custom-call | flops 5000000000 | bytes 6000000 | tf_op jit(solution)/shard_map/pallas_call | solution.py:182
  474.7 23.7 %all-to-all-done.15.b2_ref.back_ref = bf16[4,192,640]{2,1,0:T(8,128)(2,1)S(1)} async-done(((bf16[4,192,640]{2,1,0:T(8,128)(2,1)}), bf16[4,192,640]{2,1,0:T(8,128)(2,1)S(1)}, u32[]{:S(2)}, u32[]{:S(2)}) %all-to-all-start.15) | async-done | bytes 983072 | tf_op jit(solution)/shard_map/all_to_all | solution.py:841
  532.4 11.0 %reduce-scatter.33.cloned.1.call-done = bf16[16,768]{1,0:T(8,128)(2,1)} async-done(((bf16[128,768]{1,0:T(8,128)(2,1)}), bf16[16,768]{1,0:T(8,128)(2,1)}) %reduce-scatter.33.cloned.1.call-update) | async-done | bytes 24592
  544.3 40.3 %reduce-scatter.27.cloned.1.call-done = bf16[96,768]{1,0:T(8,128)(2,1)} async-done(((bf16[768,768]{1,0:T(8,128)(2,1)}), bf16[96,768]{1,0:T(8,128)(2,1)}) %reduce-scatter.27.cloned.1.call-update) | async-done | bytes 147472
  585.6 38.8 %reduce-scatter.29.cloned.1.call-done = bf16[96,768]{1,0:T(8,128)(2,1)} async-done(((bf16[768,768]{1,0:T(8,128)(2,1)}), bf16[96,768]{1,0:T(8,128)(2,1)}) %reduce-scatter.29.cloned.1.call-update) | async-done | bytes 147472
  625.5 39.1 %reduce-scatter.31.cloned.1.call-done = bf16[96,768]{1,0:T(8,128)(2,1)} async-done(((bf16[768,768]{1,0:T(8,128)(2,1)}), bf16[96,768]{1,0:T(8,128)(2,1)}) %reduce-scatter.31.cloned.1.call-update) | async-done | bytes 147472
  665.7 40.3 %reduce-scatter.25.cloned.1.call-done = bf16[112,768]{1,0:T(8,128)(2,1)} async-done(((bf16[896,768]{1,0:T(8,128)(2,1)}), bf16[112,768]{1,0:T(8,128)(2,1)}) %reduce-scatter.25.cloned.1.call-update) | async-done | bytes 172048
  707.7 23.4 %all_to_all.97 = bf16[4,192,416]{2,1,0:T(8,128)(2,1)} all-to-all(bf16[4,192,416]{2,1,0:T(8,128)(2,1)S(1)} %bitcast.127), channel_id=1, replica_groups=mesh['expert'=4,'xy'=4,'core'=2] {'expert'}, dimensions={0} | all-to-all | bytes 1277952 | tf_op jit(solution)/shard_map/all_to_all | solution.py:841
  739.4 21.6 %all-to-all-done.11 = bf16[8,80,768]{2,1,0:T(8,128)(2,1)S(1)} async-done(((bf16[8,80,768]{2,1,0:T(8,128)(2,1)}), bf16[8,80,768]{2,1,0:T(8,128)(2,1)S(1)}, u32[]{:S(2)}, u32[]{:S(2)}) %all-to-all-start.11) | async-done | bytes 983072 | tf_op jit(solution)/shard_map/all_to_all | solution.py:841
  770.3 30.2 %reduce-scatter.21.cloned.1.call-done = bf16[192,2048]{1,0:T(8,128)(2,1)} async-done(((bf16[768,2048]{1,0:T(8,128)(2,1)}), bf16[192,2048]{1,0:T(8,128)(2,1)}) %reduce-scatter.21.cloned.1.call-update) | async-done | bytes 786448 | tf_op jit(solution)/shard_map/reduce_scatter | solution.py:850
  805.2 24.1 %all-gather.3.cloned.1.call-done = bf16[1536,416]{1,0:T(8,128)(2,1)} async-done(((bf16[192,416]{1,0:T(8,128)(2,1)}), bf16[1536,416]{1,0:T(8,128)(2,1)}) %all-gather.3.cloned.1.call-update) | async-done | bytes 1277968 | tf_op jit(solution)/shard_map/all_gather | solution.py:937
  (288 shorter events, 186.1 us)
Async XLA Ops:
  173.5 28.9 %all-to-all-start.3 = ((bf16[8,80,768]{2,1,0:T(8,128)(2,1)}), bf16[8,80,768]{2,1,0:T(8,128)(2,1)S(1)}, u32[]{:S(2)}, u32[]{:S(2)}) async-start(bf16[8,80,768]{2,1,0:T(8,128)(2,1)} %bitcast.18), calls=%async_computation.3 | async-start | bytes 1966080 | tf_op jit(solution)/shard_map/all_to_all | solution.py:841
  230.6 28.8 %all-to-all-start.1 = ((bf16[8,80,768]{2,1,0:T(8,128)(2,1)}), bf16[8,80,768]{2,1,0:T(8,128)(2,1)S(1)}, u32[]{:S(2)}, u32[]{:S(2)}) async-start(bf16[8,80,768]{2,1,0:T(8,128)(2,1)} %bitcast.11), calls=%async_computation.1 | async-start | bytes 1966080 | tf_op jit(solution)/shard_map/all_to_all | solution.py:841
  259.3 26.9 %all-to-all-start.7 = ((f32[8,1,80]{2,1,0:T(1,128)}), f32[8,1,80]{2,1,0:T(1,128)S(1)}, u32[]{:S(2)}, u32[]{:S(2)}) async-start(f32[8,1,80]{2,1,0:T(1,128)} %bitcast.25), calls=%async_computation.7 | async-start | bytes 8192 | tf_op jit(solution)/shard_map/all_to_all | solution.py:841
  324.1 28.8 %all-to-all-start.5 = ((bf16[8,80,768]{2,1,0:T(8,128)(2,1)}), bf16[8,80,768]{2,1,0:T(8,128)(2,1)S(1)}, u32[]{:S(2)}, u32[]{:S(2)}) async-start(bf16[8,80,768]{2,1,0:T(8,128)(2,1)} %bitcast.22), calls=%async_computation.5 | async-start | bytes 1966080 | tf_op jit(solution)/shard_map/all_to_all | solution.py:841
  372.3 12.1 %all-to-all-start.9 = ((bf16[4,64,640]{2,1,0:T(8,128)(2,1)}), bf16[4,64,640]{2,1,0:T(8,128)(2,1)S(1)}, u32[]{:S(2)}, u32[]{:S(2)}) async-start(bf16[4,64,640]{2,1,0:T(8,128)(2,1)} %bitcast.140), calls=%async_computation.9 | async-start | bytes 655360 | tf_op jit(solution)/shard_map/all_to_all | solution.py:841
  375.8 143.6 %reduce-scatter.19.cloned.1.call-start = ((), (), s32[]{:S(2)}) async-start(), calls=%async_computation.25 | async-start | bytes 3932160 | tf_op jit(solution)/shard_map/reduce_scatter | solution.py:850
  384.4 10.4 %all-to-all-start.12 = ((bf16[4,64,640]{2,1,0:T(8,128)(2,1)}), bf16[4,64,640]{2,1,0:T(8,128)(2,1)}, u32[]{:S(2)}, u32[]{:S(2)}) async-start(bf16[4,64,640]{2,1,0:T(8,128)(2,1)} %bitcast.38), calls=%async_computation.12 | async-start | bytes 655360 | tf_op jit(solution)/shard_map/all_to_all | solution.py:841
  394.8 21.3 %all-to-all-start.14 = ((bf16[4,64,640]{2,1,0:T(8,128)(2,1)}), bf16[4,64,640]{2,1,0:T(8,128)(2,1)}, u32[]{:S(2)}, u32[]{:S(2)}) async-start(bf16[4,64,640]{2,1,0:T(8,128)(2,1)} %bitcast.139), calls=%async_computation.14 | async-start | bytes 655360 | tf_op jit(solution)/shard_map/all_to_all | solution.py:841
  416.2 27.3 %all-to-all-start.10 = ((bf16[4,192,640]{2,1,0:T(8,128)(2,1)}), bf16[4,192,640]{2,1,0:T(8,128)(2,1)S(1)}, u32[]{:S(2)}, u32[]{:S(2)}) async-start(bf16[4,192,640]{2,1,0:T(8,128)(2,1)} %copy-done.17), calls=%async_computation.10 | async-start | bytes 1966080 | tf_op jit(solution)/shard_map/all_to_all | solution.py:841
  443.4 27.7 %all-to-all-start.13 = ((bf16[4,192,640]{2,1,0:T(8,128)(2,1)}), bf16[4,192,640]{2,1,0:T(8,128)(2,1)S(1)}, u32[]{:S(2)}, u32[]{:S(2)}) async-start(bf16[4,192,640]{2,1,0:T(8,128)(2,1)} %copy-done.15), calls=%async_computation.13 | async-start | bytes 1966080 | tf_op jit(solution)/shard_map/all_to_all | solution.py:841
  471.1 27.3 %all-to-all-start.15 = ((bf16[4,192,640]{2,1,0:T(8,128)(2,1)}), bf16[4,192,640]{2,1,0:T(8,128)(2,1)S(1)}, u32[]{:S(2)}, u32[]{:S(2)}) async-start(bf16[4,192,640]{2,1,0:T(8,128)(2,1)} %copy-done.16), calls=%async_computation.15 | async-start | bytes 1966080 | tf_op jit(solution)/shard_map/all_to_all | solution.py:841
  474.7 68.7 %reduce-scatter.33.cloned.1.call-start = ((), (), s32[]{:S(2)}) async-start(), calls=%async_computation.33 | async-start | bytes 221184
  510.3 74.2 %reduce-scatter.27.cloned.1.call-start = ((), (), s32[]{:S(2)}) async-start(), calls=%async_computation.30 | async-start | bytes 1327104
  513.3 111.2 %reduce-scatter.29.cloned.1.call-start = ((), (), s32[]{:S(2)}) async-start(), calls=%async_computation.31 | async-start | bytes 1327104
  516.4 148.3 %reduce-scatter.31.cloned.1.call-start = ((), (), s32[]{:S(2)}) async-start(), calls=%async_computation.32 | async-start | bytes 1327104
  519.3 186.7 %reduce-scatter.25.cloned.1.call-start = ((), (), s32[]{:S(2)}) async-start(), calls=%async_computation.29 | async-start | bytes 1548288
  520.6 2.9 collective-permute-start
  527.1 241.0 %reduce-scatter.23.cloned.1.call-start = ((), (), s32[]{:S(2)}) async-start(), calls=%async_computation.27 | async-start | bytes 3932160 | tf_op jit(solution)/shard_map/reduce_scatter | solution.py:850
  527.8 272.7 %reduce-scatter.21.cloned.1.call-start = ((), (), s32[]{:S(2)}) async-start(), calls=%async_computation.26 | async-start | bytes 3932160 | tf_op jit(solution)/shard_map/reduce_scatter | solution.py:850
  528.6 179.1 %all-to-all-start.8 = ((bf16[8,80,768]{2,1,0:T(8,128)(2,1)}), bf16[8,80,768]{2,1,0:T(8,128)(2,1)S(1)}, u32[]{:S(2)}, u32[]{:S(2)}) async-start(bf16[8,80,768]{2,1,0:T(8,128)(2,1)} %bitcast.28), calls=%async_computation.8 | async-start | bytes 1966080 | tf_op jit(solution)/shard_map/all_to_all | solution.py:841
  731.1 29.8 %all-to-all-start.11 = ((bf16[8,80,768]{2,1,0:T(8,128)(2,1)}), bf16[8,80,768]{2,1,0:T(8,128)(2,1)S(1)}, u32[]{:S(2)}, u32[]{:S(2)}) async-start(bf16[8,80,768]{2,1,0:T(8,128)(2,1)} %bitcast.33), calls=%async_computation.11 | async-start | bytes 1966080 | tf_op jit(solution)/shard_map/all_to_all | solution.py:841
  736.6 92.7 %all-gather.3.cloned.1.call-start = ((), (), s32[]{:S(2)}) async-start(), calls=%async_computation.28 | async-start | bytes 1769472 | tf_op jit(solution)/shard_map/all_gather | solution.py:937
  769.4 33.0 %collective-permute-start.2 = (bf16[256,768]{1,0:T(8,128)(2,1)S(1)}, bf16[256,768]{1,0:T(8,128)(2,1)S(1)}, u32[]{:S(2)}, u32[]{:S(2)}) collective-permute-start(bf16[256,768]{1,0:T(8,128)(2,1)S(1)} %broadcast_select_fusion), channel_id=1, source_target_pairs={{0,1},{1,0},{2,3},{3,2},{4,5},{5,4},{6,7},{7,6},{8,9},{9,8},{10,11... | collective-permute-start | bytes 1179656 | tf_op jit(solution)/shard_map/ppermute | solution.py:838
  801.7 2.1 collective-permute-start.1
  (61 other events, 798.2 us)
Sparse Core Ops, SparseCore 0:
  379.6 45.2 reduce-scatter.18
  510.4 32.8 reduce-scatter.32
  547.5 36.9 reduce-scatter.26
  587.6 36.7 reduce-scatter.28
  627.8 36.7 reduce-scatter.30
  668.3 37.6 reduce-scatter.24
  709.2 44.0 reduce-scatter.22
  756.5 43.9 reduce-scatter.20
  803.1 26.0 all-gather.2

commit v3 on v2

--- a/solution.py
+++ b/solution.py
@@ -1,3 +1,5 @@
+import functools
+
 import jax
 import jax.numpy as jnp
 from jax import lax
@@ -110,7 +112,7 @@
         out_ref[z] = o_ref[:, pl.ds(z * rows, rows)]
 
 
-def attend_back_kernel(
+def attend_back_head(
     bias_ref, cos_ref, sin_ref, qkv_ref, out_ref, lse_ref, grad_ref, back_ref,
     qt_ref, kt_ref, dt_ref, q_ref, k_ref, v_ref, d_ref, delta_ref, dq_ref, dk_ref, dv_ref, triangle,
 ):
@@ -171,27 +173,6 @@
                 [first * cosine + second * sine, second * cosine - first * sine], 0
             ).astype(jnp.bfloat16)
         back_ref[z, 2 * HEAD_DIM :] = dv_ref[span, :].T.astype(jnp.bfloat16)
-
-
-def attend_back(bias, cosine, sine, qkv, out, lse, grad):
-    sources, _, rows = qkv.shape
-    length = sources * rows
-    turned = pltpu.VMEM((HEAD_DIM, length), jnp.bfloat16)
-    plain = pltpu.VMEM((length, HEAD_DIM), jnp.bfloat16)
-    wide = pltpu.VMEM((length, HEAD_DIM), jnp.float32)
-    return pl.pallas_call(
-        attend_back_kernel,
-        out_shape=jax.ShapeDtypeStruct((sources, 3 * HEAD_DIM, rows), jnp.bfloat16),
-        scratch_shapes=[
-            turned, turned, turned, plain, plain, plain, plain,
-            pltpu.VMEM((1, length), jnp.float32),
-            pltpu.VMEM((HEAD_DIM, length), jnp.float32),
-            wide, wide,
-            pltpu.VMEM((TILE, TILE), jnp.float32),
-        ],
-        compiler_params=pltpu.CompilerParams(vmem_limit_bytes=48 * MIB),
-        cost_estimate=pl.CostEstimate(flops=5 * 10**9, bytes_accessed=6 * 10**6, transcendentals=3 * 10**6),
-    )(bias, cosine, sine, qkv, out, lse, grad)
 
 
 def params(limit):
@@ -380,7 +361,7 @@
 
 
 def middle_kernel(
-    tokens_ref, a0_ref, a1_ref, a2_ref, out_weight_ref, gain_ref, mixer_ref, prior_ref, prior_weight_ref,
+    tokens_ref, attended_ref, out_weight_ref, gain_ref, mixer_ref, prior_ref, prior_weight_ref,
     routes_ref, codes_ref, resid_ref, small_ref, first_ref, second_ref, hidden_ref,
 ):
     rows, width = tokens_ref.shape
@@ -388,8 +369,7 @@
     @pl.loop(0, rows // SEG)
     def _(step):
         span = pl.ds(pl.multiple_of(step * SEG, SEG), SEG)
-        attended = jnp.concatenate([ref[:, span] for ref in (a0_ref, a1_ref, a2_ref)], 0)
-        attended = attended.astype(jnp.float32).T.astype(jnp.bfloat16)
+        attended = attended_ref[:, span].astype(jnp.float32).T.astype(jnp.bfloat16)
         resid = tokens_ref[span, :].astype(jnp.float32) + dot_nn(attended, out_weight_ref[...])
         inverse = lax.rsqrt(jnp.mean(resid * resid, -1, keepdims=True) + epsilon)
         hidden = (resid * inverse * gain_ref[...]).astype(jnp.bfloat16)
@@ -435,139 +415,218 @@
         scratch_shapes=[pltpu.VMEM((rows, width), jnp.bfloat16)],
         compiler_params=params(48),
         cost_estimate=cost(4 * rows * width * width + 4 * rows * rows * width, 1e7),
-    )(tokens, *attended, out_weight, gain, mixer, prior, prior_weight, routes, codes_row)
-
-
-def scatter_kernel(small_ref, grad_ref, codes_ref, first_ref, second_ref, scaled_ref):
-    rows, width = grad_ref.shape
-    small = small_ref[...]
-    grad = grad_ref[...].astype(jnp.float32)
+    )(tokens, attended, out_weight, gain, mixer, prior, prior_weight, routes, codes_row)
+
+
+def plane_partners(owners):
+    total = 2 * owners
+    place = lax.axis_index("expert") * 2 + lax.axis_index("core")
+    result = []
+    for step in sorted(range(1, total), key=lambda k: -min(k, total - k)):
+        index = lax.rem(place + step, total)
+        result.append((step, index, {"expert": index // 2, "core": lax.rem(index, 2)}))
+    return result
+
+
+def expert_phase_kernel(
+    xa_ref, xb_ref, small_ref, grad_ref, codes_ref, gate_hbm, up_hbm, down_hbm,
+    back_out, dots_out, f_out, gate_grad, up_grad, down_grad,
+    gate_ref, up_ref, down_ref, scaled_ref, d_sent, x_got, d_got, back_sent, back_got, dots_sent, dots_got,
+    f_sum, back_sum, hid_ref, one_ref, two_ref, x_turned, d_turned, stage, stage_down,
+    x_send, x_recv, d_send, d_recv, back_send, back_recv, dots_send, dots_recv, local_sem, stage_sem,
+):
+    experts, slots, width = x_got.shape[1:]
+    rows = experts * slots
+    units = gate_ref.shape[1]
+    owners = experts // 2
+    place = lax.axis_index("expert") * 2 + lax.axis_index("core")
+    partners = plane_partners(owners)
+    greet([item[2] for item in partners], [])
+    loads = [
+        pltpu.make_async_copy(source, target, local_sem.at[i])
+        for i, (source, target) in enumerate(((gate_hbm, gate_ref), (up_hbm, up_ref), (down_hbm, down_ref)))
+    ]
+    for load in loads:
+        load.start()
+
+    def send(source, target, sends, receives, half, locals_at):
+        copies = []
+        local = pltpu.make_async_copy(source(place), target.at[half, place], local_sem.at[locals_at + half])
+        local.start()
+        for step, index, device in partners:
+            copy = remote(source(index), target.at[half, place], sends.at[half, step], receives.at[half, step], device)
+            copy.start()
+            copies.append(copy)
+        return local, copies
+
+    def arrive(group):
+        group[0].wait()
+        for copy in group[1]:
+            copy.wait_recv()
+
+    x_refs = (xa_ref, xb_ref)
+    x_groups = [send(lambda e, ref=ref: ref.at[e], x_got, x_send, x_recv, h, 3) for h, ref in enumerate(x_refs)]
     for c in range(2):
-        scaled_ref[c * rows : (c + 1) * rows, :] = (small[:, c : c + 1] * grad).astype(jnp.bfloat16)
-    slots = first_ref.shape[0]
-    for half, ref in enumerate((first_ref, second_ref)):
-        index = lax.broadcasted_iota(jnp.int32, (slots, rows), 0) + half * slots
+        scaled_ref[c * rows : (c + 1) * rows, :] = (
+            small_ref[:, c : c + 1] * grad_ref[...].astype(jnp.float32)
+        ).astype(jnp.bfloat16)
+    d_groups = []
+    for half in range(2):
+        index = lax.broadcasted_iota(jnp.int32, (rows, rows), 0) + half * rows
         chosen = jnp.concatenate([(codes_ref[c : c + 1, :] == index).astype(jnp.bfloat16) for c in range(2)], 1)
-        ref[...] = dot_nn(chosen, scaled_ref[...]).astype(jnp.bfloat16)
-
-
-def scatter(small, grad, codes_row):
+        d_sent[half] = dot_nn(chosen, scaled_ref[...]).astype(jnp.bfloat16).reshape(experts, slots, width)
+        d_groups.append(send(lambda e, half=half: d_sent.at[half, e], d_got, d_send, d_recv, half, 5))
+    for load in loads:
+        load.wait()
+
+    part = 512
+    tile = rows // 2
+
+    def forward(half):
+        x = x_got[half].reshape(rows, width)
+        f_sum[...] = jnp.zeros_like(f_sum)
+        x_turned[:, half * rows : (half + 1) * rows] = x.astype(jnp.float32).T.astype(jnp.bfloat16)
+
+        @pl.loop(0, units // part)
+        def _(step):
+            columns = pl.ds(pl.multiple_of(step * part, part), part)
+            for r in range(2):
+                near = slice(r * tile, (r + 1) * tile)
+                far = pl.ds(half * rows + r * tile, tile)
+                gate_pre = dot_nn(x[near], gate_ref[:, columns])
+                up_pre = dot_nn(x[near], up_ref[:, columns])
+                sigmoid = 1.0 / (1.0 + jnp.exp(-gate_pre))
+                active = gate_pre * sigmoid
+                hid = (active * up_pre).astype(jnp.bfloat16)
+                hid_ref[far, columns] = hid
+                one_ref[far, columns] = (up_pre * (sigmoid + active * (1.0 - sigmoid))).astype(jnp.bfloat16)
+                two_ref[far, columns] = active.astype(jnp.bfloat16)
+                f_sum[near, :] += dot_nn(hid, down_ref[columns, :])
+
+        f_out[half] = f_sum[...].astype(jnp.bfloat16).reshape(experts, slots, width)
+
+    def backward(half):
+        d = d_got[half].reshape(rows, width)
+        back_sum[...] = jnp.zeros_like(back_sum)
+        d_turned[:, half * rows : (half + 1) * rows] = d.astype(jnp.float32).T.astype(jnp.bfloat16)
+
+        @pl.loop(0, units // part)
+        def _(step):
+            columns = pl.ds(pl.multiple_of(step * part, part), part)
+            for r in range(2):
+                near = slice(r * tile, (r + 1) * tile)
+                far = pl.ds(half * rows + r * tile, tile)
+                mid = dot_nt(d[near], down_ref[columns, :])
+                dg = (mid * one_ref[far, columns].astype(jnp.float32)).astype(jnp.bfloat16)
+                du = (mid * two_ref[far, columns].astype(jnp.float32)).astype(jnp.bfloat16)
+                one_ref[far, columns] = dg
+                two_ref[far, columns] = du
+                back_sum[near, :] += dot_nt(dg, gate_ref[:, columns]) + dot_nt(du, up_ref[:, columns])
+
+        back_sent[half] = back_sum[...].astype(jnp.bfloat16).reshape(experts, slots, width)
+
+    def dots(half):
+        ones = jnp.ones((8, width), jnp.float32)
+        for e in range(experts):
+            product = f_out[half, e].astype(jnp.float32) * d_got[half, e].astype(jnp.float32)
+            total = lax.dot_general(
+                ones, product, (((1,), (1,)), ((), ())), precision=precise, preferred_element_type=jnp.float32
+            )
+            dots_sent[half, e] = jnp.concatenate([total, jnp.zeros((8, 128 - slots), jnp.float32)], 1)
+
+    for half in range(2):
+        arrive(x_groups[half])
+        forward(half)
+    back_groups, dots_groups = [], []
+    for half in range(2):
+        arrive(d_groups[half])
+        backward(half)
+        back_groups.append(send(lambda e, half=half: back_sent.at[half, e], back_got, back_send, back_recv, half, 7))
+        dots(half)
+        dots_groups.append(send(lambda e, half=half: dots_sent.at[half, e], dots_got, dots_send, dots_recv, half, 9))
+
+    piece = 256
+    steps = units // piece
+
+    def stores(step, slot):
+        columns = pl.ds(pl.multiple_of(step * piece, piece), piece)
+        return [
+            pltpu.make_async_copy(stage.at[0, slot], gate_grad.at[:, columns], stage_sem.at[0, slot]),
+            pltpu.make_async_copy(stage.at[1, slot], up_grad.at[:, columns], stage_sem.at[1, slot]),
+            pltpu.make_async_copy(stage_down.at[slot], down_grad.at[columns, :], stage_sem.at[2, slot]),
+        ]
+
+    @pl.loop(0, steps // 2)
+    def _(pair):
+        for slot in range(2):
+            step = pair * 2 + slot
+            columns = pl.ds(pl.multiple_of(step * piece, piece), piece)
+
+            @pl.when(pair > 0)
+            def _():
+                for store in stores(step, slot):
+                    store.wait()
+
+            stage[0, slot] = dot_nn(x_turned[...], one_ref[:, columns]).astype(jnp.bfloat16)
+            stage[1, slot] = dot_nn(x_turned[...], two_ref[:, columns]).astype(jnp.bfloat16)
+            stage_down[slot] = dot_nn(d_turned[...], hid_ref[:, columns]).T.astype(jnp.bfloat16)
+            for store in stores(step, slot):
+                store.start()
+
+    for slot in range(2):
+        for store in stores(steps - 2 + slot, slot):
+            store.wait()
+    for group in back_groups + dots_groups:
+        arrive(group)
+    back_out[...] = back_got[...]
+    dots_out[...] = dots_got[...]
+    for group in x_groups + d_groups + back_groups + dots_groups:
+        for copy in group[1]:
+            copy.wait_send()
+
+
+def expert_phase(x_parts, small, grad, codes_row, gate, up, down):
     rows, width = grad.shape
+    units = gate.shape[1]
+    slots = rows // NFFN
+    both = (2, NFFN, slots, width)
+    dots = (2, NFFN, 8, 128)
+    vmem, hbm = pl.BlockSpec(memory_space=pltpu.VMEM), pl.BlockSpec(memory_space=pl.ANY)
+    sems = pltpu.SemaphoreType.DMA((2, NFFN))
+    wide = pltpu.VMEM((rows, width), jnp.float32)
+    mids = pltpu.VMEM((2 * rows, units), jnp.bfloat16)
+    turned = pltpu.VMEM((width, 2 * rows), jnp.bfloat16)
+    moved = pltpu.VMEM(both, jnp.bfloat16)
     return pl.pallas_call(
-        scatter_kernel,
-        out_shape=(jax.ShapeDtypeStruct((rows, width), jnp.bfloat16),) * 2,
-        scratch_shapes=[pltpu.VMEM((2 * rows, width), jnp.bfloat16)],
-        compiler_params=params(48),
-        cost_estimate=cost(8 * rows * rows * width, 4e6),
-    )(small, grad, codes_row)
-
-
-def expert_kernel(
-    x_ref, d_ref, gate_ref, up_ref, down_ref, f_ref, back_ref, dots_ref, hid_ref, dg_ref, du_ref, f_sum, back_sum
-):
-    step = pl.program_id(0)
-    rows = x_ref.shape[0]
-    part = rows // 2
-    for r in range(2):
-        span = pl.ds(r * part, part)
-        x, d = x_ref[span, :], d_ref[span, :]
-        gate_pre = dot_nn(x, gate_ref[...])
-        up_pre = dot_nn(x, up_ref[...])
-        mid = dot_nt(d, down_ref[...])
-        sigmoid = 1.0 / (1.0 + jnp.exp(-gate_pre))
-        active = gate_pre * sigmoid
-        hid = (active * up_pre).astype(jnp.bfloat16)
-        du = (mid * active).astype(jnp.bfloat16)
-        dg = (mid * up_pre * (sigmoid + active * (1.0 - sigmoid))).astype(jnp.bfloat16)
-        hid_ref[span, :] = hid
-        du_ref[span, :] = du
-        dg_ref[span, :] = dg
-        f_term = dot_nn(hid, down_ref[...])
-        back_term = dot_nt(dg, gate_ref[...]) + dot_nt(du, up_ref[...])
-
-        @pl.when(step == 0)
-        def _():
-            f_sum[span, :] = f_term
-            back_sum[span, :] = back_term
-
-        @pl.when(step > 0)
-        def _():
-            f_sum[span, :] += f_term
-            back_sum[span, :] += back_term
-
-    @pl.when(step == pl.num_programs(0) - 1)
-    def _():
-        back_ref[...] = back_sum[...].astype(jnp.bfloat16)
-        f = f_sum[...].astype(jnp.bfloat16)
-        f_ref[...] = f
-        dots = jnp.sum(f.astype(jnp.float32) * d_ref[...].astype(jnp.float32), -1, keepdims=True)
-        dots_ref[...] = jnp.broadcast_to(dots, (rows, 128)).T[:8]
-
-
-def expert(x, d, gate, up, down):
-    rows, width = x.shape
-    units = gate.shape[1]
-    part = 512
-    whole = pl.BlockSpec((rows, width), lambda i: (0, 0))
-    columns = pl.BlockSpec((width, part), lambda i: (0, i))
-    mids = pl.BlockSpec((rows, part), lambda i: (0, i))
-    return pl.pallas_call(
-        expert_kernel,
-        grid=(units // part,),
-        in_specs=[whole, whole, columns, columns, pl.BlockSpec((part, width), lambda i: (i, 0))],
-        out_specs=(whole, whole, pl.BlockSpec((8, rows), lambda i: (0, 0)), mids, mids, mids),
+        expert_phase_kernel,
+        in_specs=[vmem] * 5 + [hbm] * 3,
+        out_specs=(vmem, vmem, vmem, hbm, hbm, hbm),
         out_shape=(
-            jax.ShapeDtypeStruct((rows, width), jnp.bfloat16),
-            jax.ShapeDtypeStruct((rows, width), jnp.bfloat16),
-            jax.ShapeDtypeStruct((8, rows), jnp.float32),
-        )
-        + (jax.ShapeDtypeStruct((rows, units), jnp.bfloat16),) * 3,
-        scratch_shapes=[pltpu.VMEM((rows, width), jnp.float32)] * 2,
-        compiler_params=params(52),
-        cost_estimate=cost(12 * rows * width * units, 3e7),
-    )(x, d, gate, up, down)
-
-
-def weights_kernel(
-    xa_ref, xb_ref, da_ref, db_ref, ha_ref, hb_ref, ga_ref, gb_ref, ua_ref, ub_ref,
-    gate_ref, up_ref, down_ref, x_turned, d_turned,
-):
-    rows = xa_ref.shape[0]
-
-    @pl.when(pl.program_id(0) == 0)
-    def _():
-        for i, (x, d) in enumerate(((xa_ref, da_ref), (xb_ref, db_ref))):
-            span = pl.ds(i * rows, rows)
-            x_turned[:, span] = x[...].astype(jnp.float32).T.astype(jnp.bfloat16)
-            d_turned[:, span] = d[...].astype(jnp.float32).T.astype(jnp.bfloat16)
-
-    both = lambda one, two: jnp.concatenate([one[...], two[...]], 0)
-    gate_ref[...] = dot_nn(x_turned[...], both(ga_ref, gb_ref)).astype(jnp.bfloat16)
-    up_ref[...] = dot_nn(x_turned[...], both(ua_ref, ub_ref)).astype(jnp.bfloat16)
-    down_ref[...] = dot_nn(d_turned[...], both(ha_ref, hb_ref)).T.astype(jnp.bfloat16)
-
-
-def weight_grads(xs, ds, hids, gates, ups):
-    rows, width = xs[0].shape
-    units = hids[0].shape[1]
-    part = 256
-    whole = pl.BlockSpec((rows, width), lambda i: (0, 0))
-    mids = pl.BlockSpec((rows, part), lambda i: (0, i))
-    columns = pl.BlockSpec((width, part), lambda i: (0, i))
-    return pl.pallas_call(
-        weights_kernel,
-        grid=(units // part,),
-        in_specs=[whole] * 4 + [mids] * 6,
-        out_specs=(columns, columns, pl.BlockSpec((part, width), lambda i: (i, 0))),
-        out_shape=(
-            jax.ShapeDtypeStruct((width, units), jnp.bfloat16),
-            jax.ShapeDtypeStruct((width, units), jnp.bfloat16),
-            jax.ShapeDtypeStruct((units, width), jnp.bfloat16),
+            jax.ShapeDtypeStruct(both, jnp.bfloat16),
+            jax.ShapeDtypeStruct(dots, jnp.float32),
+            jax.ShapeDtypeStruct(both, jnp.bfloat16),
+            jax.ShapeDtypeStruct(gate.shape, jnp.bfloat16),
+            jax.ShapeDtypeStruct(up.shape, jnp.bfloat16),
+            jax.ShapeDtypeStruct(down.shape, jnp.bfloat16),
         ),
-        scratch_shapes=[pltpu.VMEM((width, 2 * rows), jnp.bfloat16)] * 2,
-        compiler_params=params(52),
-        cost_estimate=cost(12 * rows * width * units, 3e7),
-    )(*xs, *ds, *hids, *gates, *ups)
+        scratch_shapes=[
+            pltpu.VMEM(gate.shape, jnp.bfloat16),
+            pltpu.VMEM(up.shape, jnp.bfloat16),
+            pltpu.VMEM(down.shape, jnp.bfloat16),
+            pltpu.VMEM((2 * rows, width), jnp.bfloat16),
+            moved, moved, moved, moved, moved,
+            pltpu.VMEM(dots, jnp.float32),
+            pltpu.VMEM(dots, jnp.float32),
+            wide, wide, mids, mids, mids, turned, turned,
+            pltpu.VMEM((2, 2, width, 256), jnp.bfloat16),
+            pltpu.VMEM((2, 256, width), jnp.bfloat16),
+            *(sems,) * 8,
+            pltpu.SemaphoreType.DMA((11,)),
+            pltpu.SemaphoreType.DMA((3, 2)),
+        ],
+        compiler_params=pltpu.CompilerParams(vmem_limit_bytes=63 * MIB, collective_id=2, has_side_effects=True),
+        cost_estimate=cost(36 * rows * width * units, 5e7),
+    )(*(part.reshape(NFFN, slots, width) for part in x_parts), small, grad, codes_row, gate, up, down)
 
 
 def split_dot(dot, left, right):
@@ -578,8 +637,8 @@
 
 def turn_kernel(
     resid_ref, small_ref, grad_ref, prior_ref, routes_ref, codes_ref, ra_ref, rb_ref, dots_ref, vector_ref,
-    gain_ref, mixer_ref, prior_turned_ref, out_weight_ref, a0_ref, a1_ref, a2_ref,
-    resid_grad_ref, g0_ref, g1_ref, g2_ref, out_grad_ref, prior_grad_ref, back_ref, sums_ref, prior_sums_ref, extra_ref,
+    gain_ref, mixer_ref, prior_turned_ref, out_weight_ref, attended_ref,
+    resid_grad_ref, grads_ref, out_grad_ref, prior_grad_ref, back_ref, sums_ref, prior_sums_ref, extra_ref, *, owners,
 ):
     rows, width = resid_ref.shape
     slots = 2 * ra_ref.shape[0]
@@ -655,28 +714,24 @@
 
     sums_ref[24:25, :] = jnp.sum(sums_ref[24:32, :], 0, keepdims=True)
     extra_ref[...] = jnp.concatenate([sums_ref[...], jnp.zeros((96, width), jnp.float32)], 0).T
-    owners = a0_ref.shape[0] // HEAD_DIM
     kept = NEXP // owners
     for z in range(owners):
         extra_ref[pl.ds(z * (width // owners), kept), :] += prior_sums_ref[z * kept : (z + 1) * kept, :]
-    out_grad_ref[:, width:] = extra_ref[...].astype(jnp.bfloat16)
+    out_grad_ref[:, width : width + 128] = extra_ref[...].astype(jnp.bfloat16)
+    out_grad_ref[:, width + 128 :] = jnp.zeros((width, 128), jnp.bfloat16)
     back = back_ref[...]
-    part = a0_ref.shape[0]
-    for j, (a_ref, g_ref) in enumerate(((a0_ref, g0_ref), (a1_ref, g1_ref), (a2_ref, g2_ref))):
-        span = pl.ds(j * part, part)
-        g_ref[...] = dot_nt(out_weight_ref[span, :], back).astype(jnp.bfloat16)
-        out_grad_ref[span, :width] = dot_nn(a_ref[...], back).astype(jnp.bfloat16)
+    grads_ref[...] = dot_nt(out_weight_ref[...], back).astype(jnp.bfloat16)
+    out_grad_ref[:, :width] = dot_nn(attended_ref[...], back).astype(jnp.bfloat16)
 
 
 def turn(resid, small, grad, prior, routes, codes, returned, dots, vector, gain, mixer_turned, prior_turned, out_weight, attended):
     rows, width = resid.shape
-    part = attended[0].shape[0]
     return pl.pallas_call(
-        turn_kernel,
+        functools.partial(turn_kernel, owners=lax.axis_size("expert")),
         out_shape=(
             jax.ShapeDtypeStruct((rows, width), jnp.float32),
-            *(jax.ShapeDtypeStruct((part, rows), jnp.bfloat16),) * 3,
-            jax.ShapeDtypeStruct((width, width + 128), jnp.bfloat16),
+            jax.ShapeDtypeStruct((width, rows), jnp.bfloat16),
+            jax.ShapeDtypeStruct((width, width + 256), jnp.bfloat16),
             jax.ShapeDtypeStruct(prior.shape, jnp.float32),
         ),
         scratch_shapes=[
@@ -687,7 +742,7 @@
         ],
         compiler_params=params(56),
         cost_estimate=cost(4 * rows * width * width + 4 * rows * rows * width, 1.5e7),
-    )(resid, small, grad, prior, routes, codes, *returned, dots, vector, gain, mixer_turned, prior_turned, out_weight, *attended)
+    )(resid, small, grad, prior, routes, codes, *returned, dots, vector, gain, mixer_turned, prior_turned, out_weight, attended)
 
 
 def combine_kernel(resid_ref, small_ref, routes_ref, codes_ref, fa_ref, fb_ref, vector_ref, gain_ref, out_ref):
@@ -727,70 +782,300 @@
     )(resid, small, routes, codes, *outs, vector, gain)
 
 
-def head_grads_kernel(tokens_ref, gain_ref, back_ref, out_ref, turned_ref):
+def attend_back_phase_kernel(
+    grads_ref, heads_ref, outs_ref, lse_ref, bias_ref, cos_ref, sin_ref, tokens_ref, gain_ref,
+    query_ref, key_ref, value_ref, resid_grad_ref, out_part_ref, f_ref, gate_ref, up_ref, down_ref,
+    tokens_grad_ref, f_got, gate_got, up_got, down_got, *rest, reduce,
+):
+    if reduce:
+        total_ref, *rest = rest
+    else:
+        parts_ref, *rest = rest
+    (
+        d_got, back_sent, back_got, normed_turned, turned_ref, back_sum,
+        qt_ref, kt_ref, dt_ref, q_ref, k_ref, v_ref, d_ref, delta_ref, dq_ref, dk_ref, dv_ref, triangle,
+        d_send, d_recv, back_send, back_recv, weight_send, weight_recv, f_send, f_recv, local_sem, *rest,
+    ) = rest
+    if reduce:
+        (
+            parts_ref, half_got, half_sum, chip_got, chip_sum, ring_got, ring_sum, all_got,
+            half_send, half_recv, chip_send, chip_recv, ring_send, ring_recv, all_send, all_recv,
+        ) = rest
+    chunks, owners, _, rows = grads_ref.shape
+    width = tokens_ref.shape[1]
+    copies = gate_ref.shape[0]
+    member, xy, core = (lax.axis_index(name) for name in ("expert", "xy", "core"))
+    place = xy * 2 + core
+    ring, others, planes = ring_partners(owners), copy_partners(copies), plane_partners(owners)
+    greet([item[2] for item in planes], [item[2] for item in others])
+
+    d_groups = []
+    for j in range(chunks):
+        local = pltpu.make_async_copy(grads_ref.at[j, member], d_got.at[j, member], local_sem.at[j])
+        local.start()
+        group = []
+        for step, index, device in ring:
+            copy = remote(
+                grads_ref.at[j, index], d_got.at[j, member], d_send.at[j, step - 1], d_recv.at[j, step - 1], device
+            )
+            copy.start()
+            group.append(copy)
+        d_groups.append((local, group))
+
     inputs = tokens_ref[...].astype(jnp.float32)
     inverse = lax.rsqrt(jnp.mean(inputs * inputs, -1, keepdims=True) + epsilon)
-    normed = (inputs * inverse * gain_ref[...]).T.astype(jnp.bfloat16)
-    owners = back_ref.shape[0]
-    for i in range(3):
-        for z in range(owners):
-            row = (i * owners + z) * HEAD_DIM
-            turned_ref[row : row + HEAD_DIM, :] = back_ref[z, i * HEAD_DIM : (i + 1) * HEAD_DIM]
-    out_ref[...] = dot_nt(normed, turned_ref[...]).astype(jnp.bfloat16)
-
-
-def head_grads(tokens, gain, back):
-    rows, width = tokens.shape
-    columns = back.shape[0] * back.shape[1]
-    return pl.pallas_call(
-        head_grads_kernel,
-        out_shape=jax.ShapeDtypeStruct((width, columns), jnp.bfloat16),
-        scratch_shapes=[pltpu.VMEM((columns, rows), jnp.bfloat16)],
-        compiler_params=params(48),
-        cost_estimate=cost(2 * rows * width * columns, 4e6),
-    )(tokens, gain, back)
-
-
-def last_kernel(
-    tokens_ref, gain_ref, b0_ref, b1_ref, b2_ref, query_ref, key_ref, value_ref, resid_grad_ref,
-    tokens_grad_ref, gain_grad_ref, back_turned,
-):
-    rows, width = tokens_ref.shape
-    inputs = tokens_ref[...].astype(jnp.float32)
-    inverse = lax.rsqrt(jnp.mean(inputs * inputs, -1, keepdims=True) + epsilon)
+    normed_turned[...] = (inputs * inverse * gain_ref[...]).T.astype(jnp.bfloat16)
+    share = width // owners
+    part_shape = (owners, share // 48, 48)
+
+    def fill(p, values, begin, size):
+        if reduce:
+            parts_ref[p, :, :, :, begin : begin + size] = values.reshape(*part_shape, size)
+        else:
+            parts_ref[p, :, begin : begin + size] = values
+
+    fill(0, out_part_ref[...], 0, out_part_ref.shape[1])
+    columns_total = out_part_ref.shape[1]
+    for p in range(1, chunks + 1):
+        fill(p, jnp.zeros((width, columns_total - width), jnp.bfloat16), width, columns_total - width)
+
+    stages = {}
+
+    def over_cores(p):
+        half = columns_total // 2
+        away = pl.ds(pl.multiple_of((1 - core) * half, half), half)
+        copy = remote(
+            parts_ref.at[p, :, :, :, away], half_got.at[p], half_send.at[p], half_recv.at[p], {"core": 1 - core}
+        )
+        copy.start()
+        stages[p, 0] = [copy]
+
+    def over_chips(p):
+        for copy in stages[p, 0]:
+            copy.wait_recv()
+        half = columns_total // 2
+        mine = pl.ds(pl.multiple_of(core * half, half), half)
+        half_sum[p] = (
+            parts_ref[p, :, :, :, mine].astype(jnp.float32) + half_got[p].astype(jnp.float32)
+        ).astype(jnp.bfloat16)
+        stages[p, 1] = []
+        for step in (3, 1, 2):
+            index = lax.rem(xy + step, 4)
+            copy = remote(
+                half_sum.at[p, :, index], chip_got.at[p, xy], chip_send.at[p, step - 1], chip_recv.at[p, step - 1],
+                {"xy": index},
+            )
+            copy.start()
+            stages[p, 1].append(copy)
+        chip_got[p, xy] = half_sum[p, :, xy]
+
+    def over_owners(p):
+        for copy in stages[p, 1]:
+            copy.wait_recv()
+        chip_sum[p] = jnp.sum(chip_got[p].astype(jnp.float32), 0).astype(jnp.bfloat16)
+        stages[p, 2] = []
+        for step, index, device in ring:
+            copy = remote(
+                chip_sum.at[p, index], ring_got.at[p, member], ring_send.at[p, step - 1], ring_recv.at[p, step - 1],
+                device,
+            )
+            copy.start()
+            stages[p, 2].append(copy)
+        ring_got[p, member] = chip_sum[p, member]
+
+    def to_copies(p):
+        for copy in stages[p, 2]:
+            copy.wait_recv()
+        half = columns_total // 2
+        mine = pl.ds(pl.multiple_of(core * half, half), half)
+        ring_sum[p] = jnp.sum(ring_got[p].astype(jnp.float32), 0).astype(jnp.bfloat16)
+        stages[p, 3] = []
+        for step, _, device in others:
+            copy = remote(
+                ring_sum.at[p], all_got.at[p, xy, :, mine], all_send.at[p, step - 1], all_recv.at[p, step - 1], device
+            )
+            copy.start()
+            stages[p, 3].append(copy)
+        all_got[p, xy, :, mine] = ring_sum[p]
+
+    def advance(*pairs):
+        if reduce:
+            for stage, p in pairs:
+                (over_cores, over_chips, over_owners, to_copies)[stage](p)
+
+    advance((0, 0))
+
+    background = []
+    for i, (source, target) in enumerate(((gate_ref, gate_got), (up_ref, up_got), (down_ref, down_got))):
+        local = pltpu.make_async_copy(source.at[place], target.at[place], weight_send.at[i, 0])
+        local.start()
+        background.append((local, None))
+        for step, index, device in others:
+            copy = remote(
+                source.at[2 * device["xy"] + device["core"]], target.at[place],
+                weight_send.at[i, step], weight_recv.at[i, step], device,
+            )
+            copy.start()
+            background.append((None, copy))
+
+    def head(j):
+        local, group = d_groups[j]
+        local.wait()
+        for copy in group:
+            copy.wait_recv()
+        attend_back_head(
+            bias_ref, cos_ref, sin_ref, heads_ref.at[j], outs_ref.at[j], lse_ref.at[j : j + 1], d_got.at[j],
+            back_sent.at[j], qt_ref, kt_ref, dt_ref, q_ref, k_ref, v_ref, d_ref, delta_ref, dq_ref, dk_ref, dv_ref,
+            triangle,
+        )
+        local = pltpu.make_async_copy(back_sent.at[j, member], back_got.at[j, member], local_sem.at[chunks + j])
+        local.start()
+        group = []
+        for step, index, device in ring:
+            copy = remote(
+                back_sent.at[j, index], back_got.at[j, member],
+                back_send.at[j, step - 1], back_recv.at[j, step - 1], device,
+            )
+            copy.start()
+            group.append(copy)
+        return local, group
+
+    span_width = owners * HEAD_DIM
+
+    def weights_of(j, group):
+        local, copies_in = group
+        local.wait()
+        for copy in copies_in:
+            copy.wait_recv()
+        for i in range(3):
+            for z in range(owners):
+                row = i * span_width + z * HEAD_DIM
+                turned_ref[row : row + HEAD_DIM, :] = back_got[j, z, i * HEAD_DIM : (i + 1) * HEAD_DIM]
+        total = None
+        for i, weight in enumerate((query_ref, key_ref, value_ref)):
+            term = dot_nn(weight[:, j * span_width : (j + 1) * span_width], turned_ref[i * span_width : (i + 1) * span_width, :])
+            total = term if total is None else total + term
+        back_sum[...] = total if j == 0 else back_sum[...] + total
+        fill(j + 1, dot_nt(normed_turned[...], turned_ref[...]).astype(jnp.bfloat16), 0, 3 * span_width)
+
+    groups = [head(0)]
+    advance((1, 0))
+    groups.append(head(1))
+    weights_of(0, groups[0])
+    advance((2, 0), (0, 1))
+    groups.append(head(2))
+    for half in range(2):
+        expert = member * 2 + core
+        local = pltpu.make_async_copy(f_ref.at[half, expert], f_got.at[half, expert], f_send.at[half, 0])
+        local.start()
+        background.append((local, None))
+        for step, index, device in planes:
+            copy = remote(
+                f_ref.at[half, index], f_got.at[half, expert], f_send.at[half, step], f_recv.at[half, step], device
+            )
+            copy.start()
+            background.append((None, copy))
+    advance((3, 0), (1, 1))
+    weights_of(1, groups[1])
+    advance((0, 2), (2, 1), (1, 2))
+    weights_of(2, groups[2])
     normed = inputs * inverse
-    owners = b0_ref.shape[0]
-    for i in range(3):
-        for j, ref in enumerate((b0_ref, b1_ref, b2_ref)):
-            for z in range(owners):
-                head = j * owners + z
-                back_turned[i, head * HEAD_DIM : (head + 1) * HEAD_DIM, :] = ref[z, i * HEAD_DIM : (i + 1) * HEAD_DIM]
-    total = None
-    for i, ref in enumerate((query_ref, key_ref, value_ref)):
-        term = dot_nn(ref[...], back_turned[i])
-        total = term if total is None else total + term
-    first_grads = total.T
+    first_grads = back_sum[...].T
     summed = jnp.sum((first_grads * normed).reshape(rows // 8, 8, width), 0)
     column = jnp.sum(summed.T, -1, keepdims=True)
-    gain_grad_ref[...] = jnp.broadcast_to(column, (width, 128)).astype(jnp.bfloat16)
+    fill(chunks, jnp.broadcast_to(column, (width, 128)).astype(jnp.bfloat16), width, 128)
+    advance((0, 3), (3, 1), (2, 2))
     scaled = first_grads * gain_ref[...]
     tokens_grad_ref[...] = (
         inverse * (scaled - normed * jnp.mean(scaled * normed, -1, keepdims=True)) + resid_grad_ref[...]
     )
-
-
-def last(tokens, gain, backs, weights, resid_grads):
-    rows, width = tokens.shape
-    return pl.pallas_call(
-        last_kernel,
+    advance((1, 3), (3, 2), (2, 3), (3, 3))
+    if reduce:
+        for p in range(chunks + 1):
+            for copy in stages[p, 3]:
+                copy.wait_recv()
+            total_ref[p] = all_got[p].astype(jnp.float32).reshape(share, columns_total)
+            for stage in range(4):
+                for copy in stages[p, stage]:
+                    copy.wait_send()
+    for local, group in d_groups + groups:
+        for copy in group:
+            copy.wait_send()
+    for local, copy in background:
+        if copy is None:
+            local.wait()
+        else:
+            copy.wait()
+
+
+def attend_back_phase(
+    grads, heads, outs, lse, bias, cosine, sine, tokens, gain, weights, resid_grads, out_part, fs, expert_grads, copies
+):
+    chunks, owners, _, rows = grads.shape
+    width = tokens.shape[1]
+    length = owners * rows
+    head = (chunks, owners, 3 * HEAD_DIM, rows)
+    columns = out_part.shape[1]
+    share = width // owners
+    total = chunks + 1
+    reduce = copies == 8 and share == 4 * 48
+    vmem, hbm = pl.BlockSpec(memory_space=pltpu.VMEM), pl.BlockSpec(memory_space=pl.ANY)
+    pieces = [item.reshape(copies, -1, item.shape[-1]) for item in expert_grads]
+    turned = pltpu.VMEM((HEAD_DIM, length), jnp.bfloat16)
+    plain = pltpu.VMEM((length, HEAD_DIM), jnp.bfloat16)
+    wide = pltpu.VMEM((length, HEAD_DIM), jnp.float32)
+    sems = lambda *shape: pltpu.SemaphoreType.DMA(shape)
+    scratch = [
+        pltpu.VMEM(grads.shape, jnp.bfloat16),
+        pltpu.VMEM(head, jnp.bfloat16),
+        pltpu.VMEM(head, jnp.bfloat16),
+        pltpu.VMEM((width, rows), jnp.bfloat16),
+        pltpu.VMEM((3 * owners * HEAD_DIM, rows), jnp.bfloat16),
+        pltpu.VMEM((width, rows), jnp.float32),
+        turned, turned, turned, plain, plain, plain, plain,
+        pltpu.VMEM((1, length), jnp.float32),
+        pltpu.VMEM((HEAD_DIM, length), jnp.float32),
+        wide, wide,
+        pltpu.VMEM((TILE, TILE), jnp.float32),
+        *(sems(chunks, owners - 1),) * 4,
+        sems(3, copies), sems(3, copies), sems(2, 2 * owners), sems(2, 2 * owners), sems(2 * chunks),
+    ]
+    if reduce:
+        half = columns // 2
+        low = lambda *shape: pltpu.VMEM(shape, jnp.bfloat16)
+        scratch += [
+            low(total, owners, 4, 48, columns),
+            low(total, owners, 4, 48, half),
+            low(total, owners, 4, 48, half),
+            low(total, 4, owners, 48, half),
+            low(total, owners, 48, half),
+            low(total, owners, 48, half),
+            low(total, 48, half),
+            low(total, 4, 48, columns),
+            sems(total), sems(total), sems(total, 3), sems(total, 3),
+            sems(total, owners - 1), sems(total, owners - 1), sems(total, copies - 1), sems(total, copies - 1),
+        ]
+        last_spec, last_shape = vmem, jax.ShapeDtypeStruct((total, share, columns), jnp.float32)
+    else:
+        last_spec, last_shape = vmem, jax.ShapeDtypeStruct((total, width, columns), jnp.bfloat16)
+    *result, totals = pl.pallas_call(
+        functools.partial(attend_back_phase_kernel, reduce=reduce),
+        in_specs=[vmem] * 14 + [hbm] * 4,
+        out_specs=(vmem, hbm, hbm, hbm, hbm, last_spec),
         out_shape=(
             jax.ShapeDtypeStruct((rows, width), jnp.float32),
-            jax.ShapeDtypeStruct((width, 128), jnp.bfloat16),
+            jax.ShapeDtypeStruct(fs.shape, fs.dtype),
+            *(jax.ShapeDtypeStruct(piece.shape, piece.dtype) for piece in pieces),
+            last_shape,
         ),
-        scratch_shapes=[pltpu.VMEM((3, width, rows), jnp.bfloat16)],
-        compiler_params=params(56),
-        cost_estimate=cost(6 * rows * width * width, 2e7),
-    )(tokens, gain, *backs, *weights, resid_grads)
+        scratch_shapes=scratch,
+        compiler_params=pltpu.CompilerParams(vmem_limit_bytes=63 * MIB, collective_id=3, has_side_effects=True),
+        cost_estimate=cost(2e10, 5e7),
+    )(grads, heads, outs, lse, bias, cosine, sine, tokens, gain, *weights, resid_grads, out_part, fs, *pieces)
+    if not reduce:
+        totals = lax.psum_scatter(totals, "expert", scatter_dimension=1, tiled=True)
+        totals = lax.psum(totals, ("xy", "core")).astype(jnp.float32)
+    return (*result, totals)
 
 
 def lineage_of(parent_row):
@@ -832,28 +1117,9 @@
     length = rows * owners
     chunks = width // HEAD_DIM // owners
     half_slots = rows // 8
-    planes, everyone = ("expert", "core"), ("expert", "xy", "core")
-
-    def swap(values):
-        return lax.ppermute(values, "core", [(0, 1), (1, 0)])
-
-    def exchange(values, axes):
-        return lax.all_to_all(values, axes, split_axis=0, concat_axis=0, tiled=True)
-
-    def gather_weight(weight):
-        mine = jnp.where(core == 0, weight[0], weight[1])
-        other = swap(jnp.where(core == 0, weight[1], weight[0]))
-        pair = jnp.concatenate([jnp.where(core == 0, mine, other), jnp.where(core == 0, other, mine)], 0)
-        return lax.all_gather(pair, "xy", axis=0, tiled=True)
-
-    def scatter_weight(grads):
-        part = lax.psum_scatter(grads, "xy", scatter_dimension=0, tiled=True)
-        part = part.reshape(2, part.shape[0] // 2, part.shape[1])
-        mine = jnp.where(core == 0, part[0], part[1])
-        other = swap(jnp.where(core == 0, part[1], part[0]))
-        return jnp.stack(
-            [jnp.where(core == 0, mine, other), jnp.where(core == 0, other, mine)], 0
-        ).astype(jnp.float32)
+
+    def own_sum(got):
+        return jnp.sum(got.reshape(copies // 2, 2, *got.shape[1:]).astype(jnp.float32), 0)
 
     lineage = lineage_of(parents[0])
     segments = lineage.shape[0]
@@ -877,7 +1143,7 @@
     attended, logs, heads, outs, gate, up, down = attend_phase(
         tokens, attention_row, qkv_weights, own_cosine, own_sine, bias, (gate_weight, up_weight, down_weight), copies
     )
-    attended = [attended[j].reshape(owners * HEAD_DIM, rows) for j in range(chunks)]
+    attended = attended.reshape(width, rows)
     gate, up, down = (full.reshape(-1, full.shape[-1]) for full in (gate, up, down))
     codes = slot_codes(routes, half_slots)
     codes_row = codes.T
@@ -890,69 +1156,32 @@
     resid, small, *x_out = middle(
         tokens, attended, out_weight, expert_row, mixer, prior, prior_wide, routes, codes_row
     )
-    d_out = scatter(small, grad, codes_row)
-
-    def to_experts(values):
-        return exchange(values.reshape(NFFN, half_slots, -1), planes).reshape(values.shape)
-
-    xs, ds, fs, backs, dots, hids, gates, ups = ([] for _ in range(8))
-    for x_part, d_part in zip(x_out, d_out):
-        x, d = to_experts(x_part), to_experts(d_part)
-        f, back, dot, hid, dg, du = expert(x, d, gate, up, down)
-        backs.append(to_experts(back))
-        dots.append(exchange(dot[0].reshape(NFFN, half_slots), planes).reshape(1, rows))
-        for kept, item in zip((xs, ds, fs, hids, gates, ups), (x, d, f, hid, dg, du)):
-            kept.append(item)
-    *backs, grads_gate, grads_up, grads_down = lax.optimization_barrier(
-        (*backs, *weight_grads(xs, ds, hids, gates, ups))
-    )
-    gate_part, up_part, down_part = (scatter_weight(grads) for grads in (grads_gate, grads_up, grads_down))
-
+    backs, dots, fs, grads_gate, grads_up, grads_down = expert_phase(x_out, small, grad, codes_row, gate, up, down)
+    dots = dots[:, :, 0, :half_slots].reshape(1, 2 * rows)
+    backs = backs.reshape(2, rows, width)
     vector = jnp.concatenate([constant_vector, jnp.zeros((6, width), jnp.float32)], 0)
-    resid_grads, *grads_out, out_grad, prior_grad = turn(
-        resid, small, grad, prior, routes, codes, backs, jnp.concatenate(dots, 1), vector, expert_row,
+    resid_grads, grads_out, out_part, prior_grad = turn(
+        resid, small, grad, prior, routes, codes, backs, dots, vector, expert_row,
         mixer.T, prior_turned, out_weight, attended,
     )
-    fs[0], grads_out[0] = lax.optimization_barrier((fs[0], grads_out[0]))
-
-    def over_copies(partial):
-        return lax.psum_scatter(partial, ("xy", "core"), scatter_dimension=1, tiled=True)
-
-    out_grad, gate_part = lax.optimization_barrier((out_grad, gate_part))
-    own_backs, parts = [], [over_copies(out_grad)]
-    for j in range(chunks):
-        grads_in = exchange(grads_out[j].reshape(owners, HEAD_DIM, rows), "expert")
-        back = exchange(attend_back(bias, cosine, sine, heads[j], outs[j], logs[j : j + 1], grads_in), "expert")
-        own_backs.append(back)
-        parts.append(over_copies(head_grads(tokens, attention_row, back)))
-    fs[1], own_backs[0] = lax.optimization_barrier((fs[1], own_backs[0]))
-    result = combine(resid, small, routes, codes, [to_experts(f) for f in fs], vector, expert_row)
-    tokens_grad, gain_grads = last(tokens, attention_row, own_backs, qkv_weights, resid_grads)
-    parts.append(over_copies(gain_grads))
-    sizes = [part.shape[1] for part in parts]
-    share = width // owners
-    joined = jnp.concatenate(parts, 1)
-    joined = exchange(joined.reshape(owners, share, joined.shape[1]), "expert")
-    joined = jnp.sum(joined.astype(jnp.float32), 0).astype(jnp.bfloat16)
-    joined = lax.all_gather(joined, ("xy", "core"), axis=0, tiled=False)
-    totals, begin = [], 0
-    for size in sizes:
-        part = joined[:, :, begin : begin + size].transpose(1, 0, 2).reshape(share, -1)
-        totals.append(part.astype(jnp.float32))
-        begin += size
-    out_total, *head_totals, gain_total = totals
+    tokens_grad, fs, gate_got, up_got, down_got, totals = attend_back_phase(
+        grads_out.reshape(chunks, owners, HEAD_DIM, rows), heads, outs, logs, bias, cosine, sine, tokens,
+        attention_row, qkv_weights, resid_grads, out_part, fs, (grads_gate, grads_up, grads_down), copies,
+    )
+    result = combine(resid, small, routes, codes, fs.reshape(2, rows, width), vector, expert_row)
+    gate_part, up_part, down_part = (own_sum(got) for got in (gate_got, up_got, down_got))
     span = owners * HEAD_DIM
     qkv_totals = [
-        jnp.concatenate([part[:, i * span : (i + 1) * span] for part in head_totals], 1) for i in range(3)
+        jnp.concatenate([part[:, i * span : (i + 1) * span] for part in totals[1:]], 1) for i in range(3)
     ]
-    small_total = out_total[:, width:]
+    small_total = totals[0, :, width:]
     return (
         result[None],
         tokens_grad[None],
         prior_grad[None],
         *qkv_totals,
-        out_total[:, :width],
-        gain_total[:, 0],
+        totals[0, :, :width],
+        totals[chunks, :, width],
         small_total[:, 24],
         small_total[:, :NEXP],
         small_total[: NEXP // owners, 32 : 32 + NEXP],

time: 860 us -> 564 us (0.66)
  waiting for transfers between devices: 320 us -> 0 us
  Pallas kernels: 268 us -> 517 us
  blocking collectives: 117 us -> 0 us
  starting transfers between devices: 56 us -> 0 us
  local copies, waits for them, and re-layouts: 55.2 us -> 28.6 us
  between operations: 15.1 us -> 1.63 us
  other arithmetic: 21.8 us -> 11.7 us
    pallas_call x12 -> x3, Pallas kernels: 138 us -> 388 us  [the longest x1 233 us: attend_back_phase(): pl.pallas_call(functools.partial(attend_back_phase_kernel, reduce=reduce)...]
    unnamed x14 -> x0, waiting for transfers between devices: 172 us -> none
    all_to_all x5 -> x0, blocking collectives: 117 us -> none  [exchange(): return lax.all_to_all(values, axes, split_axis=0, concat_axis=0, tiled=True)]
    all_to_all x12 -> x0, waiting for transfers between devices: 93 us -> none  [exchange(): return lax.all_to_all(values, axes, split_axis=0, concat_axis=0, tiled=True)]
    all_to_all x12 -> x0, starting transfers between devices: 52.3 us -> none  [exchange(): return lax.all_to_all(values, axes, split_axis=0, concat_axis=0, tiled=True)]
    reduce_scatter x3 -> x0, waiting for transfers between devices: 30.2 us -> none  [scatter_weight(): part = lax.psum_scatter(grads, 'xy', scatter_dimension=0, tiled=True)]
    all_gather x1 -> x0, waiting for transfers between devices: 24.1 us -> none  [per_device(): joined = lax.all_gather(joined, ('xy', 'core'), axis=0, tiled=False)]
    unnamed x141 -> x62, local copies, waits for them, and re-layouts: 30.5 us -> 11.9 us
  transfers between devices with their start and end apart: 24 -> 0, of which waited for: 17 -> 0; matrix products, arithmetic and copies ran while one was open for 4% -> 0% of each run, Pallas kernels for 15% -> 0%
where the time goes in v3:
time: 564 us; the launch traced here: 559 us
  Pallas kernels  517 us (92%)
  local copies, waits for them, and re-layouts  28.6 us (5%)
  other arithmetic  11.7 us (2%)
    pallas_call x1, Pallas kernels, attend_back_phase(): pl.pallas_call(functools.partial(attend_back_phase_kernel, reduce=reduce)...  233 us
    pallas_call x1, Pallas kernels, expert_phase(): pl.pallas_call(expert_phase_kernel, in_specs=[vmem] * 5 + [hbm] * 3, out_...  137 us
    pallas_call x1, Pallas kernels, attend_phase(): pl.pallas_call(attend_phase_kernel, in_specs=[vmem] * 8 + [hbm] * 3, out_...  114 us
    pallas_call x1, Pallas kernels, turn(): pl.pallas_call(functools.partial(turn_kernel, owners=lax.axis_size('exper...  18.6 us
    unnamed x62, local copies, waits for them, and re-layouts  11.9 us

profile of v3, /device:TPU:1, one launch (start us, length us, event | category | flops | bytes accessed | tf_op | source)
XLA Modules:
  0.0 559.4 jit_solution(9584899023087666720)
XLA Ops:
  2.7 1.3 broadcast_in_dim.104.gain_ref
  5.6 1.3 concatenate.24.vector_ref
  8.6 0.9 copy.76
  12.0 1.2 multiply_sine_fusion
  14.0 114.3 %shard_map.297 = (bf16[3,4,64,640]{3,2,1,0:T(8,128)(2,1)}, f32[8,2560]{1,0:T(8,128)}, bf16[3,4,192,640]{3,2,1,0:T(8,128)(2,1)}, bf16[3,4,64,640]{3,2,1,0:T(8,128...) custom-call(bf16[640,768]{1,0:T(8,128)(2,1)} %bitcast.56, ...), custom_call_target="tpu_custom_call" | custom-call | flops 10000000000 | bytes 50000000 | tf_op jit(solution)/shard_map/pallas_call | solution.py:328
  128.4 1.2 copy-done.10
  129.6 9.4 %shard_map.298 = (f32[640,768]{1,0:T(8,128)}, f32[640,128]{1,0:T(8,128)S(1)}, bf16[640,768]{1,0:T(8,128)(2,1)S(1)}, bf16[640,768]{1,0:T(8,128)(2,1)S(1)}) custom-call(bf16[640,768]{1,0:T(8,128)(2,1)S(1)} %bitcast.58, bf16[768,640]{1,0:T(8,128)(2,1)S(1)} %bitcast.60, bf16[768,768]{1,0:T(8,128)(2,1)} %out_weight_ref.3, ...), custom_call_target="tpu_custom_call" | custom-call | flops 2768240640 | bytes 10000000 | tf_op jit(solution)/shard_map/pallas_call | solution.py:407
  139.0 0.9 copy-done.11
  139.9 0.9 copy-done.12
  141.6 136.9 %shard_map.299 = (bf16[2,8,80,768]{3,2,1,0:T(8,128)(2,1)}, f32[2,8,8,128]{3,2,1,0:T(8,128)}, bf16[2,8,80,768]{3,2,1,0:T(8,128)(2,1)}, bf16[768,2048]{1,0:T(8,128...) custom-call(bf16[8,80,768]{2,1,0:T(8,128)(2,1)} %bitcast.61, bf16[8,80,768]{2,1,0:T(8,128)(2,1)} %bitcast.62, ...), custom_call_target="tpu_custom_call" | custom-call | flops 36238786560 | bytes 50000000 | tf_op jit(solution)/shard_map/pallas_call | solution.py:600
  278.4 2.9 fusion.16
  281.3 0.9 slice_reduce_fusion.2
  282.9 18.6 %shard_map.300 = (f32[640,768]{1,0:T(8,128)}, bf16[768,640]{1,0:T(8,128)(2,1)}, bf16[768,1024]{1,0:T(8,128)(2,1)}, f32[640,12]{1,0:T(8,128)}) custom-call(f32[640,768]{1,0:T(8,128)} %get-tuple-element.44.resid_ref, f32[640,128]{1,0:T(8,128)} %copy-done.14, bf16[640,768]{1,0:T(8,128)(2,1)} %bitcast.72, f32[640,12]{1,0:T(8,128)} %bitcast.55, ...), custom_call_target="tpu_custom_call" | custom-call | flops 2768240640 | bytes 15000000 | tf_op jit(solution)/shard_map/pallas_call | solution.py:729
  301.5 232.6 %shard_map.301 = (f32[640,768]{1,0:T(8,128)}, bf16[2,8,80,768]{3,2,1,0:T(8,128)(2,1)}, bf16[8,96,2048]{2,1,0:T(8,128)(2,1)}, bf16[8,96,2048]{2,1,0:T(8,128)(2,1)...) custom-call(bf16[3,4,64,640]{3,2,1,0:T(8,128)(2,1)} %bitcast.81, ...), custom_call_target="tpu_custom_call" | custom-call | flops 20000000000 | bytes 50000000 | tf_op jit(solution)/shard_map/pallas_call | solution.py:1061
  534.2 1.8 fusion.15
  536.5 5.5 shard_map.302
  547.1 0.9 slice_bitcast_fusion.3
  548.4 0.9 pad_maximum_fusion.2
  549.2 0.9 pad_maximum_fusion.1
  550.1 0.9 pad_maximum_fusion
  550.9 1.7 convert_reduce_fusion.2
  553.4 1.7 convert_reduce_fusion.1
  555.8 1.6 convert_reduce_fusion
  557.6 1.3 copy.91
  (105 shorter events, 17.5 us)
Async XLA Ops:
  2.7 125.6 %copy-start.7 = (f32[1,768]{1,0:T(1,128)}, f32[1,768]{1,0:T(1,128)S(1)}, u32[]{:S(2)}) copy-start(f32[1,768]{1,0:T(1,128)S(1)} %broadcast_in_dim.114.gain_ref) | copy-start | bytes 9220
  9.5 118.9 %copy-start = (s32[1,640,2]{2,1,0:T(8,128)}, s32[1,640,2]{2,1,0:T(8,128)S(1)}, u32[]{:S(2)}) copy-start(s32[1,640,2]{2,1,0:T(8,128)S(1)} %copy.76) | copy-start | bytes 15364
  9.6 1.1 copy-start.24
  9.7 1.3 copy-start.25
  9.7 1.3 copy-start.26
  10.6 117.7 %copy-start.2 = (s32[640,2]{1,0:T(8,128)}, s32[640,2]{1,0:T(8,128)S(1)}, u32[]{:S(2)}) copy-start(s32[640,2]{1,0:T(8,128)S(1)} %compare_select_fusion.codes_ref) | copy-start | bytes 15364
  10.8 117.6 %copy-start.6 = (s32[2,640]{1,0:T(2,128)}, s32[2,640]{1,0:T(2,128)S(1)}, u32[]{:S(2)}) copy-start(s32[2,640]{1,0:T(2,128)S(1)} %copy.83.codes_ref) | copy-start | bytes 15364
  11.0 117.4 %copy-start.4 = (f32[1,640,12]{2,1,0:T(8,128)}, f32[1,640,12]{2,1,0:T(8,128)S(1)}, u32[]{:S(2)}) copy-start(f32[1,640,12]{2,1,0:T(8,128)S(1)} %copy.75) | copy-start | bytes 92164
  13.2 115.1 %copy-start.21 = (f32[32,2560]{1,0:T(8,128)}, f32[32,2560]{1,0:T(8,128)S(1)}, u32[]{:S(2)}) copy-start(f32[32,2560]{1,0:T(8,128)S(1)} %get-tuple-element.152.sin_ref) | copy-start | bytes 983044
  13.2 115.1 %copy-start.22 = (f32[32,2560]{1,0:T(8,128)}, f32[32,2560]{1,0:T(8,128)S(1)}, u32[]{:S(2)}) copy-start(f32[32,2560]{1,0:T(8,128)S(1)} %get-tuple-element.153.cos_ref) | copy-start | bytes 983044
  14.0 114.4 %copy-start.9 = (bf16[1,640,768]{2,1,0:T(8,128)(2,1)S(1)}, bf16[1,640,768]{2,1,0:T(8,128)(2,1)}, u32[]{:S(2)}) copy-start(bf16[1,640,768]{2,1,0:T(8,128)(2,1)} %param.18) | copy-start | bytes 2949124
  128.4 1.2 copy-start.10
  534.1 1.9 copy-start.1
  534.1 1.9 copy-start.3
  534.1 1.8 copy-start.5
  534.1 1.8 copy-start.8
  534.2 2.3 copy-start.13
  534.2 2.3 copy-start.15
  536.5 5.5 copy-start.16
  536.5 6.2 %copy-start.23 = (f32[640,12]{1,0:T(8,128)S(1)}, f32[640,12]{1,0:T(8,128)}, u32[]{:S(2)}) copy-start(f32[640,12]{1,0:T(8,128)} %get-tuple-element.65) | copy-start | bytes 92164
  548.4 2.6 copy-start.19
  550.9 2.5 copy-start.18
  553.4 2.5 copy-start.17
  555.8 1.8 copy-start.20
  (3 other events, 2.6 us)

commit v4 on v3

--- a/solution.py
+++ b/solution.py
@@ -208,6 +208,20 @@
     return result
 
 
+def plane_chips(xy):
+    return xy + 1 - 2 * lax.rem(xy, 2), lax.rem(xy + 2, 4), 3 - xy
+
+
+def first_hops(beside, behind, across):
+    return (
+        (across * 2, 2, beside), (across * 2 + 1, 3, behind), (beside * 2, 0, beside), (behind * 2 + 1, 1, behind),
+    )
+
+
+def relayed(copies):
+    return copies == 8
+
+
 def remote(source, target, send, receive, device):
     return pltpu.make_async_remote_copy(
         src_ref=source, dst_ref=target, send_sem=send, recv_sem=receive,
@@ -215,9 +229,61 @@
     )
 
 
+def reach_of(parents):
+    shape = (128, 128)
+    one, two = lax.broadcasted_iota(jnp.int32, shape, 0), lax.broadcasted_iota(jnp.int32, shape, 1)
+    count = parents.shape[1]
+    none = lambda size: jnp.full((1, size), -1, jnp.int32)
+    parent_row = jnp.concatenate([none(1), parents, none(127 - count)], 1)
+    reach = jnp.where((one == two) | (one == parent_row), 1.0, 0.0).astype(jnp.bfloat16)
+    for _ in range(3):
+        reach = jnp.minimum(dot_nn(reach, reach), 1.0).astype(jnp.bfloat16)
+    return reach
+
+
+def place_tables(reach, first, size):
+    ids = lax.broadcasted_iota(jnp.int32, (1, size), 1) + first
+    later = ids - TRUNK
+    segment = jnp.where(later < 0, 0, 1 + lax.shift_right_arithmetic(later, 7))
+    inside = jnp.where(later < 0, later, (later & (SEG - 1)) - SEG)
+    own = jnp.where(segment == lax.broadcasted_iota(jnp.int32, (128, size), 0), 1.0, 0.0).astype(jnp.bfloat16)
+    seen = dot_nn(reach[:16], own)
+    index = lax.broadcasted_iota(jnp.int32, (16, 1), 0)
+    lengths = jnp.where(index == 0, float(TRUNK), float(SEG))
+    places = jnp.sum(seen * lengths, 0, keepdims=True) + inside.astype(jnp.float32)
+    turn = lax.broadcasted_iota(jnp.int32, (HEAD_DIM // 2, 1), 0).astype(jnp.float32)
+    angles = jnp.exp(turn * (-2.0 / HEAD_DIM * 9.210340371976184)) * places
+    return seen, jnp.cos(angles), jnp.sin(angles)
+
+
+def slot_codes(routes_ref, codes_ref, codes_row_ref):
+    rows = routes_ref.shape[0]
+    half_slots = rows // NFFN
+    routes = routes_ref[...]
+    lanes = lax.broadcasted_iota(jnp.int32, (rows, 128), 1)
+    matches = [
+        jnp.where((lanes == routes[:, c : c + 1]) & (lanes < NFFN), 1.0, 0.0).astype(jnp.float32) for c in range(2)
+    ]
+    square = (rows, rows)
+    earlier = lax.broadcasted_iota(jnp.int32, square, 0) > lax.broadcasted_iota(jnp.int32, square, 1)
+    before = dot_nn(
+        jnp.where(earlier, 1.0, 0.0).astype(jnp.bfloat16), (matches[0] + matches[1]).astype(jnp.bfloat16)
+    )
+    codes = jnp.zeros((rows, 128), jnp.float32)
+    for c in range(2):
+        rank = jnp.sum(matches[c] * before, -1, keepdims=True)
+        route = routes[:, c : c + 1].astype(jnp.float32)
+        late = jnp.where(rank >= half_slots, float((NFFN - 1) * half_slots), 0.0)
+        code = jnp.where(route < NFFN, route * half_slots + rank + late, float(4 * rows))
+        codes = jnp.where(lanes == c, code, codes)
+    codes_ref[...] = codes.astype(jnp.int32)
+    codes_row_ref[...] = codes.T[:8].astype(jnp.int32)
+
+
 def attend_phase_kernel(
-    tokens_ref, gain_ref, query_ref, key_ref, value_ref, cos_ref, sin_ref, bias_ref, gate_ref, up_ref, down_ref,
-    attended_ref, lse_ref, heads_ref, outs_ref, gate_full, up_full, down_full,
+    tokens_ref, table_ref, query_ref, key_ref, value_ref, parents_ref, routes_ref, gate_ref, up_ref, down_ref,
+    attended_ref, lse_ref, bias_ref, cos_ref, sin_ref, codes_ref, codes_row_ref, heads_ref, outs_ref,
+    gate_full, up_full, down_full,
     normed_ref, qkv_sent, qkv_got, out_sent, out_got, q_ref, k_ref, v_ref, o_ref, s_ref, triangle,
     qkv_send, qkv_recv, out_send, out_recv, weight_send, weight_recv, local_sem,
 ):
@@ -231,9 +297,57 @@
     core = lax.axis_index("core")
     started = []
 
+    relays = relayed(copies)
+    xy = lax.axis_index("xy")
+    beside, behind, across = plane_chips(xy)
+    arrivals = {}
+
+    def send_weight(i):
+        shard, full = weights[i]
+        local = pltpu.make_async_copy(shard.at[core], full.at[place], weight_send.at[i, 0])
+        local.start()
+        started.append(local.wait)
+        if relays:
+            targets = [(2, beside, 0), (4, behind, 0), (2, beside, 1), (4, behind, 1)]
+            targets = [(1, 1 - core, {"core": 1 - core})] + [
+                (base + core, other, {"xy": chip, "core": other}) for base, chip, other in targets
+            ]
+            for n, (slot, other, device) in enumerate(targets):
+                copy = remote(
+                    shard.at[other], full.at[place], weight_send.at[i, 1 + n], weight_recv.at[i, slot], device
+                )
+                copy.start()
+                started.append(copy.wait_send)
+            for slot in range(1, 8):
+                arrivals[i, slot] = remote(
+                    shard.at[core], full.at[place], weight_send.at[i, 0], weight_recv.at[i, slot], {"core": 1 - core}
+                )
+        else:
+            for step, other_core, device in others:
+                copy = remote(
+                    shard.at[other_core], full.at[place], weight_send.at[i, step], weight_recv.at[i, step], device
+                )
+                copy.start()
+                started.append(copy.wait)
+
+    def relay_weight(i):
+        full = weights[i][1]
+        for slot, piece, chip, landing in ((4, behind * 2, beside, 6), (3, beside * 2 + 1, behind, 7)):
+            arrivals.pop((i, slot)).wait_recv()
+            copy = remote(
+                full.at[piece], full.at[piece], weight_send.at[i, landing], weight_recv.at[i, landing], {"xy": chip}
+            )
+            copy.start()
+            started.append(copy.wait_send)
+
+    for i in range(3):
+        send_weight(i)
+
     inputs = tokens_ref[...].astype(jnp.float32)
     inverse = lax.rsqrt(jnp.mean(inputs * inputs, -1, keepdims=True) + epsilon)
-    normed_ref[...] = (inputs * inverse * gain_ref[...]).astype(jnp.bfloat16)
+    normed_ref[...] = (inputs * inverse * table_ref[0:1, :]).astype(jnp.bfloat16)
+    reach = reach_of(parents_ref[...])
+    _, cosine, sine = place_tables(reach, member * rows, rows)
     half = HEAD_DIM // 2
     span_width = owners * HEAD_DIM
     qkv_copies = []
@@ -245,7 +359,6 @@
                 first = turned[z * HEAD_DIM : z * HEAD_DIM + half]
                 second = turned[z * HEAD_DIM + half : (z + 1) * HEAD_DIM]
                 if i < 2:
-                    cosine, sine = cos_ref[...], sin_ref[...]
                     first, second = first * cosine - second * sine, second * cosine + first * sine
                 qkv_sent[j, z, base : base + half] = first.astype(jnp.bfloat16)
                 qkv_sent[j, z, base + half : base + HEAD_DIM] = second.astype(jnp.bfloat16)
@@ -260,17 +373,11 @@
             copy.start()
             group.append(copy)
         qkv_copies.append((local, group))
-        if j == 0:
-            for i, (shard, full) in enumerate(weights):
-                local = pltpu.make_async_copy(shard.at[core], full.at[place], weight_send.at[i, 0])
-                local.start()
-                started.append((local, None))
-                for step, other_core, device in others:
-                    copy = remote(
-                        shard.at[other_core], full.at[place], weight_send.at[i, step], weight_recv.at[i, step], device
-                    )
-                    copy.start()
-                    started.append((None, copy))
+    seen, whole_cosine, whole_sine = place_tables(reach, 0, owners * rows)
+    bias_ref[...] = jnp.where(seen > 0.5, 0.0, masked_score)
+    cos_ref[...] = whole_cosine
+    sin_ref[...] = whole_sine
+    slot_codes(routes_ref, codes_ref, codes_row_ref)
 
     out_copies = []
     kept = []
@@ -297,6 +404,9 @@
             )
             copy.start()
             out_copies.append(copy)
+        if relays and j == 1:
+            for i in range(3):
+                relay_weight(i)
     for copy in out_copies:
         copy.wait_recv()
     for copy in kept:
@@ -307,14 +417,13 @@
             copy.wait_send()
     for copy in out_copies:
         copy.wait_send()
-    for local, copy in started:
-        if copy is None:
-            local.wait()
-        else:
-            copy.wait()
-
-
-def attend_phase(tokens, gain, weights, cosine, sine, bias, shards, copies):
+    for copy in arrivals.values():
+        copy.wait_recv()
+    for wait in started:
+        wait()
+
+
+def attend_phase(tokens, table, weights, parents, routes, shards, copies):
     rows, width = tokens.shape
     owners = lax.axis_size("expert")
     length = rows * owners
@@ -327,11 +436,15 @@
     sems = lambda *shape: pltpu.SemaphoreType.DMA(shape)
     return pl.pallas_call(
         attend_phase_kernel,
-        in_specs=[vmem] * 8 + [hbm] * 3,
-        out_specs=(vmem, vmem, hbm, hbm, hbm, hbm, hbm),
+        in_specs=[vmem] * 7 + [hbm] * 3,
+        out_specs=(vmem,) * 7 + (hbm,) * 5,
         out_shape=(
             jax.ShapeDtypeStruct(out, jnp.bfloat16),
             jax.ShapeDtypeStruct((8, length), jnp.float32),
+            jax.ShapeDtypeStruct((16, length), jnp.float32),
+            *(jax.ShapeDtypeStruct((HEAD_DIM // 2, length), jnp.float32),) * 2,
+            jax.ShapeDtypeStruct((rows, 128), jnp.int32),
+            jax.ShapeDtypeStruct((8, rows), jnp.int32),
             jax.ShapeDtypeStruct(head, jnp.bfloat16),
             jax.ShapeDtypeStruct(out, jnp.bfloat16),
             *fulls,
@@ -353,7 +466,7 @@
         ],
         compiler_params=pltpu.CompilerParams(vmem_limit_bytes=56 * MIB, collective_id=1, has_side_effects=True),
         cost_estimate=cost(1e10, 5e7),
-    )(tokens, gain, *weights, cosine, sine, bias, *shards)
+    )(tokens, table, *weights, parents, routes, *shards)
 
 
 def lane_pick(values, lanes, index):
@@ -361,10 +474,13 @@
 
 
 def middle_kernel(
-    tokens_ref, attended_ref, out_weight_ref, gain_ref, mixer_ref, prior_ref, prior_weight_ref,
-    routes_ref, codes_ref, resid_ref, small_ref, first_ref, second_ref, hidden_ref,
+    tokens_ref, attended_ref, out_weight_ref, table_ref, router_ref, constant_ref, prior_ref, prior_weight_ref,
+    routes_ref, codes_ref, resid_ref, small_ref, first_ref, second_ref, mixer_ref, hidden_ref,
 ):
     rows, width = tokens_ref.shape
+    mixer_ref[...] = jnp.concatenate(
+        [router_ref[...], constant_ref[...], jnp.zeros((width, 128 - NEXP - 4), jnp.bfloat16)], 1
+    )
 
     @pl.loop(0, rows // SEG)
     def _(step):
@@ -372,13 +488,14 @@
         attended = attended_ref[:, span].astype(jnp.float32).T.astype(jnp.bfloat16)
         resid = tokens_ref[span, :].astype(jnp.float32) + dot_nn(attended, out_weight_ref[...])
         inverse = lax.rsqrt(jnp.mean(resid * resid, -1, keepdims=True) + epsilon)
-        hidden = (resid * inverse * gain_ref[...]).astype(jnp.bfloat16)
+        hidden = (resid * inverse * table_ref[1:2, :]).astype(jnp.bfloat16)
         resid_ref[span, :] = resid
         hidden_ref[span, :] = hidden
         logits = dot_nn(hidden, mixer_ref[...])
-        logits = logits + jnp.dot(
+        carried = jnp.dot(
             prior_ref[span, :], prior_weight_ref[...], precision=precise, preferred_element_type=jnp.float32
         )
+        logits = logits + jnp.concatenate([carried, jnp.zeros((SEG, 128 - NEXP), jnp.float32)], 1)
         lanes = lax.broadcasted_iota(jnp.int32, logits.shape, 1)
         routes = routes_ref[span, :]
         columns = []
@@ -401,7 +518,7 @@
         ref[...] = dot_nn(chosen.astype(jnp.bfloat16), hidden_ref[...]).astype(jnp.bfloat16)
 
 
-def middle(tokens, attended, out_weight, gain, mixer, prior, prior_weight, routes, codes_row):
+def middle(tokens, attended, out_weight, table, router, constant, prior, prior_weight, routes, codes_row):
     rows, width = tokens.shape
     slots = rows
     return pl.pallas_call(
@@ -411,11 +528,12 @@
             jax.ShapeDtypeStruct((rows, 128), jnp.float32),
             jax.ShapeDtypeStruct((slots, width), jnp.bfloat16),
             jax.ShapeDtypeStruct((slots, width), jnp.bfloat16),
+            jax.ShapeDtypeStruct((width, 128), jnp.bfloat16),
         ),
         scratch_shapes=[pltpu.VMEM((rows, width), jnp.bfloat16)],
         compiler_params=params(48),
         cost_estimate=cost(4 * rows * width * width + 4 * rows * rows * width, 1e7),
-    )(tokens, attended, out_weight, gain, mixer, prior, prior_weight, routes, codes_row)
+    )(tokens, attended, out_weight, table, router, constant, prior, prior_weight, routes, codes_row)
 
 
 def plane_partners(owners):
@@ -430,7 +548,7 @@
 
 def expert_phase_kernel(
     xa_ref, xb_ref, small_ref, grad_ref, codes_ref, gate_hbm, up_hbm, down_hbm,
-    back_out, dots_out, f_out, gate_grad, up_grad, down_grad,
+    back_out, dots_out, fa_out, fb_out, gate_grad, up_grad, down_grad,
     gate_ref, up_ref, down_ref, scaled_ref, d_sent, x_got, d_got, back_sent, back_got, dots_sent, dots_got,
     f_sum, back_sum, hid_ref, one_ref, two_ref, x_turned, d_turned, stage, stage_down,
     x_send, x_recv, d_send, d_recv, back_send, back_recv, dots_send, dots_recv, local_sem, stage_sem,
@@ -503,7 +621,7 @@
                 two_ref[far, columns] = active.astype(jnp.bfloat16)
                 f_sum[near, :] += dot_nn(hid, down_ref[columns, :])
 
-        f_out[half] = f_sum[...].astype(jnp.bfloat16).reshape(experts, slots, width)
+        (fa_out, fb_out)[half][...] = f_sum[...].astype(jnp.bfloat16).reshape(experts, slots, width)
 
     def backward(half):
         d = d_got[half].reshape(rows, width)
@@ -528,7 +646,7 @@
     def dots(half):
         ones = jnp.ones((8, width), jnp.float32)
         for e in range(experts):
-            product = f_out[half, e].astype(jnp.float32) * d_got[half, e].astype(jnp.float32)
+            product = (fa_out, fb_out)[half][e].astype(jnp.float32) * d_got[half, e].astype(jnp.float32)
             total = lax.dot_general(
                 ones, product, (((1,), (1,)), ((), ())), precision=precise, preferred_element_type=jnp.float32
             )
@@ -600,11 +718,11 @@
     return pl.pallas_call(
         expert_phase_kernel,
         in_specs=[vmem] * 5 + [hbm] * 3,
-        out_specs=(vmem, vmem, vmem, hbm, hbm, hbm),
+        out_specs=(vmem, vmem, vmem, vmem, hbm, hbm, hbm),
         out_shape=(
             jax.ShapeDtypeStruct(both, jnp.bfloat16),
             jax.ShapeDtypeStruct(dots, jnp.float32),
-            jax.ShapeDtypeStruct(both, jnp.bfloat16),
+            *(jax.ShapeDtypeStruct(both[1:], jnp.bfloat16),) * 2,
             jax.ShapeDtypeStruct(gate.shape, jnp.bfloat16),
             jax.ShapeDtypeStruct(up.shape, jnp.bfloat16),
             jax.ShapeDtypeStruct(down.shape, jnp.bfloat16),
@@ -636,12 +754,32 @@
 
 
 def turn_kernel(
-    resid_ref, small_ref, grad_ref, prior_ref, routes_ref, codes_ref, ra_ref, rb_ref, dots_ref, vector_ref,
-    gain_ref, mixer_ref, prior_turned_ref, out_weight_ref, attended_ref,
-    resid_grad_ref, grads_ref, out_grad_ref, prior_grad_ref, back_ref, sums_ref, prior_sums_ref, extra_ref, *, owners,
+    resid_ref, small_ref, grad_ref, prior_ref, routes_ref, codes_ref, returned_ref, dots_ref, table_ref,
+    mixer_ref, prior_weight_ref, out_weight_ref, attended_ref, f_ref, gate_ref,
+    resid_grad_ref, grads_ref, out_grad_ref, prior_grad_ref, f_got, gate_first,
+    back_ref, sums_ref, prior_sums_ref, extra_ref, f_send, f_recv, gate_send, gate_recv, *, owners, reduce,
 ):
     rows, width = resid_ref.shape
-    slots = 2 * ra_ref.shape[0]
+    planes = plane_partners(owners)
+    beside, behind, across = plane_chips(lax.axis_index("xy"))
+    greet([item[2] for item in planes], [{"xy": beside}, {"xy": behind}] if reduce else [])
+    expert = lax.axis_index("expert") * 2 + lax.axis_index("core")
+    copies = [pltpu.make_async_copy(f_ref.at[expert], f_got.at[expert], f_send.at[0])]
+    copies += [
+        remote(f_ref.at[index], f_got.at[expert], f_send.at[step], f_recv.at[step], device)
+        for step, index, device in planes
+    ]
+    if reduce:
+        for piece, landing, chip in first_hops(beside, behind, across):
+            copies.append(
+                remote(
+                    gate_ref.at[piece], gate_first.at[landing], gate_send.at[landing], gate_recv.at[landing],
+                    {"xy": chip},
+                )
+            )
+    for copy in copies:
+        copy.start()
+    slots = returned_ref.shape[0]
     sums_ref[...] = jnp.zeros_like(sums_ref)
     prior_sums_ref[...] = jnp.zeros_like(prior_sums_ref)
 
@@ -654,7 +792,8 @@
         mixing = [[small[:, 2 + 2 * m + c : 3 + 2 * m + c] for c in range(2)] for m in range(2)]
         inverse = small[:, 6:7]
         normed = resid_ref[span, :] * inverse
-        hidden = normed * gain_ref[...]
+        gain = table_ref[1:2, :]
+        hidden = normed * gain
         hidden_b = hidden.astype(jnp.bfloat16)
         grad_b = grad_ref[span, :]
         grad = grad_b.astype(jnp.float32)
@@ -663,10 +802,9 @@
         dots = dots_ref[...]
         terms = [jnp.sum(jnp.where(hit, dots, 0.0), -1, keepdims=True) for hit in hits]
         chosen = (hits[0] | hits[1]).astype(jnp.bfloat16)
-        half = slots // 2
-        routed = dot_nn(chosen[:, :half], ra_ref[...]) + dot_nn(chosen[:, half:], rb_ref[...])
+        routed = dot_nn(chosen, returned_ref[...])
         along = jnp.sum(grad * hidden, -1, keepdims=True)
-        across = [jnp.sum(grad * vector_ref[m : m + 1, :], -1, keepdims=True) for m in range(2)]
+        across = [jnp.sum(grad * table_ref[2 + m : 3 + m, :], -1, keepdims=True) for m in range(2)]
         to_copy = 0.0
         to_mix = [0.0, 0.0]
         for c in range(2):
@@ -691,11 +829,12 @@
             for c in range(2):
                 scores = jnp.where(lanes == NEXP + 2 * m + c, mixing[m][c] * (pair[c] - mean), scores)
             direct = direct + mixing[m][0] * to_mix[m]
-        prior_grad_ref[span, :] = jnp.dot(
-            logit_grads, prior_turned_ref[...], precision=precise, preferred_element_type=jnp.float32
-        )[:, : prior_grad_ref.shape[1]]
-        hidden_grads = split_dot(dot_nn, scores, mixer_ref[...]) + direct * grad + routed
-        scaled = hidden_grads * gain_ref[...]
+        prior_grad_ref[span, :] = lax.dot_general(
+            logit_grads[:, :NEXP], prior_weight_ref[...], (((1,), (1,)), ((), ())),
+            precision=precise, preferred_element_type=jnp.float32,
+        )
+        hidden_grads = split_dot(dot_nt, scores, mixer_ref[...]) + direct * grad + routed
+        scaled = hidden_grads * gain
         resid_grads = inverse * (scaled - normed * jnp.mean(scaled * normed, -1, keepdims=True)) + grad
         resid_grad_ref[span, :] = resid_grads
         back_ref[span, :] = resid_grads.astype(jnp.bfloat16)
@@ -722,30 +861,52 @@
     back = back_ref[...]
     grads_ref[...] = dot_nt(out_weight_ref[...], back).astype(jnp.bfloat16)
     out_grad_ref[:, :width] = dot_nn(attended_ref[...], back).astype(jnp.bfloat16)
-
-
-def turn(resid, small, grad, prior, routes, codes, returned, dots, vector, gain, mixer_turned, prior_turned, out_weight, attended):
+    for copy in copies:
+        copy.wait()
+
+
+def turn(resid, small, grad, prior, routes, codes, returned, dots, table, mixer, prior_weight, out_weight, attended, f, gate):
     rows, width = resid.shape
+    owners = lax.axis_size("expert")
+    vmem, hbm = pl.BlockSpec(memory_space=pltpu.VMEM), pl.BlockSpec(memory_space=pl.ANY)
     return pl.pallas_call(
-        functools.partial(turn_kernel, owners=lax.axis_size("expert")),
+        functools.partial(turn_kernel, owners=owners, reduce=relayed(gate.shape[0])),
+        in_specs=[vmem] * 13 + [hbm] * 2,
+        out_specs=(vmem, vmem, vmem, vmem, hbm, hbm),
         out_shape=(
             jax.ShapeDtypeStruct((rows, width), jnp.float32),
             jax.ShapeDtypeStruct((width, rows), jnp.bfloat16),
             jax.ShapeDtypeStruct((width, width + 256), jnp.bfloat16),
             jax.ShapeDtypeStruct(prior.shape, jnp.float32),
+            jax.ShapeDtypeStruct(f.shape, f.dtype),
+            jax.ShapeDtypeStruct((4, *gate.shape[1:]), gate.dtype),
         ),
         scratch_shapes=[
             pltpu.VMEM((rows, width), jnp.bfloat16),
             pltpu.VMEM((32, width), jnp.float32),
             pltpu.VMEM((prior.shape[1], 128), jnp.float32),
             pltpu.VMEM((width, 128), jnp.float32),
+            pltpu.SemaphoreType.DMA((2 * owners,)),
+            pltpu.SemaphoreType.DMA((2 * owners,)),
+            pltpu.SemaphoreType.DMA((4,)),
+            pltpu.SemaphoreType.DMA((4,)),
         ],
-        compiler_params=params(56),
+        compiler_params=pltpu.CompilerParams(vmem_limit_bytes=60 * MIB, collective_id=4, has_side_effects=True),
         cost_estimate=cost(4 * rows * width * width + 4 * rows * rows * width, 1.5e7),
-    )(resid, small, grad, prior, routes, codes, *returned, dots, vector, gain, mixer_turned, prior_turned, out_weight, attended)
-
-
-def combine_kernel(resid_ref, small_ref, routes_ref, codes_ref, fa_ref, fb_ref, vector_ref, gain_ref, out_ref):
+    )(resid, small, grad, prior, routes, codes, returned, dots, table, mixer, prior_weight, out_weight, attended, f, gate)
+
+
+def finish_kernel(
+    resid_ref, small_ref, routes_ref, codes_ref, fa_ref, fb_ref, table_ref, totals_ref, *refs, owners
+):
+    count = (len(refs) - 11) // 3
+    sources, targets, refs = refs[:count], refs[count : 2 * count], refs[2 * count :]
+    out_ref, *weight_refs, router_ref, prior_ref, constant_ref, rows_ref = refs[:9]
+    held, (load_sem, store_sem) = refs[9:-2], refs[-2:]
+    loads = [pltpu.make_async_copy(one, two, load_sem.at[i]) for i, (one, two) in enumerate(zip(sources, held))]
+    stores = [pltpu.make_async_copy(one, two, store_sem.at[i]) for i, (one, two) in enumerate(zip(held, targets))]
+    for move in loads:
+        move.start()
     rows, width = resid_ref.shape
     half = fa_ref.shape[0]
 
@@ -755,7 +916,7 @@
         small = small_ref[span, :]
         routes, codes = routes_ref[span, :], codes_ref[span, :]
         resid = resid_ref[span, :]
-        hidden = resid * small[:, 6:7] * gain_ref[...]
+        hidden = resid * small[:, 6:7] * table_ref[1:2, :]
         index = lax.broadcasted_iota(jnp.int32, (SEG, 2 * half), 1)
         total = resid
         direct = 0.0
@@ -768,38 +929,79 @@
             for m in range(2):
                 mixed = jnp.where(route == NFFN + 2 + m, gate, 0.0)
                 direct = direct + mixed * small[:, 2 + 2 * m : 3 + 2 * m]
-                total = total + mixed * small[:, 3 + 2 * m : 4 + 2 * m] * vector_ref[m : m + 1, :]
+                total = total + mixed * small[:, 3 + 2 * m : 4 + 2 * m] * table_ref[2 + m : 3 + m, :]
         out_ref[span, :] = (total + direct * hidden).astype(jnp.bfloat16)
 
-
-def combine(resid, small, routes, codes, outs, vector, gain):
+    for load, store in zip(loads, stores):
+        load.wait()
+        store.start()
+    heads_width = owners * HEAD_DIM
+    for i, ref in enumerate(weight_refs[:3]):
+        for p in range(1, totals_ref.shape[0]):
+            ref[:, (p - 1) * heads_width : p * heads_width] = totals_ref[
+                p, :, i * heads_width : (i + 1) * heads_width
+            ].astype(jnp.float32)
+    weight_refs[3][...] = totals_ref[0, :, :width].astype(jnp.float32)
+    extra = totals_ref[0, :, width : width + 128].astype(jnp.float32)
+    router_ref[...] = extra[:, :NEXP]
+    constant_ref[...] = extra[:, NEXP : NEXP + 4]
+    prior_ref[...] = extra[: NEXP // owners, 32 : 32 + NEXP]
+    turned = extra.T
+    gains = totals_ref[totals_ref.shape[0] - 1, :, width : width + 128].astype(jnp.float32).T
+    rows_ref[0:2, :] = turned[16:18]
+    rows_ref[2:3, :] = turned[24:25]
+    rows_ref[3:4, :] = gains[0:1]
+    rows_ref[4:8, :] = jnp.zeros((4, rows_ref.shape[1]), jnp.float32)
+    for move in stores:
+        move.wait()
+
+
+def finish(resid, small, routes, codes, outs, table, totals, moved):
     rows, width = resid.shape
+    owners = lax.axis_size("expert")
+    share = width // owners
+    vmem, hbm = pl.BlockSpec(memory_space=pltpu.VMEM), pl.BlockSpec(memory_space=pl.ANY)
+    shape = lambda *dims: jax.ShapeDtypeStruct(dims, jnp.float32)
+    count = len(moved)
     return pl.pallas_call(
-        combine_kernel,
-        out_shape=jax.ShapeDtypeStruct((rows, width), jnp.bfloat16),
+        functools.partial(finish_kernel, owners=owners),
+        in_specs=[vmem] * 8 + [hbm] * count,
+        out_specs=(hbm,) * count + (vmem,) * 9,
+        out_shape=(
+            *(jax.ShapeDtypeStruct(item.shape, item.dtype) for item in moved),
+            jax.ShapeDtypeStruct((rows, width), jnp.bfloat16),
+            *(shape(share, width),) * 4,
+            shape(share, NEXP), shape(NEXP // owners, NEXP), shape(share, 4), shape(8, share),
+        ),
+        scratch_shapes=[
+            *(pltpu.VMEM(item.shape, item.dtype) for item in moved),
+            pltpu.SemaphoreType.DMA((count,)),
+            pltpu.SemaphoreType.DMA((count,)),
+        ],
         compiler_params=params(48),
         cost_estimate=cost(8 * rows * rows * width, 8e6),
-    )(resid, small, routes, codes, *outs, vector, gain)
+    )(resid, small, routes, codes, *outs, table, totals, *moved)
 
 
 def attend_back_phase_kernel(
-    grads_ref, heads_ref, outs_ref, lse_ref, bias_ref, cos_ref, sin_ref, tokens_ref, gain_ref,
-    query_ref, key_ref, value_ref, resid_grad_ref, out_part_ref, f_ref, gate_ref, up_ref, down_ref,
+    grads_ref, heads_ref, outs_ref, lse_ref, bias_ref, cos_ref, sin_ref, tokens_ref, table_ref,
+    query_ref, key_ref, value_ref, resid_grad_ref, out_part_ref, f_ref, gate_ref, up_ref, down_ref, gate_first,
     tokens_grad_ref, f_got, gate_got, up_got, down_got, *rest, reduce,
 ):
     if reduce:
-        total_ref, *rest = rest
+        total_ref, gate_out, up_out, down_out, *rest = rest
     else:
         parts_ref, *rest = rest
     (
-        d_got, back_sent, back_got, normed_turned, turned_ref, back_sum,
+        d_got, back_sent, back_got, normed_turned, turned_ref, back_sum, column_ref,
         qt_ref, kt_ref, dt_ref, q_ref, k_ref, v_ref, d_ref, delta_ref, dq_ref, dk_ref, dv_ref, triangle,
-        d_send, d_recv, back_send, back_recv, weight_send, weight_recv, f_send, f_recv, local_sem, *rest,
+        d_send, d_recv, back_send, back_recv, weight_send, weight_recv, f_send, f_recv, local_sem, early_sem, *rest,
     ) = rest
     if reduce:
         (
-            parts_ref, half_got, half_sum, chip_got, chip_sum, ring_got, ring_sum, all_got,
+            parts_ref, half_got, chip_got, chip_sum, ring_got, ring_sum, all_got,
             half_send, half_recv, chip_send, chip_recv, ring_send, ring_recv, all_send, all_recv,
+            gate_work, gate_sums, up_sums, gate_wide, down_work, down_sums, down_wide, work_sem, wide_sem,
         ) = rest
     chunks, owners, _, rows = grads_ref.shape
     width = tokens_ref.shape[1]
@@ -824,7 +1026,7 @@
 
     inputs = tokens_ref[...].astype(jnp.float32)
     inverse = lax.rsqrt(jnp.mean(inputs * inputs, -1, keepdims=True) + epsilon)
-    normed_turned[...] = (inputs * inverse * gain_ref[...]).T.astype(jnp.bfloat16)
+    normed_turned[...] = (inputs * inverse * table_ref[0:1, :]).T.astype(jnp.bfloat16)
     share = width // owners
     part_shape = (owners, share // 48, 48)
 
@@ -834,18 +1036,25 @@
         else:
             parts_ref[p, :, begin : begin + size] = values
 
-    fill(0, out_part_ref[...], 0, out_part_ref.shape[1])
-    columns_total = out_part_ref.shape[1]
-    for p in range(1, chunks + 1):
-        fill(p, jnp.zeros((width, columns_total - width), jnp.bfloat16), width, columns_total - width)
+    columns_total = parts_ref.shape[-1]
+    early = [
+        pltpu.make_async_copy(resid_grad_ref, tokens_grad_ref, early_sem.at[0]),
+        pltpu.make_async_copy(out_part_ref, parts_ref.at[0], early_sem.at[1]),
+    ]
+    for copy in early:
+        copy.start()
+    fill(chunks, jnp.zeros((width, 128), jnp.bfloat16), width + 128, columns_total - width - 128)
 
     stages = {}
 
+    def half_of(p):
+        return (columns_total if p in (0, chunks) else width) // 2
+
     def over_cores(p):
-        half = columns_total // 2
-        away = pl.ds(pl.multiple_of((1 - core) * half, half), half)
+        half = half_of(p)
+        away = pl.ds(pl.multiple_of((1 - core) * half, 128), half)
         copy = remote(
-            parts_ref.at[p, :, :, :, away], half_got.at[p], half_send.at[p], half_recv.at[p], {"core": 1 - core}
+            parts_ref.at[p, :, :, :, away], half_got.at[p, :, :, :, pl.ds(0, half)], half_send.at[p], half_recv.at[p], {"core": 1 - core}
         )
         copy.start()
         stages[p, 0] = [copy]
@@ -853,70 +1062,150 @@
     def over_chips(p):
         for copy in stages[p, 0]:
             copy.wait_recv()
-        half = columns_total // 2
-        mine = pl.ds(pl.multiple_of(core * half, half), half)
-        half_sum[p] = (
-            parts_ref[p, :, :, :, mine].astype(jnp.float32) + half_got[p].astype(jnp.float32)
+        half = half_of(p)
+        mine, near = pl.ds(pl.multiple_of(core * half, 128), half), pl.ds(0, half)
+        half_got[p, :, :, :, near] = (
+            parts_ref[p, :, :, :, mine].astype(jnp.float32) + half_got[p, :, :, :, near].astype(jnp.float32)
         ).astype(jnp.bfloat16)
         stages[p, 1] = []
         for step in (3, 1, 2):
             index = lax.rem(xy + step, 4)
             copy = remote(
-                half_sum.at[p, :, index], chip_got.at[p, xy], chip_send.at[p, step - 1], chip_recv.at[p, step - 1],
+                half_got.at[p, :, index, :, near], chip_got.at[p, xy, :, :, near], chip_send.at[p, step - 1], chip_recv.at[p, step - 1],
                 {"xy": index},
             )
             copy.start()
             stages[p, 1].append(copy)
-        chip_got[p, xy] = half_sum[p, :, xy]
+        chip_got[p, xy, :, :, near] = half_got[p, :, xy, :, near]
 
     def over_owners(p):
         for copy in stages[p, 1]:
             copy.wait_recv()
-        chip_sum[p] = jnp.sum(chip_got[p].astype(jnp.float32), 0).astype(jnp.bfloat16)
+        near = pl.ds(0, half_of(p))
+        chip_sum[p, :, :, near] = jnp.sum(chip_got[p, :, :, :, near].astype(jnp.float32), 0).astype(jnp.bfloat16)
         stages[p, 2] = []
         for step, index, device in ring:
             copy = remote(
-                chip_sum.at[p, index], ring_got.at[p, member], ring_send.at[p, step - 1], ring_recv.at[p, step - 1],
+                chip_sum.at[p, index, :, near], ring_got.at[p, member, :, near], ring_send.at[p, step - 1], ring_recv.at[p, step - 1],
                 device,
             )
             copy.start()
             stages[p, 2].append(copy)
-        ring_got[p, member] = chip_sum[p, member]
+        ring_got[p, member, :, near] = chip_sum[p, member, :, near]
 
     def to_copies(p):
         for copy in stages[p, 2]:
             copy.wait_recv()
-        half = columns_total // 2
-        mine = pl.ds(pl.multiple_of(core * half, half), half)
-        ring_sum[p] = jnp.sum(ring_got[p].astype(jnp.float32), 0).astype(jnp.bfloat16)
+        half = half_of(p)
+        mine, near = pl.ds(pl.multiple_of(core * half, 128), half), pl.ds(0, half)
+        ring_sum[p, :, near] = jnp.sum(ring_got[p, :, :, near].astype(jnp.float32), 0).astype(jnp.bfloat16)
         stages[p, 3] = []
         for step, _, device in others:
             copy = remote(
-                ring_sum.at[p], all_got.at[p, xy, :, mine], all_send.at[p, step - 1], all_recv.at[p, step - 1], device
+                ring_sum.at[p, :, near], all_got.at[p, xy, :, mine], all_send.at[p, step - 1], all_recv.at[p, step - 1], device
             )
             copy.start()
             stages[p, 3].append(copy)
-        all_got[p, xy, :, mine] = ring_sum[p]
+        all_got[p, xy, :, mine] = ring_sum[p, :, near]
 
     def advance(*pairs):
         if reduce:
             for stage, p in pairs:
                 (over_cores, over_chips, over_owners, to_copies)[stage](p)
 
+    for copy in early:
+        copy.wait()
     advance((0, 0))
 
     background = []
-    for i, (source, target) in enumerate(((gate_ref, gate_got), (up_ref, up_got), (down_ref, down_got))):
-        local = pltpu.make_async_copy(source.at[place], target.at[place], weight_send.at[i, 0])
-        local.start()
-        background.append((local, None))
-        for step, index, device in others:
-            copy = remote(
-                source.at[2 * device["xy"] + device["core"]], target.at[place],
-                weight_send.at[i, step], weight_recv.at[i, step], device,
-            )
-            copy.start()
-            background.append((None, copy))
+
+    pieces = ((gate_ref, gate_got), (up_ref, up_got), (down_ref, down_got))
+
+    def send_experts():
+        for i, (source, target) in enumerate(pieces):
+            local = pltpu.make_async_copy(source.at[place], target.at[place], weight_send.at[i, 0])
+            local.start()
+            background.append(local.wait)
+            for step, index, device in others:
+                copy = remote(
+                    source.at[2 * device["xy"] + device["core"]], target.at[place],
+                    weight_send.at[i, step], weight_recv.at[i, step], device,
+                )
+                copy.start()
+                background.append(copy.wait)
+
+    beside, behind, across = plane_chips(xy)
+    landed = {}
+
+    def relay(i, source, landing, device):
+        target = landing_ref(i, landing)
+        copy = remote(source, target, weight_send.at[i, landing], weight_recv.at[i, landing], device)
+        copy.start()
+        landed[i, landing] = copy
+
+    def landing_ref(i, landing):
+        return gate_first.at[landing] if i == 0 and landing < 4 else pieces[i][1].at[landing]
+
+    def arrive(i, *landings):
+        for landing in landings:
+            if (i, landing) in landed:
+                landed[i, landing].wait_recv()
+
+    def first_hop(i):
+        for piece, landing, chip in first_hops(beside, behind, across):
+            relay(i, pieces[i][0].at[piece], landing, {"xy": chip})
+
+    def buffers(i):
+        if i < 2:
+            return gate_work, (gate_sums, up_sums)[i], gate_wide, (gate_out, up_out)[i]
+        return down_work, down_sums, down_wide, down_out
+
+    def load(i, items):
+        work = buffers(i)[0]
+        loads = [pltpu.make_async_copy(ref, work.at[n], work_sem.at[n]) for n, ref in enumerate(items)]
+        for item in loads:
+            item.start()
+        for item in loads:
+            item.wait()
+
+    def second_hop(i):
+        source = pieces[i][0]
+        work, sums = buffers(i)[:2]
+        arrive(i, 2, 3)
+        load(i, (source.at[behind * 2], landing_ref(i, 2), source.at[beside * 2 + 1], landing_ref(i, 3)))
+        for n, device in enumerate(({"xy": behind}, {"xy": beside})):
+            sums[n] = (work[2 * n].astype(jnp.float32) + work[2 * n + 1].astype(jnp.float32)).astype(jnp.bfloat16)
+            relay(i, sums.at[n], 4 + n, device)
+
+    def core_hop(i):
+        source = pieces[i][0]
+        work, sums, wide, out = buffers(i)
+        arrive(i, 0, 1, 4, 5)
+        got = [landing_ref(i, landing) for landing in (0, 4, 1, 5)]
+        load(i, (source.at[xy * 2], got[0], got[1], source.at[xy * 2 + 1], got[2], got[3]))
+        if i == 1:
+            store(0).wait()
+        totals = [jnp.sum(work[3 * n : 3 * n + 3].astype(jnp.float32), 0) for n in range(2)]
+        wide[core] = jnp.where(core == 0, totals[0], totals[1])
+        sums[2] = jnp.where(core == 0, totals[1], totals[0]).astype(jnp.bfloat16)
+        relay(i, sums.at[2], 6, {"core": 1 - core})
+
+    def store(i):
+        wide, out = buffers(i)[2:]
+        return pltpu.make_async_copy(wide, out, wide_sem.at[i])
+
+    def finish(i):
+        work, sums, wide, out = buffers(i)
+        arrive(i, 6)
+        load(i, (landing_ref(i, 6),))
+        wide[1 - core] = work[0].astype(jnp.float32)
+        store(i).start()
+
+    if reduce:
+        for i in (1, 2):
+            first_hop(i)
+    else:
+        send_experts()
 
     def head(j):
         local, group = d_groups[j]
@@ -956,60 +1245,78 @@
             term = dot_nn(weight[:, j * span_width : (j + 1) * span_width], turned_ref[i * span_width : (i + 1) * span_width, :])
             total = term if total is None else total + term
         back_sum[...] = total if j == 0 else back_sum[...] + total
+        column = jnp.sum(total * normed_turned[...].astype(jnp.float32), -1, keepdims=True)
+        column_ref[...] = column if j == 0 else column_ref[...] + column
+        if j == chunks - 1:
+            fill(chunks, jnp.broadcast_to(column_ref[...], (width, 128)).astype(jnp.bfloat16), width, 128)
         fill(j + 1, dot_nt(normed_turned[...], turned_ref[...]).astype(jnp.bfloat16), 0, 3 * span_width)
 
+    def send_f():
+        expert = member * 2 + core
+        local = pltpu.make_async_copy(f_ref.at[expert], f_got.at[expert], f_send.at[0])
+        local.start()
+        background.append(local.wait)
+        for step, index, device in planes:
+            copy = remote(f_ref.at[index], f_got.at[expert], f_send.at[step], f_recv.at[step], device)
+            copy.start()
+            background.append(copy.wait)
+
+    def expert_step(step, i):
+        if reduce:
+            step(i)
+
     groups = [head(0)]
+    expert_step(second_hop, 0)
+    groups.append(head(1))
     advance((1, 0))
-    groups.append(head(1))
+    expert_step(second_hop, 1)
+    groups.append(head(2))
+    expert_step(second_hop, 2)
+    advance((2, 0))
     weights_of(0, groups[0])
-    advance((2, 0), (0, 1))
-    groups.append(head(2))
-    for half in range(2):
-        expert = member * 2 + core
-        local = pltpu.make_async_copy(f_ref.at[half, expert], f_got.at[half, expert], f_send.at[half, 0])
-        local.start()
-        background.append((local, None))
-        for step, index, device in planes:
-            copy = remote(
-                f_ref.at[half, index], f_got.at[half, expert], f_send.at[half, step], f_recv.at[half, step], device
-            )
-            copy.start()
-            background.append((None, copy))
-    advance((3, 0), (1, 1))
+    advance((0, 1), (3, 0))
+    expert_step(core_hop, 0)
     weights_of(1, groups[1])
-    advance((0, 2), (2, 1), (1, 2))
+    advance((0, 2), (1, 1))
+    expert_step(finish, 0)
+    expert_step(core_hop, 1)
+    advance((1, 2), (2, 1))
     weights_of(2, groups[2])
+    advance((0, 3))
+    send_f()
     normed = inputs * inverse
     first_grads = back_sum[...].T
-    summed = jnp.sum((first_grads * normed).reshape(rows // 8, 8, width), 0)
-    column = jnp.sum(summed.T, -1, keepdims=True)
-    fill(chunks, jnp.broadcast_to(column, (width, 128)).astype(jnp.bfloat16), width, 128)
-    advance((0, 3), (3, 1), (2, 2))
-    scaled = first_grads * gain_ref[...]
-    tokens_grad_ref[...] = (
-        inverse * (scaled - normed * jnp.mean(scaled * normed, -1, keepdims=True)) + resid_grad_ref[...]
-    )
-    advance((1, 3), (3, 2), (2, 3), (3, 3))
+    advance((1, 3))
+    expert_step(core_hop, 2)
+    advance((2, 2), (3, 1))
+    expert_step(finish, 1)
+    scaled = first_grads * table_ref[0:1, :]
+    tokens_grad_ref[...] += inverse * (scaled - normed * jnp.mean(scaled * normed, -1, keepdims=True))
+    advance((2, 3), (3, 2))
+    expert_step(finish, 2)
+    advance((3, 3))
     if reduce:
         for p in range(chunks + 1):
             for copy in stages[p, 3]:
                 copy.wait_recv()
-            total_ref[p] = all_got[p].astype(jnp.float32).reshape(share, columns_total)
+            size = 2 * half_of(p)
+            total_ref[p, :, :size] = all_got[p, :, :, :size].reshape(share, size)
             for stage in range(4):
                 for copy in stages[p, stage]:
                     copy.wait_send()
+        for copy in landed.values():
+            copy.wait_send()
+        for i in range(1, 3):
+            store(i).wait()
     for local, group in d_groups + groups:
         for copy in group:
             copy.wait_send()
-    for local, copy in background:
-        if copy is None:
-            local.wait()
-        else:
-            copy.wait()
+    for wait in background:
+        wait()
 
 
 def attend_back_phase(
-    grads, heads, outs, lse, bias, cosine, sine, tokens, gain, weights, resid_grads, out_part, fs, expert_grads, copies
+    grads, heads, outs, lse, bias, cosine, sine, tokens, table, weights, resid_grads, out_part, f, pieces, gate_first, copies
 ):
     chunks, owners, _, rows = grads.shape
     width = tokens.shape[1]
@@ -1018,9 +1325,9 @@
     columns = out_part.shape[1]
     share = width // owners
     total = chunks + 1
-    reduce = copies == 8 and share == 4 * 48
+    reduce = relayed(copies)
     vmem, hbm = pl.BlockSpec(memory_space=pltpu.VMEM), pl.BlockSpec(memory_space=pl.ANY)
-    pieces = [item.reshape(copies, -1, item.shape[-1]) for item in expert_grads]
+    gate_shape, down_shape = pieces[0].shape[1:], pieces[2].shape[1:]
     turned = pltpu.VMEM((HEAD_DIM, length), jnp.bfloat16)
     plain = pltpu.VMEM((length, HEAD_DIM), jnp.bfloat16)
     wide = pltpu.VMEM((length, HEAD_DIM), jnp.float32)
@@ -1032,20 +1339,20 @@
         pltpu.VMEM((width, rows), jnp.bfloat16),
         pltpu.VMEM((3 * owners * HEAD_DIM, rows), jnp.bfloat16),
         pltpu.VMEM((width, rows), jnp.float32),
+        pltpu.VMEM((width, 1), jnp.float32),
         turned, turned, turned, plain, plain, plain, plain,
         pltpu.VMEM((1, length), jnp.float32),
         pltpu.VMEM((HEAD_DIM, length), jnp.float32),
         wide, wide,
         pltpu.VMEM((TILE, TILE), jnp.float32),
         *(sems(chunks, owners - 1),) * 4,
-        sems(3, copies), sems(3, copies), sems(2, 2 * owners), sems(2, 2 * owners), sems(2 * chunks),
+        sems(3, copies), sems(3, copies), sems(2 * owners), sems(2 * owners), sems(2 * chunks), sems(2),
     ]
     if reduce:
         half = columns // 2
         low = lambda *shape: pltpu.VMEM(shape, jnp.bfloat16)
         scratch += [
             low(total, owners, 4, 48, columns),
-            low(total, owners, 4, 48, half),
             low(total, owners, 4, 48, half),
             low(total, 4, owners, 48, half),
             low(total, owners, 48, half),
@@ -1054,53 +1361,40 @@
             low(total, 4, 48, columns),
             sems(total), sems(total), sems(total, 3), sems(total, 3),
             sems(total, owners - 1), sems(total, owners - 1), sems(total, copies - 1), sems(total, copies - 1),
+            low(6, *gate_shape), low(3, *gate_shape), low(3, *gate_shape), pltpu.VMEM((2, *gate_shape), jnp.float32),
+            low(6, *down_shape), low(3, *down_shape), pltpu.VMEM((2, *down_shape), jnp.float32),
+            sems(6), sems(3),
         ]
-        last_spec, last_shape = vmem, jax.ShapeDtypeStruct((total, share, columns), jnp.float32)
+        out_part = out_part.reshape(owners, 4, 48, columns)
+        last_specs = (vmem, hbm, hbm, hbm)
+        last_shapes = (
+            jax.ShapeDtypeStruct((total, share, columns), jnp.bfloat16),
+            *(jax.ShapeDtypeStruct((2, *piece.shape[1:]), jnp.float32) for piece in pieces),
+        )
     else:
-        last_spec, last_shape = vmem, jax.ShapeDtypeStruct((total, width, columns), jnp.bfloat16)
-    *result, totals = pl.pallas_call(
+        last_specs, last_shapes = (vmem,), (jax.ShapeDtypeStruct((total, width, columns), jnp.bfloat16),)
+    tokens_grad, f_got, gate_got, up_got, down_got, totals, *sums = pl.pallas_call(
         functools.partial(attend_back_phase_kernel, reduce=reduce),
-        in_specs=[vmem] * 14 + [hbm] * 4,
-        out_specs=(vmem, hbm, hbm, hbm, hbm, last_spec),
+        in_specs=[vmem] * 12 + [hbm] * 7,
+        out_specs=(vmem, hbm, hbm, hbm, hbm, *last_specs),
         out_shape=(
             jax.ShapeDtypeStruct((rows, width), jnp.float32),
-            jax.ShapeDtypeStruct(fs.shape, fs.dtype),
+            jax.ShapeDtypeStruct(f.shape, f.dtype),
             *(jax.ShapeDtypeStruct(piece.shape, piece.dtype) for piece in pieces),
-            last_shape,
+            *last_shapes,
         ),
         scratch_shapes=scratch,
         compiler_params=pltpu.CompilerParams(vmem_limit_bytes=63 * MIB, collective_id=3, has_side_effects=True),
         cost_estimate=cost(2e10, 5e7),
-    )(grads, heads, outs, lse, bias, cosine, sine, tokens, gain, *weights, resid_grads, out_part, fs, *pieces)
+    )(grads, heads, outs, lse, bias, cosine, sine, tokens, table, *weights, resid_grads, out_part, f, *pieces, gate_first)
     if not reduce:
         totals = lax.psum_scatter(totals, "expert", scatter_dimension=1, tiled=True)
-        totals = lax.psum(totals, ("xy", "core")).astype(jnp.float32)
-    return (*result, totals)
-
-
-def lineage_of(parent_row):
-    segment_total = parent_row.shape[0] + 1
-    indices = jnp.arange(segment_total, dtype=jnp.int32)
-    parent_all = jnp.concatenate([jnp.full((1,), -1, jnp.int32), parent_row])
-    reach = (parent_all[:, None] == indices[None, :]) | (indices[:, None] == indices[None, :])
-    for repeat in range(3):
-        reach = jnp.any(reach[:, :, None] & reach[None, :, :], 1)
-    return reach
-
-
-def slot_codes(routes, half_slots):
-    rows = routes.shape[0]
-    experts = jnp.arange(NFFN, dtype=jnp.int32)
-    matches = routes[:, :, None] == experts
-    per_row = jnp.sum(matches.astype(jnp.float32), 1)
-    earlier = jnp.arange(rows)[:, None] > jnp.arange(rows)[None, :]
-    before = jnp.dot(
-        earlier.astype(jnp.bfloat16), per_row.astype(jnp.bfloat16), preferred_element_type=jnp.float32
-    )
-    rank = jnp.sum(jnp.where(matches, before[:, None, :], 0.0), -1).astype(jnp.int32)
-    late = (rank >= half_slots).astype(jnp.int32)
-    code = late * (NFFN * half_slots) + routes * half_slots + rank - late * half_slots
-    return jnp.where(routes < NFFN, code, 4 * NFFN * half_slots)
+        totals = lax.psum(totals, ("xy", "core"))
+        sums = [
+            jnp.sum(got.reshape(copies // 2, 2, *got.shape[1:]).astype(jnp.float32), 0)
+            for got in (gate_got, up_got, down_got)
+        ]
+    return (tokens_grad, f_got, totals, *sums)
 
 
 def per_device(
@@ -1110,83 +1404,50 @@
 ):
     owners = lax.axis_size("expert")
     member = lax.axis_index("expert")
-    core = lax.axis_index("core")
     tokens, prior, routes, grad = tokens[0], prior_logits[0], routes[0], cotangent[0]
     rows, width = tokens.shape
     copies = lax.axis_size("xy") * lax.axis_size("core")
-    length = rows * owners
     chunks = width // HEAD_DIM // owners
-    half_slots = rows // 8
-
-    def own_sum(got):
-        return jnp.sum(got.reshape(copies // 2, 2, *got.shape[1:]).astype(jnp.float32), 0)
-
-    lineage = lineage_of(parents[0])
-    segments = lineage.shape[0]
-    lengths = jnp.where(jnp.arange(segments) == 0, TRUNK, SEG)
-    begins = jnp.where(jnp.arange(segments) == 0, 0, TRUNK + (jnp.arange(segments) - 1) * SEG)
-    shifts = jnp.sum(jnp.where(lineage, lengths[None, :], 0), 1) - lengths - begins
-    ids = jnp.arange(length, dtype=jnp.int32)
-    segment = jnp.where(ids < TRUNK, 0, 1 + (ids - TRUNK) // SEG)
-    own = segment[None, :] == jnp.arange(segments)[:, None]
-    places = (jnp.sum(jnp.where(own, shifts[:, None], 0), 0) + ids).astype(jnp.float32)
-    reach = jnp.any(own[:, None, :] & lineage[:, :, None], 0)
-    bias = jnp.where(reach, 0.0, masked_score).astype(jnp.float32)
-    bias = jnp.concatenate([bias, jnp.zeros((16 - segments, length), jnp.float32)], 0)
-    frequency = 10000.0 ** (-(jnp.arange(HEAD_DIM // 2, dtype=jnp.float32) * 2.0 / HEAD_DIM))
-    angles = frequency[:, None] * places[None, :]
-    cosine, sine = jnp.cos(angles), jnp.sin(angles)
-    own_cosine, own_sine = (lax.dynamic_slice_in_dim(table, member * rows, rows, 1) for table in (cosine, sine))
-
-    attention_row, expert_row = attention_gain[None], expert_gain[None]
+    zeros = jnp.zeros((4, width), jnp.float32)
+    table = jnp.concatenate([attention_gain[None], expert_gain[None], constant_vector, zeros], 0)
     qkv_weights = (query_weight, key_weight, value_weight)
-    attended, logs, heads, outs, gate, up, down = attend_phase(
-        tokens, attention_row, qkv_weights, own_cosine, own_sine, bias, (gate_weight, up_weight, down_weight), copies
+    attended, logs, bias, cosine, sine, codes, codes_row, heads, outs, gate, up, down = attend_phase(
+        tokens, table, qkv_weights, parents, routes, (gate_weight, up_weight, down_weight), copies
     )
     attended = attended.reshape(width, rows)
     gate, up, down = (full.reshape(-1, full.shape[-1]) for full in (gate, up, down))
-    codes = slot_codes(routes, half_slots)
-    codes_row = codes.T
-
-    mixer = jnp.concatenate(
-        [router_weight, constant_weight, jnp.zeros((width, 128 - NEXP - 4), jnp.bfloat16)], 1
+    resid, small, *x_out, mixer = middle(
+        tokens, attended, out_weight, table, router_weight, constant_weight, prior, prior_weight, routes, codes_row
     )
-    prior_wide = jnp.pad(prior_weight, ((0, 0), (0, 128 - NEXP)))
-    prior_turned = jnp.pad(prior_weight.T, ((0, 128 - NEXP), (0, 128 - NEXP)))
-    resid, small, *x_out = middle(
-        tokens, attended, out_weight, expert_row, mixer, prior, prior_wide, routes, codes_row
+    backs, dots, fa, fb, *grads = expert_phase(x_out, small, grad, codes_row, gate, up, down)
+    pieces = [item.reshape(copies, -1, item.shape[-1]) for item in grads]
+    dots = dots[:, :, 0, : rows // NFFN].reshape(1, 2 * rows)
+    resid_grads, grads_out, out_part, prior_grad, fa, gate_first = turn(
+        resid, small, grad, prior, routes, codes, backs.reshape(2 * rows, width), dots, table, mixer, prior_weight,
+        out_weight, attended, fa, pieces[0],
     )
-    backs, dots, fs, grads_gate, grads_up, grads_down = expert_phase(x_out, small, grad, codes_row, gate, up, down)
-    dots = dots[:, :, 0, :half_slots].reshape(1, 2 * rows)
-    backs = backs.reshape(2, rows, width)
-    vector = jnp.concatenate([constant_vector, jnp.zeros((6, width), jnp.float32)], 0)
-    resid_grads, grads_out, out_part, prior_grad = turn(
-        resid, small, grad, prior, routes, codes, backs, dots, vector, expert_row,
-        mixer.T, prior_turned, out_weight, attended,
+    tokens_grad, fb, totals, *sums = attend_back_phase(
+        grads_out.reshape(chunks, owners, HEAD_DIM, rows), heads, outs, logs, bias, cosine, sine, tokens,
+        table, qkv_weights, resid_grads, out_part, fb, pieces, gate_first, copies,
     )
-    tokens_grad, fs, gate_got, up_got, down_got, totals = attend_back_phase(
-        grads_out.reshape(chunks, owners, HEAD_DIM, rows), heads, outs, logs, bias, cosine, sine, tokens,
-        attention_row, qkv_weights, resid_grads, out_part, fs, (grads_gate, grads_up, grads_down), copies,
-    )
-    result = combine(resid, small, routes, codes, fs.reshape(2, rows, width), vector, expert_row)
-    gate_part, up_part, down_part = (own_sum(got) for got in (gate_got, up_got, down_got))
-    span = owners * HEAD_DIM
-    qkv_totals = [
-        jnp.concatenate([part[:, i * span : (i + 1) * span] for part in totals[1:]], 1) for i in range(3)
-    ]
-    small_total = totals[0, :, width:]
+    fs = [f.reshape(rows, width) for f in (fa, fb)]
+    (
+        tokens_grad, gate_part, up_part, down_part, result, *qkv_out_grads, router_grad, prior_weight_grad,
+        constant_weight_grad, row_grads,
+    ) = finish(resid, small, routes, codes, fs, table, totals, (tokens_grad, *sums))
+    share = width // owners
+    own_gain = lax.dynamic_slice_in_dim(attention_gain, member * share, share)
     return (
         result[None],
         tokens_grad[None],
         prior_grad[None],
-        *qkv_totals,
-        totals[0, :, :width],
-        totals[chunks, :, width],
-        small_total[:, 24],
-        small_total[:, :NEXP],
-        small_total[: NEXP // owners, 32 : 32 + NEXP],
-        small_total[:, NEXP : NEXP + 4],
-        small_total[:, 16:18].T,
+        *qkv_out_grads,
+        row_grads[3] / own_gain,
+        row_grads[2],
+        router_grad,
+        prior_weight_grad,
+        constant_weight_grad,
+        row_grads[:2],
         gate_part,
         up_part,
         down_part,

time: 564 us -> 479 us (0.85)
  Pallas kernels: 517 us -> 448 us
  local copies, waits for them, and re-layouts: 28.6 us -> 18.2 us
  other arithmetic: 11.7 us -> 2.7 us
    pallas_call x1, Pallas kernels: 233 us -> 158 us  [attend_back_phase(): pl.pallas_call(functools.partial(attend_back_phase_kernel, reduce=reduce)...]
    pallas_call x1, Pallas kernels: 137 us -> 147 us  [expert_phase(): pl.pallas_call(expert_phase_kernel, in_specs=[vmem] * 5 + [hbm] * 3, out_...]
    unnamed x62 -> x51, local copies, waits for them, and re-layouts: 11.9 us -> 14 us
where the time goes in v4:
time: 479 us; the launch traced here: 470 us
  Pallas kernels  448 us (94%)
  local copies, waits for them, and re-layouts  18.2 us (4%)
    pallas_call x1, Pallas kernels, attend_back_phase(): pl.pallas_call(functools.partial(attend_back_phase_kernel, reduce=reduce)...  158 us
    pallas_call x1, Pallas kernels, expert_phase(): pl.pallas_call(expert_phase_kernel, in_specs=[vmem] * 5 + [hbm] * 3, out_...  147 us
    pallas_call x1, Pallas kernels, attend_phase(): pl.pallas_call(attend_phase_kernel, in_specs=[vmem] * 7 + [hbm] * 3, out_...  96.4 us
    pallas_call x1, Pallas kernels, turn(): pl.pallas_call(functools.partial(turn_kernel, owners=owners, reduce=relay...  26.4 us
    unnamed x51, local copies, waits for them, and re-layouts  14 us
    pallas_call x1, Pallas kernels, finish(): pl.pallas_call(functools.partial(finish_kernel, owners=owners), in_specs=...  11.1 us

profile of v4, /device:TPU:1, one launch (start us, length us, event | category | flops | bytes accessed | tf_op | source)
XLA Modules:
  0.0 469.5 jit_solution(11001387662078046758)
XLA Ops:
  0.6 0.7 broadcast_in_dim.18
  1.3 0.7 broadcast_in_dim.19
  2.1 1.4 maximum_maximum_fusion.table_ref
  3.5 1.6 copy.34
  5.1 96.4 %shard_map.297 = (bf16[3,4,64,640]{3,2,1,0:T(8,128)(2,1)}, f32[8,2560]{1,0:T(8,128)}, f32[16,2560]{1,0:T(8,128)}, f32[32,2560]{1,0:T(8,128)}, f32[32,2560]{1,0:T...) custom-call(bf16[640,768]{1,0:T(8,128)(2,1)} %bitcast.33, ...), custom_call_target="tpu_custom_call" | custom-call | flops 10000000000 | bytes 50000000 | tf_op jit(solution)/shard_map/pallas_call | solution.py:437
  102.2 1.2 copy-done.8
  103.4 0.7 copy-done.17
  104.1 9.3 %shard_map.298 = (f32[640,768]{1,0:T(8,128)}, f32[640,128]{1,0:T(8,128)S(1)}, bf16[640,768]{1,0:T(8,128)(2,1)S(1)}, bf16[640,768]{1,0:T(8,128)(2,1)S(1)}, bf16[768,128]{1,0:T(8,128)(2,1)S(1)}) custom-call(bf16[640,768]{1,0:T(8,128)(2,1)S(1)} %bitcast.35, bf16[768,640]{1,0:T(8,128)(2,1)S(1)} %bitcast.31, bf16[768,768]{1,0:T(8,128)(2,1)} %out_weight_ref.3, ...), custom_call_target="tpu_custom_call" | custom-call | flops 2768240640 | bytes 10000000 | tf_op jit(solution)/shard_map/pallas_call | solution.py:524
  113.5 0.7 copy-done.4
  114.9 0.9 copy-done.15
  115.8 0.9 copy-done.16
  116.7 146.9 %shard_map.299 = (bf16[2,8,80,768]{3,2,1,0:T(8,128)(2,1)}, f32[2,8,8,128]{3,2,1,0:T(8,128)}, bf16[8,80,768]{2,1,0:T(8,128)(2,1)}, bf16[8,80,768]{2,1,0:T(8,128)(...) custom-call(bf16[8,80,768]{2,1,0:T(8,128)(2,1)} %bitcast.36, ...), custom_call_target="tpu_custom_call" | custom-call | flops 36238786560 | bytes 50000000 | tf_op jit(solution)/shard_map/pallas_call | solution.py:718
  263.6 0.9 slice_reduce_fusion
  264.5 0.7 reshape_squeeze.3.dots_ref
  265.2 26.4 %shard_map.300 = (f32[640,768]{1,0:T(8,128)}, bf16[768,640]{1,0:T(8,128)(2,1)}, bf16[768,1024]{1,0:T(8,128)(2,1)}, f32[640,12]{1,0:T(8,128)}, bf16[8,80,768]{2,1,0:T(8,128)(2,1)}, /*index=5*/bf16[4,96,2048]{2,1,0:T(8,128)(2,1)}) custom-call(f32[640,768]{1,0:T(8,128)} %get-tuple-element.67.resid_ref, f32[640,128]{1,0:T(8,128)} %copy-done.4, ...), custom_call_target="tpu_custom_call" | custom-call | flops 2768240640 | bytes 15000000 | tf_op jit(solution)/shard_map/pallas_call | solution.py:872
  291.6 157.5 %shard_map.301 = (f32[640,768]{1,0:T(8,128)}, bf16[8,80,768]{2,1,0:T(8,128)(2,1)}, bf16[8,96,2048]{2,1,0:T(8,128)(2,1)}, bf16[8,96,2048]{2,1,0:T(8,128)(2,1)}, b...) custom-call(bf16[3,4,64,640]{3,2,1,0:T(8,128)(2,1)} %bitcast.49, ...), custom_call_target="tpu_custom_call" | custom-call | flops 20000000000 | bytes 50000000 | tf_op jit(solution)/shard_map/pallas_call | solution.py:1376
  449.1 1.4 copy-done.2
  450.6 1.2 copy-done.7
  451.8 1.2 copy-done.9
  453.0 0.7 copy-done.11
  453.7 11.1 %shard_map.302 = (f32[640,768]{1,0:T(8,128)}, f32[2,96,2048]{2,1,0:T(8,128)}, f32[2,96,2048]{2,1,0:T(8,128)}, f32[2,256,768]{2,1,0:T(8,128)}, bf16[640,768]{1,0:...) custom-call(f32[640,768]{1,0:T(8,128)} %get-tuple-element.67.resid_r, ...), custom_call_target="tpu_custom_call" | custom-call | flops 2516582400 | bytes 8000000 | tf_op jit(solution)/shard_map/pallas_call | solution.py:966
  464.8 0.7 copy.39
  466.0 1.3 dynamic-slice_divide_fusion
  468.6 0.8 copy.38
  (43 shorter events, 3.2 us)
Async XLA Ops:
  5.1 96.5 %copy-start.19 = (f32[1,640,12]{1,0,2:T(1,128)S(1)}, f32[1,640,12]{1,0,2:T(1,128)}, u32[]{:S(2)}) copy-start(f32[1,640,12]{1,0,2:T(1,128)} %param.19) | copy-start | bytes 92164
  5.1 96.7 %copy-start.20 = (bf16[768,12]{0,1:T(8,128)(2,1)S(1)}, bf16[768,12]{0,1:T(8,128)(2,1)}, u32[]{:S(2)}) copy-start(bf16[768,12]{0,1:T(8,128)(2,1)} %param.29) | copy-start | bytes 55300
  5.1 96.9 %copy-start.21 = (bf16[768,4]{0,1:T(4,128)(2,1)S(1)}, bf16[768,4]{0,1:T(4,128)(2,1)}, u32[]{:S(2)}) copy-start(bf16[768,4]{0,1:T(4,128)(2,1)} %param.31) | copy-start | bytes 18436
  5.1 97.0 %copy-start = (s32[1,640,2]{2,1,0:T(8,128)S(1)}, s32[1,640,2]{2,1,0:T(8,128)}, u32[]{:S(2)}) copy-start(s32[1,640,2]{2,1,0:T(8,128)} %copy.34) | copy-start | bytes 15364
  5.1 97.0 %copy-start.10 = (f32[8,768]{1,0:T(8,128)S(1)}, f32[8,768]{1,0:T(8,128)}, u32[]{:S(2)}) copy-start(f32[8,768]{1,0:T(8,128)} %maximum_maximum_fusion.table_ref) | copy-start | bytes 73732
  5.1 97.0 %copy-start.13 = (f32[12,12]{1,0:T(8,128)S(1)}, f32[12,12]{1,0:T(8,128)}, u32[]{:S(2)}) copy-start(f32[12,12]{1,0:T(8,128)} %prior_weight_ref.3) | copy-start | bytes 1732
  5.1 97.0 %copy-start.14 = (bf16[1,640,768]{2,1,0:T(8,128)(2,1)S(1)}, bf16[1,640,768]{2,1,0:T(8,128)(2,1)}, u32[]{:S(2)}) copy-start(bf16[1,640,768]{2,1,0:T(8,128)(2,1)} %param.18) | copy-start | bytes 2949124
  101.7 11.7 %copy-start.6 = (f32[1,640,12]{2,1,0:T(8,128)}, f32[1,640,12]{2,1,0:T(8,128)S(1)}, u32[]{:S(2)}) copy-start(f32[1,640,12]{2,1,0:T(8,128)S(1)} %copy.35) | copy-start | bytes 92164
  102.2 1.2 copy-start.8
  103.4 0.7 copy-start.17
  113.4 0.7 copy-start.4
  114.2 0.7 copy-start.12
  114.8 0.9 copy-start.15
  115.8 0.9 copy-start.16
  291.6 157.6 %copy-start.1 = (s32[1,640,2]{2,1,0:T(8,128)S(1)}, s32[1,640,2]{2,1,0:T(8,128)}, u32[]{:S(2)}) copy-start(s32[1,640,2]{2,1,0:T(8,128)} %copy.34) | copy-start | bytes 15364
  291.6 157.6 %copy-start.3 = (s32[640,128]{1,0:T(8,128)S(1)}, s32[640,128]{1,0:T(8,128)}, u32[]{:S(2)}) copy-start(s32[640,128]{1,0:T(8,128)} %get-tuple-element.69.codes_ref) | copy-start | bytes 983044
  291.6 157.6 %copy-start.5 = (f32[640,128]{1,0:T(8,128)S(1)}, f32[640,128]{1,0:T(8,128)}, u32[]{:S(2)}) copy-start(f32[640,128]{1,0:T(8,128)} %copy-done.4) | copy-start | bytes 983044
  449.1 1.4 copy-start.2
  450.5 1.2 copy-start.7
  451.8 1.2 copy-start.9
  453.0 0.7 copy-start.11
  453.7 14.9 %copy-start.18 = (f32[640,12]{1,0:T(8,128)S(1)}, f32[640,12]{1,0:T(8,128)}, u32[]{:S(2)}) copy-start(f32[640,12]{1,0:T(8,128)} %get-tuple-element.102) | copy-start | bytes 92164

commit v5 on v4

--- a/solution.py
+++ b/solution.py
@@ -257,9 +257,10 @@
 
 
 def slot_codes(routes_ref, codes_ref, codes_row_ref):
-    rows = routes_ref.shape[0]
+    rows = routes_ref.shape[1]
     half_slots = rows // NFFN
-    routes = routes_ref[...]
+    turned = jnp.concatenate([routes_ref[...].astype(jnp.float32), jnp.zeros((126, rows), jnp.float32)], 0).T
+    routes = turned.astype(jnp.int32)
     lanes = lax.broadcasted_iota(jnp.int32, (rows, 128), 1)
     matches = [
         jnp.where((lanes == routes[:, c : c + 1]) & (lanes < NFFN), 1.0, 0.0).astype(jnp.float32) for c in range(2)
@@ -275,7 +276,7 @@
         route = routes[:, c : c + 1].astype(jnp.float32)
         late = jnp.where(rank >= half_slots, float((NFFN - 1) * half_slots), 0.0)
         code = jnp.where(route < NFFN, route * half_slots + rank + late, float(4 * rows))
-        codes = jnp.where(lanes == c, code, codes)
+        codes = jnp.where(lanes == c, code, jnp.where(lanes == 2 + c, route, codes))
     codes_ref[...] = codes.astype(jnp.int32)
     codes_row_ref[...] = codes.T[:8].astype(jnp.int32)
 
@@ -464,7 +465,7 @@
             sems(chunks, owners - 1), sems(chunks, owners - 1), sems(chunks, owners - 1), sems(chunks, owners - 1),
             sems(3, copies), sems(3, copies), sems(4 * chunks),
         ],
-        compiler_params=pltpu.CompilerParams(vmem_limit_bytes=56 * MIB, collective_id=1, has_side_effects=True),
+        compiler_params=pltpu.CompilerParams(vmem_limit_bytes=63 * MIB, collective_id=1, has_side_effects=True),
         cost_estimate=cost(1e10, 5e7),
     )(tokens, table, *weights, parents, routes, *shards)
 
@@ -475,12 +476,12 @@
 
 def middle_kernel(
     tokens_ref, attended_ref, out_weight_ref, table_ref, router_ref, constant_ref, prior_ref, prior_weight_ref,
-    routes_ref, codes_ref, resid_ref, small_ref, first_ref, second_ref, mixer_ref, hidden_ref,
+    codes_ref, codes_row_ref, resid_ref, small_ref, first_ref, second_ref, mixer_ref, hidden_ref,
 ):
     rows, width = tokens_ref.shape
-    mixer_ref[...] = jnp.concatenate(
-        [router_ref[...], constant_ref[...], jnp.zeros((width, 128 - NEXP - 4), jnp.bfloat16)], 1
-    )
+    mixer = [ref[...].astype(jnp.float32) for ref in (router_ref, constant_ref)]
+    mixer_ref[...] = jnp.concatenate([*mixer, jnp.zeros((128 - NEXP - 4, width), jnp.float32)], 0).astype(jnp.bfloat16)
+    missing = jnp.zeros((16 - NEXP, SEG), jnp.float32)
 
     @pl.loop(0, rows // SEG)
     def _(step):
@@ -491,13 +492,12 @@
         hidden = (resid * inverse * table_ref[1:2, :]).astype(jnp.bfloat16)
         resid_ref[span, :] = resid
         hidden_ref[span, :] = hidden
-        logits = dot_nn(hidden, mixer_ref[...])
-        carried = jnp.dot(
-            prior_ref[span, :], prior_weight_ref[...], precision=precise, preferred_element_type=jnp.float32
-        )
+        logits = dot_nt(hidden, mixer_ref[...])
+        prior = jnp.concatenate([prior_ref[:, span], missing], 0).T[:, :NEXP]
+        carried = jnp.dot(prior, prior_weight_ref[...], precision=precise, preferred_element_type=jnp.float32)
         logits = logits + jnp.concatenate([carried, jnp.zeros((SEG, 128 - NEXP), jnp.float32)], 1)
         lanes = lax.broadcasted_iota(jnp.int32, logits.shape, 1)
-        routes = routes_ref[span, :]
+        routes = codes_ref[span, 2:4]
         columns = []
         pairs = [[lane_pick(logits, lanes, routes[:, c : c + 1]) for c in range(2)]]
         pairs += [[logits[:, NEXP + 2 * m + c : NEXP + 2 * m + c + 1] for c in range(2)] for m in range(2)]
@@ -514,11 +514,11 @@
     slots = first_ref.shape[0]
     for half, ref in enumerate((first_ref, second_ref)):
         index = lax.broadcasted_iota(jnp.int32, (slots, rows), 0) + half * slots
-        chosen = (codes_ref[0:1, :] == index) | (codes_ref[1:2, :] == index)
+        chosen = (codes_row_ref[0:1, :] == index) | (codes_row_ref[1:2, :] == index)
         ref[...] = dot_nn(chosen.astype(jnp.bfloat16), hidden_ref[...]).astype(jnp.bfloat16)
 
 
-def middle(tokens, attended, out_weight, table, router, constant, prior, prior_weight, routes, codes_row):
+def middle(tokens, attended, out_weight, table, router, constant, prior, prior_weight, codes, codes_row):
     rows, width = tokens.shape
     slots = rows
     return pl.pallas_call(
@@ -528,12 +528,12 @@
             jax.ShapeDtypeStruct((rows, 128), jnp.float32),
             jax.ShapeDtypeStruct((slots, width), jnp.bfloat16),
             jax.ShapeDtypeStruct((slots, width), jnp.bfloat16),
-            jax.ShapeDtypeStruct((width, 128), jnp.bfloat16),
+            jax.ShapeDtypeStruct((128, width), jnp.bfloat16),
         ),
         scratch_shapes=[pltpu.VMEM((rows, width), jnp.bfloat16)],
-        compiler_params=params(48),
+        compiler_params=params(63),
         cost_estimate=cost(4 * rows * width * width + 4 * rows * rows * width, 1e7),
-    )(tokens, attended, out_weight, table, router, constant, prior, prior_weight, routes, codes_row)
+    )(tokens, attended, out_weight, table, router, constant, prior, prior_weight, codes, codes_row)
 
 
 def plane_partners(owners):
@@ -753,8 +753,22 @@
     return dot(high, right) + dot(low, right)
 
 
+def put_part(ref, values, begin):
+    _, chips, owners, tall, half = ref.shape
+    end = begin + values.shape[1]
+    for core in range(2):
+        low, high = max(begin, core * half), min(end, (core + 1) * half)
+        if low < high:
+            for z in range(owners):
+                for chip in range(chips):
+                    row = (z * chips + chip) * tall
+                    ref[core, chip, z, :, low - core * half : high - core * half] = values[
+                        row : row + tall, low - begin : high - begin
+                    ]
+
+
 def turn_kernel(
-    resid_ref, small_ref, grad_ref, prior_ref, routes_ref, codes_ref, returned_ref, dots_ref, table_ref,
+    resid_ref, small_ref, grad_ref, prior_ref, codes_ref, returned_ref, dots_ref, table_ref,
     mixer_ref, prior_weight_ref, out_weight_ref, attended_ref, f_ref, gate_ref,
     resid_grad_ref, grads_ref, out_grad_ref, prior_grad_ref, f_got, gate_first,
     back_ref, sums_ref, prior_sums_ref, extra_ref, f_send, f_recv, gate_send, gate_recv, *, owners, reduce,
@@ -787,7 +801,8 @@
     def _(step):
         span = pl.ds(pl.multiple_of(step * SEG, SEG), SEG)
         small = small_ref[span, :]
-        routes, codes = routes_ref[span, :], codes_ref[span, :]
+        codes = codes_ref[span, :]
+        routes = codes[:, 2:4]
         gates = [small[:, c : c + 1] for c in range(2)]
         mixing = [[small[:, 2 + 2 * m + c : 3 + 2 * m + c] for c in range(2)] for m in range(2)]
         inverse = small[:, 6:7]
@@ -829,11 +844,11 @@
             for c in range(2):
                 scores = jnp.where(lanes == NEXP + 2 * m + c, mixing[m][c] * (pair[c] - mean), scores)
             direct = direct + mixing[m][0] * to_mix[m]
-        prior_grad_ref[span, :] = lax.dot_general(
-            logit_grads[:, :NEXP], prior_weight_ref[...], (((1,), (1,)), ((), ())),
+        prior_grad_ref[:, span] = lax.dot_general(
+            prior_weight_ref[...], logit_grads[:, :NEXP], (((1,), (1,)), ((), ())),
             precision=precise, preferred_element_type=jnp.float32,
         )
-        hidden_grads = split_dot(dot_nt, scores, mixer_ref[...]) + direct * grad + routed
+        hidden_grads = split_dot(dot_nn, scores, mixer_ref[...]) + direct * grad + routed
         scaled = hidden_grads * gain
         resid_grads = inverse * (scaled - normed * jnp.mean(scaled * normed, -1, keepdims=True)) + grad
         resid_grad_ref[span, :] = resid_grads
@@ -845,7 +860,7 @@
         sums_ref[16:24, :] += split_dot(dot_nn, weights.T[0:8], grad_b)
         sums_ref[24:32, :] += jnp.sum((hidden_grads * normed).reshape(SEG // 8, 8, width), 0)
         prior_sums_ref[...] += jnp.dot(
-            prior_ref[span, :].T,
+            prior_ref[:, span],
             jnp.concatenate([logit_grads[:, 96:], logit_grads[:, :96]], 1),
             precision=precise,
             preferred_element_type=jnp.float32,
@@ -856,27 +871,27 @@
     kept = NEXP // owners
     for z in range(owners):
         extra_ref[pl.ds(z * (width // owners), kept), :] += prior_sums_ref[z * kept : (z + 1) * kept, :]
-    out_grad_ref[:, width : width + 128] = extra_ref[...].astype(jnp.bfloat16)
-    out_grad_ref[:, width + 128 :] = jnp.zeros((width, 128), jnp.bfloat16)
+    small_part = jnp.concatenate([extra_ref[...], jnp.zeros((width, 128), jnp.float32)], 1).astype(jnp.bfloat16)
+    put_part(out_grad_ref, small_part, width)
     back = back_ref[...]
     grads_ref[...] = dot_nt(out_weight_ref[...], back).astype(jnp.bfloat16)
-    out_grad_ref[:, :width] = dot_nn(attended_ref[...], back).astype(jnp.bfloat16)
+    put_part(out_grad_ref, dot_nn(attended_ref[...], back).astype(jnp.bfloat16), 0)
     for copy in copies:
         copy.wait()
 
 
-def turn(resid, small, grad, prior, routes, codes, returned, dots, table, mixer, prior_weight, out_weight, attended, f, gate):
+def turn(resid, small, grad, prior, codes, returned, dots, table, mixer, prior_weight, out_weight, attended, f, gate):
     rows, width = resid.shape
     owners = lax.axis_size("expert")
     vmem, hbm = pl.BlockSpec(memory_space=pltpu.VMEM), pl.BlockSpec(memory_space=pl.ANY)
     return pl.pallas_call(
         functools.partial(turn_kernel, owners=owners, reduce=relayed(gate.shape[0])),
-        in_specs=[vmem] * 13 + [hbm] * 2,
+        in_specs=[vmem] * 12 + [hbm] * 2,
         out_specs=(vmem, vmem, vmem, vmem, hbm, hbm),
         out_shape=(
             jax.ShapeDtypeStruct((rows, width), jnp.float32),
             jax.ShapeDtypeStruct((width, rows), jnp.bfloat16),
-            jax.ShapeDtypeStruct((width, width + 256), jnp.bfloat16),
+            jax.ShapeDtypeStruct((2, 4, owners, width // owners // 4, (width + 256) // 2), jnp.bfloat16),
             jax.ShapeDtypeStruct(prior.shape, jnp.float32),
             jax.ShapeDtypeStruct(f.shape, f.dtype),
             jax.ShapeDtypeStruct((4, *gate.shape[1:]), gate.dtype),
@@ -884,29 +899,44 @@
         scratch_shapes=[
             pltpu.VMEM((rows, width), jnp.bfloat16),
             pltpu.VMEM((32, width), jnp.float32),
-            pltpu.VMEM((prior.shape[1], 128), jnp.float32),
+            pltpu.VMEM((prior.shape[0], 128), jnp.float32),
             pltpu.VMEM((width, 128), jnp.float32),
             pltpu.SemaphoreType.DMA((2 * owners,)),
             pltpu.SemaphoreType.DMA((2 * owners,)),
             pltpu.SemaphoreType.DMA((4,)),
             pltpu.SemaphoreType.DMA((4,)),
         ],
-        compiler_params=pltpu.CompilerParams(vmem_limit_bytes=60 * MIB, collective_id=4, has_side_effects=True),
+        compiler_params=pltpu.CompilerParams(vmem_limit_bytes=63 * MIB, collective_id=4, has_side_effects=True),
         cost_estimate=cost(4 * rows * width * width + 4 * rows * rows * width, 1.5e7),
-    )(resid, small, grad, prior, routes, codes, returned, dots, table, mixer, prior_weight, out_weight, attended, f, gate)
+    )(resid, small, grad, prior, codes, returned, dots, table, mixer, prior_weight, out_weight, attended, f, gate)
 
 
 def finish_kernel(
-    resid_ref, small_ref, routes_ref, codes_ref, fa_ref, fb_ref, table_ref, totals_ref, *refs, owners
+    resid_ref, small_ref, codes_ref, fa_ref, fb_ref, table_ref, totals_ref, tokens_grad_ref, *refs, owners, count, reduce
 ):
-    count = (len(refs) - 11) // 3
-    sources, targets, refs = refs[:count], refs[count : 2 * count], refs[2 * count :]
-    out_ref, *weight_refs, router_ref, prior_ref, constant_ref, rows_ref = refs[:9]
-    held, (load_sem, store_sem) = refs[9:-2], refs[-2:]
-    loads = [pltpu.make_async_copy(one, two, load_sem.at[i]) for i, (one, two) in enumerate(zip(sources, held))]
-    stores = [pltpu.make_async_copy(one, two, store_sem.at[i]) for i, (one, two) in enumerate(zip(held, targets))]
-    for move in loads:
-        move.start()
+    experts, refs = refs[: 3 * count], refs[3 * count :]
+    tokens_grad_out, *expert_outs = refs[:4]
+    out_ref, *weight_refs, router_ref, prior_ref, constant_ref, vector_ref, gains_ref = refs[4:14]
+    held, *work = refs[14:-2]
+    load_sem, store_sem = refs[-2:]
+    core = lax.axis_index("core")
+    place = lax.axis_index("xy") * 2 + core
+    load = pltpu.make_async_copy(tokens_grad_ref, held, load_sem.at[0])
+    loads = []
+    for i in range(3):
+        if reduce:
+            piece, first, got = experts[3 * i : 3 * i + 3]
+            items = (piece.at[place], first.at[core], got.at[4 + core], got.at[6], got.at[7], got.at[5 - core])
+        else:
+            items = (experts[i],)
+        for n, item in enumerate(items):
+            target = work[2 * i].at[n] if reduce else work[2 * i + 1]
+            loads.append((i, pltpu.make_async_copy(item, target, load_sem.at[1 + 6 * i + n])))
+    load.start()
+    for _, item in loads:
+        item.start()
+    stores = [pltpu.make_async_copy(held, tokens_grad_out, store_sem.at[0])]
+    stores += [pltpu.make_async_copy(work[2 * i + 1], expert_outs[i], store_sem.at[1 + i]) for i in range(3)]
     rows, width = resid_ref.shape
     half = fa_ref.shape[0]
 
@@ -914,7 +944,8 @@
     def _(step):
         span = pl.ds(pl.multiple_of(step * SEG, SEG), SEG)
         small = small_ref[span, :]
-        routes, codes = routes_ref[span, :], codes_ref[span, :]
+        codes = codes_ref[span, :]
+        routes = codes[:, 2:4]
         resid = resid_ref[span, :]
         hidden = resid * small[:, 6:7] * table_ref[1:2, :]
         index = lax.broadcasted_iota(jnp.int32, (SEG, 2 * half), 1)
@@ -932,55 +963,73 @@
                 total = total + mixed * small[:, 3 + 2 * m : 4 + 2 * m] * table_ref[2 + m : 3 + m, :]
         out_ref[span, :] = (total + direct * hidden).astype(jnp.bfloat16)
 
-    for load, store in zip(loads, stores):
-        load.wait()
-        store.start()
-    heads_width = owners * HEAD_DIM
+    load.wait()
+    stores[0].start()
+    for i in range(3):
+        for index, item in loads:
+            if index == i:
+                item.wait()
+        if reduce:
+            wide = work[2 * i + 1]
+            for n in range(2):
+                wide[core if n == 0 else 1 - core] = jnp.sum(work[2 * i][3 * n : 3 * n + 3].astype(jnp.float32), 0)
+        stores[1 + i].start()
+    span = owners * HEAD_DIM
+    chunks = width // span
+    offsets, _ = part_columns(width, chunks)
     for i, ref in enumerate(weight_refs[:3]):
-        for p in range(1, totals_ref.shape[0]):
-            ref[:, (p - 1) * heads_width : p * heads_width] = totals_ref[
-                p, :, i * heads_width : (i + 1) * heads_width
-            ].astype(jnp.float32)
-    weight_refs[3][...] = totals_ref[0, :, :width].astype(jnp.float32)
-    extra = totals_ref[0, :, width : width + 128].astype(jnp.float32)
-    router_ref[...] = extra[:, :NEXP]
-    constant_ref[...] = extra[:, NEXP : NEXP + 4]
+        for j in range(chunks):
+            begin = offsets[j + 1] + i * span if j < chunks - 1 or i < 2 else offsets[-1]
+            ref[:, j * span : (j + 1) * span] = totals_ref[:, begin : begin + span].astype(jnp.float32)
+    weight_refs[3][...] = totals_ref[:, :width].astype(jnp.float32)
+    extra = totals_ref[:, width : width + 128].astype(jnp.float32)
     prior_ref[...] = extra[: NEXP // owners, 32 : 32 + NEXP]
     turned = extra.T
-    gains = totals_ref[totals_ref.shape[0] - 1, :, width : width + 128].astype(jnp.float32).T
-    rows_ref[0:2, :] = turned[16:18]
-    rows_ref[2:3, :] = turned[24:25]
-    rows_ref[3:4, :] = gains[0:1]
-    rows_ref[4:8, :] = jnp.zeros((4, rows_ref.shape[1]), jnp.float32)
+    router_ref[...] = turned[:NEXP]
+    constant_ref[...] = turned[NEXP : NEXP + 4]
+    vector_ref[...] = turned[16:18]
+    begin = offsets[-1] + span
+    gains = totals_ref[:, begin : begin + 128].astype(jnp.float32).T
+    member = lax.axis_index("expert")
+    share = router_ref.shape[1]
+    own_gain = table_ref[0:1, :share]
+    for z in range(1, owners):
+        own_gain = jnp.where(member == z, table_ref[0:1, z * share : (z + 1) * share], own_gain)
+    gains_ref[0:1, :] = gains[0:1] / own_gain
+    gains_ref[1:2, :] = turned[24:25]
     for move in stores:
         move.wait()
 
 
-def finish(resid, small, routes, codes, outs, table, totals, moved):
+def finish(resid, small, codes, outs, table, totals, tokens_grad, experts, reduce):
     rows, width = resid.shape
     owners = lax.axis_size("expert")
     share = width // owners
     vmem, hbm = pl.BlockSpec(memory_space=pltpu.VMEM), pl.BlockSpec(memory_space=pl.ANY)
     shape = lambda *dims: jax.ShapeDtypeStruct(dims, jnp.float32)
-    count = len(moved)
+    count = 3 if reduce else 1
+    shapes = [item.shape[1:] for item in experts[count - 1 :: count]]
+    work = []
+    for dims in shapes:
+        work += [pltpu.VMEM((6 if reduce else 1, *dims), jnp.bfloat16), pltpu.VMEM((2, *dims), jnp.float32)]
     return pl.pallas_call(
-        functools.partial(finish_kernel, owners=owners),
-        in_specs=[vmem] * 8 + [hbm] * count,
-        out_specs=(hbm,) * count + (vmem,) * 9,
+        functools.partial(finish_kernel, owners=owners, count=count, reduce=reduce),
+        in_specs=[vmem] * 7 + [hbm] * (1 + len(experts)),
+        out_specs=(hbm,) * 4 + (vmem,) * 10,
         out_shape=(
-            *(jax.ShapeDtypeStruct(item.shape, item.dtype) for item in moved),
+            shape(rows, width),
+            *(shape(2, *dims) for dims in shapes),
             jax.ShapeDtypeStruct((rows, width), jnp.bfloat16),
             *(shape(share, width),) * 4,
-            shape(share, NEXP), shape(NEXP // owners, NEXP), shape(share, 4), shape(8, share),
+            shape(NEXP, share), shape(NEXP // owners, NEXP), shape(4, share), shape(2, share), shape(2, share),
         ),
         scratch_shapes=[
-            *(pltpu.VMEM(item.shape, item.dtype) for item in moved),
-            pltpu.SemaphoreType.DMA((count,)),
-            pltpu.SemaphoreType.DMA((count,)),
+            pltpu.VMEM((rows, width), jnp.float32), *work,
+            pltpu.SemaphoreType.DMA((19,)), pltpu.SemaphoreType.DMA((4,)),
         ],
-        compiler_params=params(48),
+        compiler_params=params(63),
         cost_estimate=cost(8 * rows * rows * width, 8e6),
-    )(resid, small, routes, codes, *outs, table, totals, *moved)
+    )(resid, small, codes, *outs, table, totals, tokens_grad, *experts)
 
 
 def attend_back_phase_kernel(
@@ -988,10 +1037,12 @@
     query_ref, key_ref, value_ref, resid_grad_ref, out_part_ref, f_ref, gate_ref, up_ref, down_ref, gate_first,
     tokens_grad_ref, f_got, gate_got, up_got, down_got, *rest, reduce,
 ):
+    chunks, owners, _, rows = grads_ref.shape
+    width = tokens_ref.shape[1]
     if reduce:
-        total_ref, gate_out, up_out, down_out, *rest = rest
+        total_ref, *rest = rest
     else:
-        parts_ref, *rest = rest
+        flat_ref, *rest = rest
     (
         d_got, back_sent, back_got, normed_turned, turned_ref, back_sum, column_ref,
         qt_ref, kt_ref, dt_ref, q_ref, k_ref, v_ref, d_ref, delta_ref, dq_ref, dk_ref, dv_ref, triangle,
@@ -999,12 +1050,14 @@
     ) = rest
     if reduce:
         (
-            parts_ref, half_got, chip_got, chip_sum, ring_got, ring_sum, all_got,
             half_send, half_recv, chip_send, chip_recv, ring_send, ring_recv, all_send, all_recv,
-            gate_work, gate_sums, up_sums, gate_wide, down_work, down_sums, down_wide, work_sem, wide_sem,
+            gate_work, gate_sums, up_sums, down_work, down_sums, work_sem, *rest,
         ) = rest
-    chunks, owners, _, rows = grads_ref.shape
-    width = tokens_ref.shape[1]
+        count = len(part_columns(width, chunks)[1])
+        own_parts, half_got, chip_got, chip_sum, ring_got, ring_sum, all_got = (
+            rest[max(0, n * count - 1) : (n + 1) * count - 1] for n in range(7)
+        )
+        parts = [out_part_ref, *own_parts]
     copies = gate_ref.shape[0]
     member, xy, core = (lax.axis_index(name) for name in ("expert", "xy", "core"))
     place = xy * 2 + core
@@ -1028,93 +1081,77 @@
     inverse = lax.rsqrt(jnp.mean(inputs * inputs, -1, keepdims=True) + epsilon)
     normed_turned[...] = (inputs * inverse * table_ref[0:1, :]).T.astype(jnp.bfloat16)
     share = width // owners
-    part_shape = (owners, share // 48, 48)
+
+    offsets, sizes = part_columns(width, chunks)
 
     def fill(p, values, begin, size):
         if reduce:
-            parts_ref[p, :, :, :, begin : begin + size] = values.reshape(*part_shape, size)
+            put_part(parts[p], values, begin)
         else:
-            parts_ref[p, :, begin : begin + size] = values
-
-    columns_total = parts_ref.shape[-1]
-    early = [
-        pltpu.make_async_copy(resid_grad_ref, tokens_grad_ref, early_sem.at[0]),
-        pltpu.make_async_copy(out_part_ref, parts_ref.at[0], early_sem.at[1]),
-    ]
-    for copy in early:
-        copy.start()
-    fill(chunks, jnp.zeros((width, 128), jnp.bfloat16), width + 128, columns_total - width - 128)
+            begin = offsets[p] + begin
+            flat_ref[:, begin : begin + size] = values
+
+    early = pltpu.make_async_copy(resid_grad_ref, tokens_grad_ref, early_sem.at[0])
+    early.start()
+    last_part = len(sizes) - 1
+    fill(last_part, jnp.zeros((width, 128), jnp.bfloat16), sizes[-1] - 128, 128)
 
     stages = {}
 
-    def half_of(p):
-        return (columns_total if p in (0, chunks) else width) // 2
-
     def over_cores(p):
-        half = half_of(p)
-        away = pl.ds(pl.multiple_of((1 - core) * half, 128), half)
-        copy = remote(
-            parts_ref.at[p, :, :, :, away], half_got.at[p, :, :, :, pl.ds(0, half)], half_send.at[p], half_recv.at[p], {"core": 1 - core}
-        )
+        copy = remote(parts[p].at[1 - core], half_got[p], half_send.at[p], half_recv.at[p], {"core": 1 - core})
         copy.start()
         stages[p, 0] = [copy]
 
     def over_chips(p):
         for copy in stages[p, 0]:
             copy.wait_recv()
-        half = half_of(p)
-        mine, near = pl.ds(pl.multiple_of(core * half, 128), half), pl.ds(0, half)
-        half_got[p, :, :, :, near] = (
-            parts_ref[p, :, :, :, mine].astype(jnp.float32) + half_got[p, :, :, :, near].astype(jnp.float32)
-        ).astype(jnp.bfloat16)
+        half_got[p][...] = (parts[p][core].astype(jnp.float32) + half_got[p][...].astype(jnp.float32)).astype(
+            jnp.bfloat16
+        )
         stages[p, 1] = []
         for step in (3, 1, 2):
             index = lax.rem(xy + step, 4)
             copy = remote(
-                half_got.at[p, :, index, :, near], chip_got.at[p, xy, :, :, near], chip_send.at[p, step - 1], chip_recv.at[p, step - 1],
-                {"xy": index},
+                half_got[p].at[index], chip_got[p].at[xy],
+                chip_send.at[p, step - 1], chip_recv.at[p, step - 1], {"xy": index},
             )
             copy.start()
             stages[p, 1].append(copy)
-        chip_got[p, xy, :, :, near] = half_got[p, :, xy, :, near]
+        chip_got[p][xy] = half_got[p][xy]
 
     def over_owners(p):
         for copy in stages[p, 1]:
             copy.wait_recv()
-        near = pl.ds(0, half_of(p))
-        chip_sum[p, :, :, near] = jnp.sum(chip_got[p, :, :, :, near].astype(jnp.float32), 0).astype(jnp.bfloat16)
+        chip_sum[p][...] = jnp.sum(chip_got[p][...].astype(jnp.float32), 0).astype(jnp.bfloat16)
         stages[p, 2] = []
         for step, index, device in ring:
             copy = remote(
-                chip_sum.at[p, index, :, near], ring_got.at[p, member, :, near], ring_send.at[p, step - 1], ring_recv.at[p, step - 1],
-                device,
+                chip_sum[p].at[index], ring_got[p].at[member],
+                ring_send.at[p, step - 1], ring_recv.at[p, step - 1], device,
             )
             copy.start()
             stages[p, 2].append(copy)
-        ring_got[p, member, :, near] = chip_sum[p, member, :, near]
+        ring_got[p][member] = chip_sum[p][member]
 
     def to_copies(p):
         for copy in stages[p, 2]:
             copy.wait_recv()
-        half = half_of(p)
-        mine, near = pl.ds(pl.multiple_of(core * half, 128), half), pl.ds(0, half)
-        ring_sum[p, :, near] = jnp.sum(ring_got[p, :, :, near].astype(jnp.float32), 0).astype(jnp.bfloat16)
+        ring_sum[p][...] = jnp.sum(ring_got[p][...].astype(jnp.float32), 0).astype(jnp.bfloat16)
         stages[p, 3] = []
         for step, _, device in others:
             copy = remote(
-                ring_sum.at[p, :, near], all_got.at[p, xy, :, mine], all_send.at[p, step - 1], all_recv.at[p, step - 1], device
+                ring_sum[p], all_got[p].at[xy, core], all_send.at[p, step - 1], all_recv.at[p, step - 1], device
             )
             copy.start()
             stages[p, 3].append(copy)
-        all_got[p, xy, :, mine] = ring_sum[p, :, near]
+        all_got[p][xy, core] = ring_sum[p][...]
 
     def advance(*pairs):
         if reduce:
             for stage, p in pairs:
                 (over_cores, over_chips, over_owners, to_copies)[stage](p)
 
-    for copy in early:
-        copy.wait()
     advance((0, 0))
 
     background = []
@@ -1136,12 +1173,15 @@
 
     beside, behind, across = plane_chips(xy)
     landed = {}
+    sent = []
 
     def relay(i, source, landing, device):
-        target = landing_ref(i, landing)
-        copy = remote(source, target, weight_send.at[i, landing], weight_recv.at[i, landing], device)
+        copy = remote(
+            source, landing_ref(i, landing), weight_send.at[i, landing], weight_recv.at[i, landing], device
+        )
         copy.start()
         landed[i, landing] = copy
+        sent.append(copy)
 
     def landing_ref(i, landing):
         return gate_first.at[landing] if i == 0 and landing < 4 else pieces[i][1].at[landing]
@@ -1155,51 +1195,30 @@
         for piece, landing, chip in first_hops(beside, behind, across):
             relay(i, pieces[i][0].at[piece], landing, {"xy": chip})
 
-    def buffers(i):
-        if i < 2:
-            return gate_work, (gate_sums, up_sums)[i], gate_wide, (gate_out, up_out)[i]
-        return down_work, down_sums, down_wide, down_out
-
-    def load(i, items):
-        work = buffers(i)[0]
+    def second_hop(i):
+        source, target = pieces[i]
+        work, sums = (gate_work, (gate_sums, up_sums)[i]) if i < 2 else (down_work, down_sums)
+        arrive(i, 2, 3)
+        items = (source.at[behind * 2], landing_ref(i, 2), source.at[beside * 2 + 1], landing_ref(i, 3))
         loads = [pltpu.make_async_copy(ref, work.at[n], work_sem.at[n]) for n, ref in enumerate(items)]
         for item in loads:
             item.start()
+        arrive(i, 0, 1)
+        other = {"core": 1 - core}
+        relay(i, source.at[xy * 2 + 1 - core], 6, other)
+        relay(i, (gate_first if i == 0 else target).at[1 - core], 7, other)
         for item in loads:
             item.wait()
-
-    def second_hop(i):
-        source = pieces[i][0]
-        work, sums = buffers(i)[:2]
-        arrive(i, 2, 3)
-        load(i, (source.at[behind * 2], landing_ref(i, 2), source.at[beside * 2 + 1], landing_ref(i, 3)))
-        for n, device in enumerate(({"xy": behind}, {"xy": beside})):
+        for n, device in enumerate(({"xy": behind, "core": 0}, {"xy": beside, "core": 1})):
             sums[n] = (work[2 * n].astype(jnp.float32) + work[2 * n + 1].astype(jnp.float32)).astype(jnp.bfloat16)
-            relay(i, sums.at[n], 4 + n, device)
-
-    def core_hop(i):
-        source = pieces[i][0]
-        work, sums, wide, out = buffers(i)
-        arrive(i, 0, 1, 4, 5)
-        got = [landing_ref(i, landing) for landing in (0, 4, 1, 5)]
-        load(i, (source.at[xy * 2], got[0], got[1], source.at[xy * 2 + 1], got[2], got[3]))
-        if i == 1:
-            store(0).wait()
-        totals = [jnp.sum(work[3 * n : 3 * n + 3].astype(jnp.float32), 0) for n in range(2)]
-        wide[core] = jnp.where(core == 0, totals[0], totals[1])
-        sums[2] = jnp.where(core == 0, totals[1], totals[0]).astype(jnp.bfloat16)
-        relay(i, sums.at[2], 6, {"core": 1 - core})
-
-    def store(i):
-        wide, out = buffers(i)[2:]
-        return pltpu.make_async_copy(wide, out, wide_sem.at[i])
-
-    def finish(i):
-        work, sums, wide, out = buffers(i)
-        arrive(i, 6)
-        load(i, (landing_ref(i, 6),))
-        wide[1 - core] = work[0].astype(jnp.float32)
-        store(i).start()
+            copy = remote(
+                sums.at[n], target.at[4 + core], weight_send.at[i, 4 + n], weight_recv.at[i, 4 + core], device
+            )
+            copy.start()
+            sent.append(copy)
+            landed[i, 4 + n] = remote(
+                sums.at[n], target.at[4 + n], weight_send.at[i, 4 + n], weight_recv.at[i, 4 + n], device
+            )
 
     if reduce:
         for i in (1, 2):
@@ -1217,46 +1236,62 @@
             back_sent.at[j], qt_ref, kt_ref, dt_ref, q_ref, k_ref, v_ref, d_ref, delta_ref, dq_ref, dk_ref, dv_ref,
             triangle,
         )
-        local = pltpu.make_async_copy(back_sent.at[j, member], back_got.at[j, member], local_sem.at[chunks + j])
-        local.start()
-        group = []
-        for step, index, device in ring:
-            copy = remote(
-                back_sent.at[j, index], back_got.at[j, member],
-                back_send.at[j, step - 1], back_recv.at[j, step - 1], device,
-            )
-            copy.start()
-            group.append(copy)
-        return local, group
+
+    def send_back(j, cuts):
+        local = None
+        if cuts[0][1] == 0:
+            local = pltpu.make_async_copy(back_sent.at[j, member], back_got.at[j, member], local_sem.at[chunks + j])
+            local.start()
+        groups = []
+        for slot, begin, size in cuts:
+            span = pl.ds(begin, size)
+            group = []
+            for step, index, device in ring:
+                copy = remote(
+                    back_sent.at[j, index, span], back_got.at[j, member, span],
+                    back_send.at[slot, step - 1], back_recv.at[slot, step - 1], device,
+                )
+                copy.start()
+                group.append(copy)
+            groups.append(group)
+        return local, groups
 
     span_width = owners * HEAD_DIM
 
-    def weights_of(j, group):
+    def weights_of(j, group, types=(0, 1, 2)):
         local, copies_in = group
-        local.wait()
-        for copy in copies_in:
+        if 0 in types:
+            local.wait()
+        for copy in copies_in[1 if 0 not in types else 0]:
             copy.wait_recv()
-        for i in range(3):
+        total = None
+        for i in types:
             for z in range(owners):
                 row = i * span_width + z * HEAD_DIM
                 turned_ref[row : row + HEAD_DIM, :] = back_got[j, z, i * HEAD_DIM : (i + 1) * HEAD_DIM]
-        total = None
-        for i, weight in enumerate((query_ref, key_ref, value_ref)):
-            term = dot_nn(weight[:, j * span_width : (j + 1) * span_width], turned_ref[i * span_width : (i + 1) * span_width, :])
+            weight = (query_ref, key_ref, value_ref)[i]
+            term = dot_nn(
+                weight[:, j * span_width : (j + 1) * span_width], turned_ref[i * span_width : (i + 1) * span_width, :]
+            )
             total = term if total is None else total + term
-        back_sum[...] = total if j == 0 else back_sum[...] + total
+        first = j == 0 and 0 in types
+        back_sum[...] = total if first else back_sum[...] + total
         column = jnp.sum(total * normed_turned[...].astype(jnp.float32), -1, keepdims=True)
-        column_ref[...] = column if j == 0 else column_ref[...] + column
-        if j == chunks - 1:
-            fill(chunks, jnp.broadcast_to(column_ref[...], (width, 128)).astype(jnp.bfloat16), width, 128)
-        fill(j + 1, dot_nt(normed_turned[...], turned_ref[...]).astype(jnp.bfloat16), 0, 3 * span_width)
-
-    def send_f():
-        expert = member * 2 + core
-        local = pltpu.make_async_copy(f_ref.at[expert], f_got.at[expert], f_send.at[0])
-        local.start()
-        background.append(local.wait)
-        for step, index, device in planes:
+        column_ref[...] = column if first else column_ref[...] + column
+        begin, size = types[0] * span_width, len(types) * span_width
+        part = j + 1 if 0 in types else j + 2
+        if part == last_part:
+            fill(part, jnp.broadcast_to(column_ref[...], (width, 128)).astype(jnp.bfloat16), span_width, 128)
+        fill(part, dot_nt(normed_turned[...], turned_ref[begin : begin + size, :]).astype(jnp.bfloat16), 0, size)
+
+    expert = member * 2 + core
+
+    def send_f(distance):
+        if distance == 0:
+            local = pltpu.make_async_copy(f_ref.at[expert], f_got.at[expert], f_send.at[0])
+            local.start()
+            background.append(local.wait)
+        for step, index, device in planes[3 * distance : 3 * distance + 3]:
             copy = remote(f_ref.at[index], f_got.at[expert], f_send.at[step], f_recv.at[step], device)
             copy.start()
             background.append(copy.wait)
@@ -1265,54 +1300,68 @@
         if reduce:
             step(i)
 
-    groups = [head(0)]
+    part_k, part_v = chunks, chunks + 1
+    both = 2 * HEAD_DIM
+    head(0)
+    groups = [send_back(0, [(0, 0, 3 * HEAD_DIM)])]
     expert_step(second_hop, 0)
-    groups.append(head(1))
     advance((1, 0))
+    head(1)
+    advance((2, 0))
+    groups.append(send_back(1, [(1, 0, 3 * HEAD_DIM)]))
     expert_step(second_hop, 1)
-    groups.append(head(2))
     expert_step(second_hop, 2)
-    advance((2, 0))
+    head(2)
+    groups.append(send_back(2, [(2, 0, both), (3, both, HEAD_DIM)]))
     weights_of(0, groups[0])
     advance((0, 1), (3, 0))
-    expert_step(core_hop, 0)
     weights_of(1, groups[1])
-    advance((0, 2), (1, 1))
-    expert_step(finish, 0)
-    expert_step(core_hop, 1)
-    advance((1, 2), (2, 1))
-    weights_of(2, groups[2])
-    advance((0, 3))
-    send_f()
+    advance((1, 1), (0, 2))
+    weights_of(2, groups[2], (0, 1))
+    advance((0, part_k), (1, 2), (2, 1))
+    weights_of(2, groups[2], (2,))
+    advance((0, part_v), (1, part_k), (2, 2))
+    send_f(0)
+    advance((1, part_v), (2, part_k))
+    send_f(1)
     normed = inputs * inverse
     first_grads = back_sum[...].T
-    advance((1, 3))
-    expert_step(core_hop, 2)
-    advance((2, 2), (3, 1))
-    expert_step(finish, 1)
+    advance((2, part_v))
+    send_f(2)
     scaled = first_grads * table_ref[0:1, :]
+    early.wait()
     tokens_grad_ref[...] += inverse * (scaled - normed * jnp.mean(scaled * normed, -1, keepdims=True))
-    advance((2, 3), (3, 2))
-    expert_step(finish, 2)
-    advance((3, 3))
+    advance((3, 1), (3, 2), (3, part_k), (3, part_v))
     if reduce:
-        for p in range(chunks + 1):
+        for p in range(len(sizes)):
             for copy in stages[p, 3]:
                 copy.wait_recv()
-            size = 2 * half_of(p)
-            total_ref[p, :, :size] = all_got[p, :, :, :size].reshape(share, size)
             for stage in range(4):
                 for copy in stages[p, stage]:
                     copy.wait_send()
-        for copy in landed.values():
+            _, _, tall, half = all_got[p].shape
+            for chip in range(4):
+                for side in range(2):
+                    begin = offsets[p] + side * half
+                    total_ref[chip * tall : (chip + 1) * tall, begin : begin + half] = all_got[p][chip, side]
+        for i in range(3):
+            arrive(i, 4, 5, 6, 7)
+        for copy in sent:
             copy.wait_send()
-        for i in range(1, 3):
-            store(i).wait()
-    for local, group in d_groups + groups:
+    for local, group in d_groups:
         for copy in group:
             copy.wait_send()
+    for local, items in groups:
+        for group in items:
+            for copy in group:
+                copy.wait_send()
     for wait in background:
         wait()
+
+
+def part_columns(width, chunks):
+    sizes = [width + 256] + [width] * (chunks - 1) + [width // 3 * 2, width // 3 + 256]
+    return [sum(sizes[:p]) for p in range(len(sizes))], sizes
 
 
 def attend_back_phase(
@@ -1322,9 +1371,9 @@
     width = tokens.shape[1]
     length = owners * rows
     head = (chunks, owners, 3 * HEAD_DIM, rows)
-    columns = out_part.shape[1]
+    sizes = part_columns(width, chunks)[1]
+    columns, total = sum(sizes), len(sizes)
     share = width // owners
-    total = chunks + 1
     reduce = relayed(copies)
     vmem, hbm = pl.BlockSpec(memory_space=pltpu.VMEM), pl.BlockSpec(memory_space=pl.ANY)
     gate_shape, down_shape = pieces[0].shape[1:], pieces[2].shape[1:]
@@ -1345,37 +1394,29 @@
         pltpu.VMEM((HEAD_DIM, length), jnp.float32),
         wide, wide,
         pltpu.VMEM((TILE, TILE), jnp.float32),
-        *(sems(chunks, owners - 1),) * 4,
+        *(sems(chunks, owners - 1),) * 2,
+        *(sems(chunks + 1, owners - 1),) * 2,
         sems(3, copies), sems(3, copies), sems(2 * owners), sems(2 * owners), sems(2 * chunks), sems(2),
     ]
     if reduce:
-        half = columns // 2
         low = lambda *shape: pltpu.VMEM(shape, jnp.bfloat16)
         scratch += [
-            low(total, owners, 4, 48, columns),
-            low(total, owners, 4, 48, half),
-            low(total, 4, owners, 48, half),
-            low(total, owners, 48, half),
-            low(total, owners, 48, half),
-            low(total, 48, half),
-            low(total, 4, 48, columns),
             sems(total), sems(total), sems(total, 3), sems(total, 3),
             sems(total, owners - 1), sems(total, owners - 1), sems(total, copies - 1), sems(total, copies - 1),
-            low(6, *gate_shape), low(3, *gate_shape), low(3, *gate_shape), pltpu.VMEM((2, *gate_shape), jnp.float32),
-            low(6, *down_shape), low(3, *down_shape), pltpu.VMEM((2, *down_shape), jnp.float32),
-            sems(6), sems(3),
+            low(4, *gate_shape), low(2, *gate_shape), low(2, *gate_shape), low(4, *down_shape), low(2, *down_shape),
+            sems(4),
         ]
-        out_part = out_part.reshape(owners, 4, 48, columns)
-        last_specs = (vmem, hbm, hbm, hbm)
-        last_shapes = (
-            jax.ShapeDtypeStruct((total, share, columns), jnp.bfloat16),
-            *(jax.ShapeDtypeStruct((2, *piece.shape[1:]), jnp.float32) for piece in pieces),
-        )
+        tall, halves = share // 4, [size // 2 for size in sizes]
+        for shape in (
+            (2, 4, owners, tall), (4, owners, tall), (4, owners, tall), (owners, tall), (owners, tall), (tall,), (4, 2, tall)
+        ):
+            scratch += [low(*shape, half) for half in (halves[1:] if len(shape) == 4 and shape[0] == 2 else halves)]
+        last_specs, last_shapes = (vmem,), (jax.ShapeDtypeStruct((share, columns), jnp.bfloat16),)
     else:
-        last_specs, last_shapes = (vmem,), (jax.ShapeDtypeStruct((total, width, columns), jnp.bfloat16),)
-    tokens_grad, f_got, gate_got, up_got, down_got, totals, *sums = pl.pallas_call(
+        last_specs, last_shapes = (vmem,), (jax.ShapeDtypeStruct((width, columns), jnp.bfloat16),)
+    tokens_grad, f_got, *gots, totals = pl.pallas_call(
         functools.partial(attend_back_phase_kernel, reduce=reduce),
-        in_specs=[vmem] * 12 + [hbm] * 7,
+        in_specs=[vmem] * 12 + [hbm, vmem] + [hbm] * 5,
         out_specs=(vmem, hbm, hbm, hbm, hbm, *last_specs),
         out_shape=(
             jax.ShapeDtypeStruct((rows, width), jnp.float32),
@@ -1388,13 +1429,12 @@
         cost_estimate=cost(2e10, 5e7),
     )(grads, heads, outs, lse, bias, cosine, sine, tokens, table, *weights, resid_grads, out_part, f, *pieces, gate_first)
     if not reduce:
-        totals = lax.psum_scatter(totals, "expert", scatter_dimension=1, tiled=True)
+        out_part = out_part.transpose(2, 1, 3, 0, 4).reshape(width, sizes[0])
+        totals = jnp.concatenate([out_part, totals[:, sizes[0] :]], 1)
+        totals = lax.psum_scatter(totals, "expert", scatter_dimension=0, tiled=True)
         totals = lax.psum(totals, ("xy", "core"))
-        sums = [
-            jnp.sum(got.reshape(copies // 2, 2, *got.shape[1:]).astype(jnp.float32), 0)
-            for got in (gate_got, up_got, down_got)
-        ]
-    return (tokens_grad, f_got, totals, *sums)
+        gots = [jnp.sum(got.reshape(copies // 2, 2, *got.shape[1:]).astype(jnp.float32), 0) for got in gots]
+    return (tokens_grad, f_got, totals, gots)
 
 
 def per_device(
@@ -1404,7 +1444,7 @@
 ):
     owners = lax.axis_size("expert")
     member = lax.axis_index("expert")
-    tokens, prior, routes, grad = tokens[0], prior_logits[0], routes[0], cotangent[0]
+    tokens, prior, routes, grad = tokens[0], prior_logits[0].T, routes[0].T, cotangent[0]
     rows, width = tokens.shape
     copies = lax.axis_size("xy") * lax.axis_size("core")
     chunks = width // HEAD_DIM // owners
@@ -1417,37 +1457,39 @@
     attended = attended.reshape(width, rows)
     gate, up, down = (full.reshape(-1, full.shape[-1]) for full in (gate, up, down))
     resid, small, *x_out, mixer = middle(
-        tokens, attended, out_weight, table, router_weight, constant_weight, prior, prior_weight, routes, codes_row
+        tokens, attended, out_weight, table, router_weight.T, constant_weight.T, prior, prior_weight, codes, codes_row
     )
     backs, dots, fa, fb, *grads = expert_phase(x_out, small, grad, codes_row, gate, up, down)
     pieces = [item.reshape(copies, -1, item.shape[-1]) for item in grads]
     dots = dots[:, :, 0, : rows // NFFN].reshape(1, 2 * rows)
     resid_grads, grads_out, out_part, prior_grad, fa, gate_first = turn(
-        resid, small, grad, prior, routes, codes, backs.reshape(2 * rows, width), dots, table, mixer, prior_weight,
+        resid, small, grad, prior, codes, backs.reshape(2 * rows, width), dots, table, mixer, prior_weight,
         out_weight, attended, fa, pieces[0],
     )
-    tokens_grad, fb, totals, *sums = attend_back_phase(
+    tokens_grad, fb, totals, gots = attend_back_phase(
         grads_out.reshape(chunks, owners, HEAD_DIM, rows), heads, outs, logs, bias, cosine, sine, tokens,
         table, qkv_weights, resid_grads, out_part, fb, pieces, gate_first, copies,
     )
     fs = [f.reshape(rows, width) for f in (fa, fb)]
+    reduce = relayed(copies)
+    experts = gots
+    if reduce:
+        experts = [item for i in range(3) for item in (pieces[i], gate_first if i == 0 else gots[i], gots[i])]
     (
         tokens_grad, gate_part, up_part, down_part, result, *qkv_out_grads, router_grad, prior_weight_grad,
-        constant_weight_grad, row_grads,
-    ) = finish(resid, small, routes, codes, fs, table, totals, (tokens_grad, *sums))
-    share = width // owners
-    own_gain = lax.dynamic_slice_in_dim(attention_gain, member * share, share)
+        constant_weight_grad, vector_grad, gain_grads,
+    ) = finish(resid, small, codes, fs, table, totals, tokens_grad, experts, reduce)
     return (
         result[None],
         tokens_grad[None],
-        prior_grad[None],
+        prior_grad.T[None],
         *qkv_out_grads,
-        row_grads[3] / own_gain,
-        row_grads[2],
-        router_grad,
+        gain_grads[0],
+        gain_grads[1],
+        router_grad.T,
         prior_weight_grad,
-        constant_weight_grad,
-        row_grads[:2],
+        constant_weight_grad.T,
+        vector_grad,
         gate_part,
         up_part,
         down_part,

time: 479 us -> 463 us (0.967)
  the two profiles are of different devices: /device:TPU:1 before, /device:TPU:17 now
where the time goes in v5:
time: 463 us; the launch traced here: 454 us
  Pallas kernels  444 us (96%)
  local copies, waits for them, and re-layouts  7.12 us (2%)
    pallas_call x1, Pallas kernels, attend_back_phase(): pl.pallas_call(functools.partial(attend_back_phase_kernel, reduce=reduce)...  151 us
    pallas_call x1, Pallas kernels, expert_phase(): pl.pallas_call(expert_phase_kernel, in_specs=[vmem] * 5 + [hbm] * 3, out_...  142 us
    pallas_call x1, Pallas kernels, attend_phase(): pl.pallas_call(attend_phase_kernel, in_specs=[vmem] * 7 + [hbm] * 3, out_...  97.7 us
    pallas_call x1, Pallas kernels, turn(): pl.pallas_call(functools.partial(turn_kernel, owners=owners, reduce=relay...  29.7 us
    pallas_call x1, Pallas kernels, finish(): pl.pallas_call(functools.partial(finish_kernel, owners=owners, count=coun...  12.1 us
    pallas_call x1, Pallas kernels, middle(): pl.pallas_call(middle_kernel, out_shape=(jax.ShapeDtypeStruct((rows, widt...  11.1 us

profile of v5, /device:TPU:17, one launch (start us, length us, event | category | flops | bytes accessed | tf_op | source)
XLA Modules:
  0.0 453.6 jit_solution(9318994458444642242)
XLA Ops:
  0.7 0.1 pad.3.clone
  0.7 0.7 broadcast_in_dim.18
  1.4 0.7 broadcast_in_dim.19
  2.1 1.4 maximum_maximum_fusion.table_ref
  3.5 1.4 copy.37
  4.8 97.7 %shard_map.297 = (bf16[3,4,64,640]{3,2,1,0:T(8,128)(2,1)}, f32[8,2560]{1,0:T(8,128)}, f32[16,2560]{1,0:T(8,128)}, f32[32,2560]{1,0:T(8,128)}, f32[32,2560]{1,0:T...) custom-call(bf16[640,768]{1,0:T(8,128)(2,1)} %bitcast.54, ...), custom_call_target="tpu_custom_call" | custom-call | flops 10000000000 | bytes 50000000 | tf_op jit(solution)/shard_map/pallas_call | solution.py:438
  102.6 11.1 %shard_map.298 = (f32[640,768]{1,0:T(8,128)}, f32[640,128]{1,0:T(8,128)}, bf16[640,768]{1,0:T(8,128)(2,1)}, bf16[640,768]{1,0:T(8,128)(2,1)}, bf16[128,768]{1,0:T(8,128)(2,1)}) custom-call(bf16[640,768]{1,0:T(8,128)(2,1)} %bitcast.55, bf16[768,640]{1,0:T(8,128)(2,1)} %bitcast.45, bf16[768,768]{1,0:T(8,128)(2,1)} %out_weight_ref.3, ...), custom_call_target="tpu_custom_call" | custom-call | flops 2768240640 | bytes 10000000 | tf_op jit(solution)/shard_map/pallas_call | solution.py:524
  113.7 142.4 %shard_map.299 = (bf16[2,8,80,768]{3,2,1,0:T(8,128)(2,1)}, f32[2,8,8,128]{3,2,1,0:T(8,128)}, bf16[8,80,768]{2,1,0:T(8,128)(2,1)}, bf16[8,80,768]{2,1,0:T(8,128)(...) custom-call(bf16[8,80,768]{2,1,0:T(8,128)(2,1)} %bitcast.67, ...), custom_call_target="tpu_custom_call" | custom-call | flops 36238786560 | bytes 50000000 | tf_op jit(solution)/shard_map/pallas_call | solution.py:718
  256.0 0.9 slice_reduce_fusion
  256.9 0.7 reshape_squeeze.3.dots_ref
  257.6 29.7 %shard_map.300 = (f32[640,768]{1,0:T(8,128)}, bf16[768,640]{1,0:T(8,128)(2,1)}, bf16[2,4,4,48,512]{4,3,2,1,0:T(8,128)(2,1)}, f32[12,640]{1,0:T(8,128)}, bf16[8,8...) custom-call(f32[640,768]{1,0:T(8,128)} %get-tuple-element.69.resid_ref, f32[640,128]{1,0:T(8,128)} %get-tuple-element.70.small_ref, ...), custom_call_target="tpu_custom_call" | custom-call | flops 2768240640 | bytes 15000000 | tf_op jit(solution)/shard_map/pallas_call | solution.py:887
  287.3 1.4 copy.34
  288.7 151.3 %shard_map.301 = (f32[640,768]{1,0:T(8,128)}, bf16[8,80,768]{2,1,0:T(8,128)(2,1)}, bf16[8,96,2048]{2,1,0:T(8,128)(2,1)}, bf16[8,96,2048]{2,1,0:T(8,128)(2,1)}, b...) custom-call(bf16[3,4,64,640]{3,2,1,0:T(8,128)(2,1)} %bitcast.58, ...), custom_call_target="tpu_custom_call" | custom-call | flops 20000000000 | bytes 50000000 | tf_op jit(solution)/shard_map/pallas_call | solution.py:1417
  440.1 12.1 %shard_map.302 = (f32[640,768]{1,0:T(8,128)}, f32[2,96,2048]{2,1,0:T(8,128)}, f32[2,96,2048]{2,1,0:T(8,128)}, f32[2,256,768]{2,1,0:T(8,128)}, bf16[640,768]{1,0:...) custom-call(f32[640,768]{1,0:T(8,128)} %get-tuple-element.69.resid_r, ...), custom_call_target="tpu_custom_call" | custom-call | flops 2516582400 | bytes 8000000 | tf_op jit(solution)/shard_map/pallas_call | solution.py:1015
  452.1 1.3 fusion
  (1 shorter events, 0.0 us)
